TPU v7x, 32 devices: a whole 2x2x4 slice. The times are simulated.
32 devices in a mesh: row: 4 (over y, x), col: 8 (over z, core).
Axes of the slice: x: 2, y: 2, z: 4, core: 2. Of those that a mesh axis runs over, the one named last changes fastest.
Arguments:
- feats: bfloat16 [8, 512, 512], P('col', 'row'), may hold values from -6 to 6
- weight: bfloat16 [512, 512], replicated, may hold values from -0.25 to 0.25
- cotangent: bfloat16 [4, 1024, 512], P('row', 'col'), may hold values from -6 to 6
- tile_values: bfloat16 [4, 8, 24, 128, 128], P('row', 'col'), may hold values from -0.15625 to 0.15625
- tile_rows: int32 [4, 8, 24], P('row', 'col'), may hold values from 0 to 7, as said below
- tile_cols: int32 [4, 8, 24], P('row', 'col'), may hold values from 0 to 3, as said below
- tile_count: int32 [4, 8], P('row', 'col'), may hold values from 1 to 24, as said below
Outputs:
- layer_out: bfloat16 [4, 1024, 512], P('row', 'col')
- feat_grad: bfloat16 [8, 512, 512], P('col', 'row')
- weight_grad: float32 [512, 512], replicated
Inputs may be any that keep to these rules, and one draw needn't show every extreme that they name: `tile_rows`: with tile_cols, the tile coordinates of each block's listed tiles; no tile appears twice in a block's list. `tile_cols`: with tile_rows, the tile coordinates of each block's listed tiles. `tile_count`: slots at or beyond a block's count are unused; some block lists exactly 24 tiles.
All inputs are finite; a program needn't handle non-finite values.
Results may differ from a plain program's by a relative error of at most 0.024.
Values may be sent and summed in bfloat16 or wider, within the bound.
No kernel may reach another device: no remote copies, remote signals or barrier semaphores. Data moves between devices by JAX's collectives and lax.ppermute only.
A program may use at most 128 MiB of HBM per device.

v0:
```python
import jax
import jax.numpy as jnp
from jax import lax
from jax.sharding import PartitionSpec as P


def tile_products(
    running, tile_block, slot_rows, slot_cols, source, first_slot, last_slot, forward
):
    slot_count = tile_block.shape[0]
    group_size = min(32, slot_count)

    def one_group(group_index, partial_value):
        group_begin = first_slot + group_index * group_size
        slot_start = jnp.minimum(group_begin, slot_count - group_size)
        slot_ids = slot_start + jnp.arange(group_size, dtype=jnp.int32)
        keep_mask = (
            (slot_ids >= group_begin)
            & (slot_ids < last_slot)
            & (slot_ids < group_begin + group_size)
        )
        tiles_now = (
            lax.dynamic_slice_in_dim(tile_block, slot_start, group_size, 0)
            * keep_mask.astype(tile_block.dtype)[:, None, None]
        )
        rows_now = lax.dynamic_slice_in_dim(slot_rows, slot_start, group_size, 0)
        cols_now = lax.dynamic_slice_in_dim(slot_cols, slot_start, group_size, 0)
        if forward:
            picked = source[cols_now]
            products = jnp.einsum(
                "gab,gbf->gaf", tiles_now, picked, preferred_element_type=jnp.float32
            )
            return partial_value.at[rows_now].add(products)
        picked = source[rows_now]
        products = jnp.einsum("gab,gaf->gbf", tiles_now, picked, preferred_element_type=jnp.float32)
        return partial_value.at[cols_now].add(products)

    group_total = (jnp.maximum(last_slot - first_slot, 0) + group_size - 1) // group_size
    return lax.fori_loop(0, group_total, one_group, running)


def local(feats, weight, cotangent, tile_values, tile_rows, tile_cols, tile_count):
    feature_width = feats.shape[2]
    local_rows = feats.shape[1]
    tile_block = tile_values[0, 0]
    slot_rows = tile_rows[0, 0]
    slot_cols = tile_cols[0, 0]
    tile_total = tile_count[0, 0]
    row_tiles = local_rows * lax.axis_size("col") // 128
    col_tiles = local_rows * lax.axis_size("row") // 128
    node_total = local_rows * lax.axis_size("row") * lax.axis_size("col")
    panel_rows = lax.all_gather(feats[0], "row", axis=0, tiled=True)
    panel_tiles = panel_rows.reshape(col_tiles, 128, feature_width)
    forward_part = jnp.zeros((row_tiles, 128, feature_width), jnp.float32)
    backward_part = jnp.zeros((col_tiles, 128, feature_width), jnp.float32)
    forward_part = tile_products(
        forward_part, tile_block, slot_rows, slot_cols, panel_tiles, 0, tile_total, True
    )
    summed = lax.psum_scatter(
        forward_part.reshape(row_tiles * 128, feature_width).astype(jnp.bfloat16),
        "col",
        scatter_dimension=0,
        tiled=True,
    )
    hidden = jnp.dot(summed, weight, preferred_element_type=jnp.float32)
    sigmoid_part = jax.nn.sigmoid(hidden)
    layer_out = (hidden * sigmoid_part).astype(jnp.bfloat16)
    hidden_grad = (
        cotangent[0].astype(jnp.float32) * sigmoid_part * (1.0 + hidden * (1.0 - sigmoid_part))
    ).astype(jnp.bfloat16)
    grad_rows = lax.dot_general(
        hidden_grad, weight, (((1,), (1,)), ((), ())), preferred_element_type=jnp.float32
    ).astype(jnp.bfloat16)
    weight_term = lax.dot_general(
        summed, hidden_grad, (((0,), (0,)), ((), ())), preferred_element_type=jnp.float32
    ) * node_total ** (-0.5)
    weight_grad = lax.psum(weight_term, ("row", "col"))
    gathered_grads = lax.all_gather(grad_rows, "col", axis=0, tiled=True).reshape(
        row_tiles, 128, feature_width
    )
    backward_part = tile_products(
        backward_part, tile_block, slot_rows, slot_cols, gathered_grads, 0, tile_total, False
    )
    feat_grad = lax.psum_scatter(
        backward_part.reshape(col_tiles * 128, feature_width).astype(jnp.bfloat16),
        "row",
        scatter_dimension=0,
        tiled=True,
    )
    return (layer_out[None], feat_grad[None], weight_grad)


def solution(mesh):
    in_specs = (
        P("col", "row", None),
        P(),
        P("row", "col", None),
        P("row", "col", None, None, None),
        P("row", "col", None),
        P("row", "col", None),
        P("row", "col"),
    )
    out_specs = (P("row", "col", None), P("col", "row", None), P())
    return jax.shard_map(local, mesh=mesh, in_specs=in_specs, out_specs=out_specs, check_vma=False)
```

profile of v0, /device:TPU:0, one launch (start us, length us, event | category | flops | bytes accessed | tf_op | source)
XLA Modules:
  0.0 266.6 jit_solution(10020554956640780072)
XLA Ops:
  7.9 11.8 %all-gather = bf16[1,512,512]{2,1,0:T(8,128)(2,1)S(1)} all-gather(bf16[1,128,512]{2,1,0:T(8,128)(2,1)} %param.11), channel_id=2, replica_groups=mesh['row'=4,'col'=8] {'row'}, dimensions={1}, use_global_device_ids=true | all-gather | bytes 655360 | tf_op jit(solution)/shard_map/all_gather | solution.py:52
  20.0 18.7 %while.20 = (s32[]{:T(128)}, f32[8,128,512]{2,1,0:T(8,128)S(1)}, s32[]{:T(128)}, s32[24]{0:T(128)}, s32[]{:T(128)}, /*index=5*/bf16[24,128,128]{2,1,0:T(8,128)(2...) while((s32[]{:T(128)}, f32[8,128,512]{2,1,0:T(8,128)S(1)}, ...), condition=%wide.region_2.3_spmd, body=%wide.region_0.2_spmd.sunk | while | flops 404620608 | bytes 35394472 | solution.py:39
  20.1 0.7 fusion.32
  20.7 2.5 gather_fusion
  23.3 0.7 and_convert_fusion.4
  24.0 5.8 %fusion.33 = f32[24,128,512]{2,1,0:T(8,128)} fusion(bf16[24,128,512]{2,1,0:T(8,128)(2,1)} %gather_fusion, bf16[24,128,128]{2,1,0:T(8,128)(2,1)} %get-tuple-element.270, bf16[24]{0:T(256)(128)(2,1)S(1)} %and_convert_fusion.4), kind=kOutput, calls=%fused_computation.4.clone.1 | convolution fusion | flops 403046400 | bytes 10223664 | tf_op jit(solution)/shard_map/while/body/gab,gbf->gaf/dot_general | solution.py:30
  29.8 8.9 %scatter_fusion = f32[8,128,512]{2,1,0:T(8,128)S(1)} fusion(f32[8,128,512]{2,1,0:T(8,128)S(1)} %get-tuple-element.255, s32[24]{0:T(128)S(1)} %get-tuple-element.231, f32[24,128,512]{2,1,0:T(8,128)} %fusion.33), kind=kCustom, calls=%fused_computation.2.clone.1 | custom fusion | flops 1572864 | bytes 18874464 | tf_op jit(solution)/shard_map/while/body/scatter-add | solution.py:33
  38.7 1.1 convert_element_type.41
  39.9 32.6 %reduce-scatter.3.cloned.1.call-done = bf16[128,512]{1,0:T(8,128)(2,1)} async-done(((bf16[1024,512]{1,0:T(8,128)(2,1)}), bf16[128,512]{1,0:T(8,128)(2,1)}) %reduce-scatter.3.cloned.1.call-update) | async-done | bytes 131088 | tf_op jit(solution)/shard_map/reduce_scatter | solution.py:59
  72.5 1.2 fusion.15
  73.7 1.0 convolution_convert_fusion
  74.8 0.4 copy.10
  75.2 1.4 convolution_multiply_fusion
  76.6 18.7 %all-gather.3.cloned.1.call-done = bf16[1024,512]{1,0:T(8,128)(2,1)} async-done(((bf16[128,512]{1,0:T(8,128)(2,1)}), bf16[1024,512]{1,0:T(8,128)(2,1)}) %all-gather.3.cloned.1.call-update) | async-done | bytes 1048592 | tf_op jit(solution)/shard_map/all_gather | solution.py:78
  95.4 19.0 %while.21 = (s32[]{:T(128)}, f32[4,128,512]{2,1,0:T(8,128)S(1)}, s32[]{:T(128)}, s32[24]{0:T(128)S(1)}, s32[]{:T(128)}, /*index=5*/bf16[24,128,128]{1,2,0:T(8,12...) while((s32[]{:T(128)}, f32[4,128,512]{2,1,0:T(8,128)S(1)}, ...), condition=%wide.region_6.7_spmd, body=%wide.region_4.6_spmd.sunk | while | flops 404620608 | bytes 35394472 | solution.py:39
  95.5 3.8 %gather_fusion.1 = bf16[24,128,512]{2,1,0:T(8,128)(2,1)} fusion(bf16[8,128,512]{2,1,0:T(8,128)(2,1)} %get-tuple-element.305, s32[1024]{0:T(1024)S(1)} %pad_clamp_fusion.5), kind=kCustom, calls=%fused_computation.1.clone.1 | custom fusion | bytes 6291552 | tf_op jit(solution)/shard_map/while/body/gather | solution.py:34
  99.2 0.7 and_convert_fusion.5
  99.9 5.6 %fusion.37 = f32[24,128,512]{2,1,0:T(8,128)} fusion(bf16[24,128,512]{2,1,0:T(8,128)(2,1)} %gather_fusion.1, bf16[24,128,128]{1,2,0:T(8,128)(2,1)S(1)} %get-tuple-element.303, bf16[24]{0:T(256)(128)(2,1)S(1)} %and_convert_fusion.5), kind=kOutput, calls=%fused_computation.13.clone.1 | convolution fusion | flops 403046400 | bytes 10223664 | tf_op jit(solution)/shard_map/while/body/gab,gaf->gbf/dot_general | solution.py:35
  105.5 8.9 %scatter_fusion.1 = f32[4,128,512]{2,1,0:T(8,128)S(1)} fusion(f32[4,128,512]{2,1,0:T(8,128)S(1)} %get-tuple-element.288, s32[24]{0:T(128)S(1)} %get-tuple-element.241, f32[24,128,512]{2,1,0:T(8,128)} %fusion.37), kind=kCustom, calls=%fused_computation.3.clone.1 | custom fusion | flops 1572864 | bytes 18874464 | tf_op jit(solution)/shard_map/while/body/scatter-add | solution.py:36
  114.4 0.9 convert_element_type.48
  115.3 0.7 fusion.12
  116.0 114.5 %all-reduce.2.cloned.1.call-done = f32[512,512]{1,0:T(8,128)} async-done(((f32[512,512]{1,0:T(8,128)}), f32[512,512]{1,0:T(8,128)}) %all-reduce.2.cloned.1.call-update) | async-done | bytes 1048592 | tf_op jit(solution)/shard_map/psum | solution.py:77
  230.5 27.3 %reduce-scatter.5.cloned.1.call-done = bf16[128,512]{1,0:T(8,128)(2,1)} async-done(((bf16[512,512]{1,0:T(8,128)(2,1)}), bf16[128,512]{1,0:T(8,128)(2,1)}) %reduce-scatter.5.cloned.1.call-update) | async-done | bytes 131088 | tf_op jit(solution)/shard_map/reduce_scatter | solution.py:84
  257.8 2.3 copy.29
  (25 shorter events, 0.6 us)
Async XLA Ops:
  7.2 65.3 %copy-start = (bf16[512,512]{1,0:T(8,128)(2,1)S(1)}, bf16[512,512]{1,0:T(8,128)(2,1)}, u32[]{:S(2)}) copy-start(bf16[512,512]{1,0:T(8,128)(2,1)} %param.12) | copy-start | bytes 1572868
  7.2 65.3 %reduce-scatter.3.cloned.1.call-start = ((), (), s32[]{:S(2)}) async-start(), calls=%async_computation.2 | async-start | bytes 1179648 | tf_op jit(solution)/shard_map/reduce_scatter | solution.py:59
  38.7 35.0 %copy-start.5 = (bf16[1,128,512]{2,1,0:T(8,128)(2,1)S(1)}, bf16[1,128,512]{2,1,0:T(8,128)(2,1)}, u32[]{:S(2)}) copy-start(bf16[1,128,512]{2,1,0:T(8,128)(2,1)} %param.13) | copy-start | bytes 393220
  39.8 34.9 %copy-start.1 = (bf16[24,128,128]{2,1,0:T(8,128)(2,1)S(1)}, bf16[24,128,128]{2,1,0:T(8,128)(2,1)}, u32[]{:S(2)}) copy-start(bf16[24,128,128]{2,1,0:T(8,128)(2,1)} %get-tuple-element.317) | copy-start | bytes 2359300
  39.9 55.4 %all-gather.3.cloned.1.call-start = ((), (), s32[]{:S(2)}) async-start(), calls=%async_computation.3 | async-start | bytes 1179648 | tf_op jit(solution)/shard_map/all_gather | solution.py:78
  72.5 2.7 copy-start.2
  74.7 20.7 %copy-start.3 = (s32[24]{0:T(128)S(1)}, s32[24]{0:T(128)}, u32[]{:S(2)}) copy-start(s32[24]{0:T(128)} %get-tuple-element.328) | copy-start | bytes 292
  74.7 20.7 %copy-start.4 = (s32[24]{0:T(128)S(1)}, s32[24]{0:T(128)}, u32[]{:S(2)}) copy-start(s32[24]{0:T(128)} %get-tuple-element.329) | copy-start | bytes 292
  74.7 155.8 %all-reduce.2.cloned.1.call-start = ((), (), s32[]{:S(2)}) async-start(), calls=%async_computation.5 | async-start | bytes 2097152 | tf_op jit(solution)/shard_map/psum | solution.py:77
  76.6 181.2 %reduce-scatter.5.cloned.1.call-start = ((), (), s32[]{:S(2)}) async-start(), calls=%async_computation.4 | async-start | bytes 655360 | tf_op jit(solution)/shard_map/reduce_scatter | solution.py:84
Sparse Core Ops, SparseCore 0:
  40.0 32.4 reduce-scatter.2
  74.8 20.3 all-gather.2
  101.0 129.4 all-reduce.1
  234.0 23.7 reduce-scatter.4
where the time goes:
time: 267 us
  waiting for transfers between devices  193 us (72%)
  other arithmetic  22.6 us (8%)
  matrix products  14.9 us (6%)
  between operations  14.6 us (5%)
  blocking collectives  11.8 us (4%)
  local copies, waits for them, and re-layouts  9.36 us (4%)
    psum x1, waiting for transfers between devices, local(): weight_grad = lax.psum(weight_term, ('row', 'col'))  114 us
    reduce_scatter x1, waiting for transfers between devices, local(): lax.psum_scatter(forward_part.reshape(row_tiles * 128, feature_width).ast...  32.6 us
    reduce_scatter x1, waiting for transfers between devices, local(): lax.psum_scatter(backward_part.reshape(col_tiles * 128, feature_width).as...  27.3 us
    all_gather x1, waiting for transfers between devices, local(): lax.all_gather(grad_rows, 'col', axis=0, tiled=True)  18.7 us
    all_gather x1, blocking collectives, local(): panel_rows = lax.all_gather(feats[0], 'row', axis=0, tiled=True)  11.8 us
    scatter-add x1, other arithmetic, one_group(): return partial_value.at[rows_now].add(products)  8.94 us
    scatter-add x1, other arithmetic, one_group(): return partial_value.at[cols_now].add(products)  8.93 us
    dot_general x1, matrix products, one_group(): jnp.einsum('gab,gbf->gaf', tiles_now, picked, preferred_element_type=jnp....  5.82 us
  transfers between devices with their start and end apart: 4, of which 4 were waited for; matrix products, arithmetic and copies ran while one was open for 8% of the time, Pallas kernels for 0%

commit v1 on v0

v1 whole, which is shorter than its diff:
```python
import functools

import jax
import jax.numpy as jnp
from jax import lax
from jax.experimental import pallas as pl
from jax.experimental.pallas import tpu as pltpu
from jax.sharding import PartitionSpec as P

F32 = jnp.float32
BF16 = jnp.bfloat16
VMEM = pl.BlockSpec(memory_space=pltpu.VMEM)
SMEM = pl.BlockSpec(memory_space=pltpu.SMEM)
TILE = 128


def call(kernel, outs, args, specs=None, scratch=(), work=0):
    held = sum(a.size * a.dtype.itemsize for a in (*args, *outs))
    return pl.pallas_call(
        kernel,
        out_shape=outs,
        in_specs=specs or [VMEM] * len(args),
        out_specs=[VMEM] * len(outs),
        scratch_shapes=scratch,
        compiler_params=pltpu.CompilerParams(vmem_limit_bytes=12 * 2**20 + 3 * held),
        cost_estimate=pl.CostEstimate(flops=work, bytes_accessed=held, transcendentals=0),
    )(*args)


def like(*shape, dtype=BF16):
    return jax.ShapeDtypeStruct(shape, dtype)


def swap(value, axis, size, mask):
    return lax.ppermute(value, axis, [(i, i ^ mask) for i in range(size)])


def tree(terms):
    while len(terms) > 1:
        terms = [terms[i] + terms[i + 1] for i in range(0, len(terms), 2)]
    return terms[0]


def densify(n_z, values, rows, cols, count, dense, dense_t):
    me_row, me_col = lax.axis_index("row"), lax.axis_index("col")
    dense[...] = jnp.zeros_like(dense)
    dense_t[...] = jnp.zeros_like(dense_t)

    def place(s, carry):
        far = rows[0, 0, s] ^ me_col
        at = pl.multiple_of(((far & 1) * n_z + (far >> 1)) * TILE, TILE)
        to = pl.multiple_of((cols[0, 0, s] ^ me_row) * TILE, TILE)
        tile = values[0, 0, s]
        dense[pl.ds(at, TILE), pl.ds(to, TILE)] = tile
        dense_t[pl.ds(to, TILE), pl.ds(at, TILE)] = tile.T
        return carry

    lax.fori_loop(0, count[0, 0], place, 0)


def forward(first, dense, *refs):
    *feats, out = refs
    size = out.shape[0]
    panel = jnp.concatenate([f[...] for f in feats], axis=0)
    out[...] = jnp.dot(
        dense[first : first + size, :], panel, preferred_element_type=F32
    ).astype(out.dtype)


def add_split(mine, other, *outs):
    rows = outs[0].shape[0]
    for k, out in enumerate(outs):
        part = pl.ds(k * rows, rows)
        out[...] = (mine[part, :].astype(F32) + other[part, :].astype(F32)).astype(out.dtype)


def add_all(*refs):
    *terms, out = refs
    out[...] = tree([t[...].astype(F32) for t in terms]).astype(out.dtype)


def dense_layer(n_z, weight, cotangent, *refs):
    terms, (layer_out, summed, hidden_grad, grad_rows) = refs[:n_z], refs[n_z:]
    total = tree([t[...].astype(F32) for t in terms]).astype(BF16)
    summed[...] = total
    hidden = jnp.dot(total, weight[...], preferred_element_type=F32)
    gate = jax.nn.sigmoid(hidden)
    layer_out[...] = (hidden * gate).astype(BF16)
    grad = (cotangent[0].astype(F32) * gate * (1.0 + hidden * (1.0 - gate))).astype(BF16)
    hidden_grad[...] = grad
    grad_rows[...] = lax.dot_general(
        grad, weight[...], (((1,), (1,)), ((), ())), preferred_element_type=F32
    ).astype(BF16)


def weight_term(n_row, scale, summed, hidden_grad, mine, other, whole):
    whole[...] = (
        lax.dot_general(
            summed[...], hidden_grad[...], (((0,), (0,)), ((), ())), preferred_element_type=F32
        )
        * scale
    )
    me_row, core = lax.axis_index("row"), lax.axis_index("col") & 1
    half = mine.shape[0]
    piece = half // n_row
    for k in range(n_row):
        inside = (me_row ^ k) * piece
        part = pl.ds(k * piece, piece)
        at = pl.multiple_of(core * half + inside, piece)
        mine[part, :] = whole[pl.ds(at, piece), :]
        at = pl.multiple_of((1 - core) * half + inside, piece)
        other[part, :] = whole[pl.ds(at, piece), :].astype(BF16)


def backward(n_z, dense_t, *refs):
    grads, outs = refs[: 2 * n_z], refs[2 * n_z :]
    panel = jnp.concatenate([g[...] for g in grads], axis=0)
    total = jnp.dot(dense_t[...], panel, preferred_element_type=F32)
    for k, out in enumerate(outs):
        out[...] = total[k * TILE : (k + 1) * TILE].astype(out.dtype)


def join(*refs):
    *pieces, out = refs
    me_row = lax.axis_index("row")
    piece = pieces[0].shape[0]
    for k, ref in enumerate(pieces):
        at = pl.multiple_of((me_row ^ k) * piece, piece)
        out[pl.ds(at, piece), :] = ref[...]


def spread(mine, other, out):
    core = lax.axis_index("col") & 1
    half = mine.shape[0]
    out[pl.ds(pl.multiple_of(core * half, half), half), :] = mine[...].astype(F32)
    out[pl.ds(pl.multiple_of((1 - core) * half, half), half), :] = other[...].astype(F32)


def local(feats, weight, cotangent, tile_values, tile_rows, tile_cols, tile_count):
    width = feats.shape[2]
    n_row, n_col = lax.axis_size("row"), lax.axis_size("col")
    n_z = n_col // 2
    row_nodes, col_nodes = n_col * TILE, n_row * TILE
    half = row_nodes // 2
    row_swap = lambda x, k: swap(x, "row", n_row, k)
    z_swap = lambda x, k: swap(x, "col", n_col, 2 * k)
    core_swap = lambda x: swap(x, "col", n_col, 1)

    own = feats[0]
    panel = [own] + [row_swap(own, k) for k in range(1, n_row)]
    dense, dense_t = call(
        functools.partial(densify, n_z),
        [like(row_nodes, col_nodes), like(col_nodes, row_nodes)],
        (tile_values, tile_rows, tile_cols, tile_count),
        specs=[VMEM, SMEM, SMEM, SMEM],
    )
    work = 2 * half * col_nodes * width
    (other,) = call(functools.partial(forward, half), [like(half, width)], (dense, *panel), work=work)
    other = core_swap(other)
    (mine,) = call(
        functools.partial(forward, 0), [like(half, width, dtype=F32)], (dense, *panel), work=work
    )
    parts = call(
        add_split,
        [like(TILE, width, dtype=F32)] + [like(TILE, width)] * (n_z - 1),
        (mine, other),
    )
    terms = [parts[0]] + [z_swap(parts[k], k) for k in range(1, n_z)]
    layer_out, summed, hidden_grad, grad_rows = call(
        functools.partial(dense_layer, n_z),
        [like(TILE, width)] * 4,
        (weight, cotangent, *terms),
        work=4 * TILE * width * width,
    )
    same = [grad_rows] + [z_swap(grad_rows, k) for k in range(1, n_z)]
    cross = [core_swap(g) for g in same]

    piece = width // 2 // n_row
    mine_w, other_w = call(
        functools.partial(weight_term, n_row, (n_row * n_col * TILE) ** -0.5),
        [like(width // 2, width, dtype=F32), like(width // 2, width)],
        (summed, hidden_grad),
        scratch=[pltpu.VMEM((width, width), F32)],
        work=2 * TILE * width * width,
    )
    other_w = core_swap(other_w)
    parts_w = call(add_split, [like(piece, width)] * n_row, (mine_w, other_w))
    terms_w = [parts_w[0]] + [row_swap(parts_w[k], k) for k in range(1, n_row)]
    (plane_w,) = call(add_all, [like(piece, width)], terms_w)
    terms_w = [plane_w] + [z_swap(plane_w, k) for k in range(1, n_z)]
    (final_w,) = call(add_all, [like(piece, width)], terms_w)
    pieces_w = [final_w] + [row_swap(final_w, k) for k in range(1, n_row)]
    (half_w,) = call(join, [like(width // 2, width)], pieces_w)
    (weight_grad,) = call(spread, [like(width, width, dtype=F32)], (half_w, core_swap(half_w)))

    back = call(
        functools.partial(backward, n_z),
        [like(TILE, width, dtype=F32)] + [like(TILE, width)] * (n_row - 1),
        (dense_t, *same, *cross),
        work=2 * work,
    )
    terms = [back[0]] + [row_swap(back[k], k) for k in range(1, n_row)]
    (feat_grad,) = call(add_all, [like(TILE, width)], terms)
    return layer_out[None], feat_grad[None], weight_grad


def solution(mesh):
    in_specs = (
        P("col", "row", None),
        P(),
        P("row", "col", None),
        P("row", "col", None, None, None),
        P("row", "col", None),
        P("row", "col", None),
        P("row", "col"),
    )
    out_specs = (P("row", "col", None), P("col", "row", None), P())
    return jax.shard_map(local, mesh=mesh, in_specs=in_specs, out_specs=out_specs, check_vma=False)
```

time: 267 us -> 78 us (0.29)
  waiting for transfers between devices: 193 us -> 34 us
  starting transfers between devices: 0.16 us -> 34.7 us
  other arithmetic: 22.6 us -> 0 us
  matrix products: 14.9 us -> 0 us
  between operations: 14.6 us -> 1.47 us
  blocking collectives: 11.8 us -> 0 us
  local copies, waits for them, and re-layouts: 9.36 us -> 1.15 us
  Pallas kernels: 0 us -> 6.46 us
    psum x1 -> x0, waiting for transfers between devices: 114 us -> none  [local(): weight_grad = lax.psum(weight_term, ('row', 'col'))]
    reduce_scatter x2 -> x0, waiting for transfers between devices: 59.9 us -> none  [the longest x1 32.6 us: local(): lax.psum_scatter(forward_part.reshape(row_tiles * 128, feature_width).ast...]
    ppermute x0 -> x28, starting transfers between devices: none -> 34.7 us  [swap(): return lax.ppermute(value, axis, [(i, i ^ mask) for i in range(size)])]
    ppermute x0 -> x28, waiting for transfers between devices: none -> 34 us  [swap(): return lax.ppermute(value, axis, [(i, i ^ mask) for i in range(size)])]
    all_gather x1 -> x0, waiting for transfers between devices: 18.7 us -> none  [local(): lax.all_gather(grad_rows, 'col', axis=0, tiled=True)]
    scatter-add x2 -> x0, other arithmetic: 17.9 us -> none  [the longest x1 8.94 us: one_group(): return partial_value.at[rows_now].add(products)]
    dot_general x5 -> x0, matrix products: 14.9 us -> none  [the longest x1 5.82 us: one_group(): jnp.einsum('gab,gbf->gaf', tiles_now, picked, preferred_element_type=jnp....]
    all_gather x1 -> x0, blocking collectives: 11.8 us -> none  [local(): panel_rows = lax.all_gather(feats[0], 'row', axis=0, tiled=True)]
  transfers between devices with their start and end apart: 4 -> 28, of which waited for: 4 -> 17; matrix products, arithmetic and copies ran while one was open for 8% -> 0% of each run, Pallas kernels for 0% -> 4%
where the time goes in v1:
time: 78 us; the launch traced here: 77.8 us
  starting transfers between devices  34.7 us (44%)
  waiting for transfers between devices  34 us (44%)
  Pallas kernels  6.46 us (8%)
  between operations  1.47 us (2%)
  local copies, waits for them, and re-layouts  1.15 us (1%)
    ppermute x28, starting transfers between devices, swap(): return lax.ppermute(value, axis, [(i, i ^ mask) for i in range(size)])  34.7 us
    ppermute x28, waiting for transfers between devices, swap(): return lax.ppermute(value, axis, [(i, i ^ mask) for i in range(size)])  34 us
    pallas_call x13, Pallas kernels, call(): pl.pallas_call(kernel, out_shape=outs, in_specs=specs or [VMEM] * len(arg...  6.46 us
  transfers between devices with their start and end apart: 28, of which 17 were waited for; matrix products, arithmetic and copies ran while one was open for 0% of the time, Pallas kernels for 4%

profile of v1, /device:TPU:0, one launch (start us, length us, event | category | flops | bytes accessed | tf_op | source)
XLA Modules:
  0.0 77.8 jit_solution(7858849687463995854)
XLA Ops:
  0.7 4.0 %collective-permute-start.2 = (bf16[128,512]{1,0:T(8,128)(2,1)}, bf16[128,512]{1,0:T(8,128)(2,1)S(1)}, u32[]{:S(2)}, u32[]{:S(2)}) collective-permute-start(bf16[128,512]{1,0:T(8,128)(2,1)} %bitcast.3), channel_id=1, source_target_pairs={{0,24},{8,16},{16,8},{24,0},{1,25},{9,17},{17,9},{25,1},{2,26},{10... | collective-permute-start | bytes 393224 | tf_op jit(solution)/shard_map/ppermute | solution.py:35
  7.1 1.5 %shard_map.94 = (bf16[1024,512]{1,0:T(8,128)(2,1)S(1)}, bf16[512,1024]{1,0:T(8,128)(2,1)S(1)}) custom-call(bf16[1,1,24,128,128]{4,3,2,1,0:T(8,128)(2,1)S(1)} %copy-done, s32[1,1,24]{2,1,0:T(1,128)S(1)} %copy-done.4, s32[1,1,24]{2,1,0:T(1,128)S(1)} %copy-done.5, s32[1,1]{1,0:T(1,128)S(6)} %copy.10.count), custom_call_target="tpu_custom_call" | custom-call | bytes 2883780 | tf_op jit(solution)/shard_map/pallas_call | solution.py:19
  8.8 2.3 %collective-permute-done.1.refs_2_ = bf16[128,512]{1,0:T(8,128)(2,1)S(1)} collective-permute-done((bf16[128,512]{1,0:T(8,128)(2,1)}, bf16[128,512]{1,0:T(8,128)(2,1)S(1)}, u32[]{:S(2)}, u32[]{:S(2)}) %collective-permute-start.1) | collective-permute-done | bytes 131104 | tf_op jit(solution)/shard_map/ppermute | solution.py:35
  12.4 1.4 %collective-permute-done.3.other = bf16[512,512]{1,0:T(8,128)(2,1)S(1)} collective-permute-done((bf16[512,512]{1,0:T(8,128)(2,1)S(1)}, bf16[512,512]{1,0:T(8,128)(2,1)S(1)}, u32[]{:S(2)}, u32[]{:S(2)}) %collective-permute-start.3) | collective-permute-done | bytes 524320 | tf_op jit(solution)/shard_map/ppermute | solution.py:35
  13.9 1.6 %collective-permute-start.4 = (bf16[128,512]{1,0:T(8,128)(2,1)S(1)}, bf16[128,512]{1,0:T(8,128)(2,1)S(1)}, u32[]{:S(2)}, u32[]{:S(2)}) collective-permute-start(bf16[128,512]{1,0:T(8,128)(2,1)S(1)} %get-tuple-element.25), channel_id=1, source_target_pairs={{0,2},{1,3},{2,0},{3,1},{4,6},{5,7},{6,4},{7,5},{8,10},{9,11},{10,... | collective-permute-start | bytes 393224 | tf_op jit(solution)/shard_map/ppermute | solution.py:35
  15.5 2.6 %collective-permute-start.5 = (bf16[128,512]{1,0:T(8,128)(2,1)S(1)}, bf16[128,512]{1,0:T(8,128)(2,1)S(1)}, u32[]{:S(2)}, u32[]{:S(2)}) collective-permute-start(bf16[128,512]{1,0:T(8,128)(2,1)S(1)} %get-tuple-element.26), channel_id=1, source_target_pairs={{0,4},{1,5},{2,6},{3,7},{4,0},{5,1},{6,2},{7,3},{8,12},{9,13},{10,... | collective-permute-start | bytes 393224 | tf_op jit(solution)/shard_map/ppermute | solution.py:35
  18.3 3.1 %collective-permute-done.4.refs_1_ = bf16[128,512]{1,0:T(8,128)(2,1)S(1)} collective-permute-done((bf16[128,512]{1,0:T(8,128)(2,1)S(1)}, bf16[128,512]{1,0:T(8,128)(2,1)S(1)}, u32[]{:S(2)}, u32[]{:S(2)}) %collective-permute-start.4) | collective-permute-done | bytes 131104 | tf_op jit(solution)/shard_map/ppermute | solution.py:35
  21.4 7.0 %collective-permute-done.5.refs_2_ = bf16[128,512]{1,0:T(8,128)(2,1)S(1)} collective-permute-done((bf16[128,512]{1,0:T(8,128)(2,1)S(1)}, bf16[128,512]{1,0:T(8,128)(2,1)S(1)}, u32[]{:S(2)}, u32[]{:S(2)}) %collective-permute-start.5) | collective-permute-done | bytes 131104 | tf_op jit(solution)/shard_map/ppermute | solution.py:35
  29.9 1.5 %collective-permute-done.17.other = bf16[256,512]{1,0:T(8,128)(2,1)S(1)} collective-permute-done((bf16[256,512]{1,0:T(8,128)(2,1)S(1)}, bf16[256,512]{1,0:T(8,128)(2,1)S(1)}, u32[]{:S(2)}, u32[]{:S(2)}) %collective-permute-start.17) | collective-permute-done | bytes 262176 | tf_op jit(solution)/shard_map/ppermute | solution.py:35
  31.5 1.6 %collective-permute-start.18 = (bf16[64,512]{1,0:T(8,128)(2,1)S(1)}, bf16[64,512]{1,0:T(8,128)(2,1)S(1)}, u32[]{:S(2)}, u32[]{:S(2)}) collective-permute-start(bf16[64,512]{1,0:T(8,128)(2,1)S(1)} %get-tuple-element.40), channel_id=1, source_target_pairs={{0,8},{8,0},{16,24},{24,16},{1,9},{9,1},{17,25},{25,17},{2,10},{10... | collective-permute-start | bytes 196616 | tf_op jit(solution)/shard_map/ppermute | solution.py:35
  33.8 1.2 %collective-permute-start.20 = (bf16[64,512]{1,0:T(8,128)(2,1)S(1)}, bf16[64,512]{1,0:T(8,128)(2,1)S(1)}, u32[]{:S(2)}, u32[]{:S(2)}) collective-permute-start(bf16[64,512]{1,0:T(8,128)(2,1)S(1)} %get-tuple-element.42), channel_id=1, source_target_pairs={{0,24},{8,16},{16,8},{24,0},{1,25},{9,17},{17,9},{25,1},{2,26},{10... | collective-permute-start | bytes 196616 | tf_op jit(solution)/shard_map/ppermute | solution.py:35
  35.8 2.2 %collective-permute-done.19.refs_2_ = bf16[64,512]{1,0:T(8,128)(2,1)S(1)} collective-permute-done((bf16[64,512]{1,0:T(8,128)(2,1)S(1)}, bf16[64,512]{1,0:T(8,128)(2,1)S(1)}, u32[]{:S(2)}, u32[]{:S(2)}) %collective-permute-start.19) | collective-permute-done | bytes 65568 | tf_op jit(solution)/shard_map/ppermute | solution.py:35
  39.0 2.5 %collective-permute-start.23 = (bf16[64,512]{1,0:T(8,128)(2,1)S(1)}, bf16[64,512]{1,0:T(8,128)(2,1)S(1)}, u32[]{:S(2)}, u32[]{:S(2)}) collective-permute-start(bf16[64,512]{1,0:T(8,128)(2,1)S(1)} %shard_map.103.refs_0_), channel_id=1, source_target_pairs={{0,6},{1,7},{2,4},{3,5},{4,2},{5,3},{6,0},{7,1},{8,14},{9,15},{10,... | collective-permute-start | bytes 196616 | tf_op jit(solution)/shard_map/ppermute | solution.py:35
  41.5 1.4 %collective-permute-start.9 = (bf16[128,512]{1,0:T(8,128)(2,1)S(1)}, bf16[128,512]{1,0:T(8,128)(2,1)S(1)}, u32[]{:S(2)}, u32[]{:S(2)}) collective-permute-start(bf16[128,512]{1,0:T(8,128)(2,1)S(1)} %get-tuple-element.30.refs_0_), channel_id=1, source_target_pairs={{0,6},{1,7},{2,4},{3,5},{4,2},{5,3},{6,0},{7,1},{8,14},{9,15},{10,... | collective-permute-start | bytes 393224 | tf_op jit(solution)/shard_map/ppermute | solution.py:35
  42.9 1.5 %collective-permute-start.8 = (bf16[128,512]{1,0:T(8,128)(2,1)S(1)}, bf16[128,512]{1,0:T(8,128)(2,1)S(1)}, u32[]{:S(2)}, u32[]{:S(2)}) collective-permute-start(bf16[128,512]{1,0:T(8,128)(2,1)S(1)} %get-tuple-element.30.refs_0_), channel_id=1, source_target_pairs={{0,4},{1,5},{2,6},{3,7},{4,0},{5,1},{6,2},{7,3},{8,12},{9,13},{10,... | collective-permute-start | bytes 393224 | tf_op jit(solution)/shard_map/ppermute | solution.py:35
  44.4 1.5 %collective-permute-start.7 = (bf16[128,512]{1,0:T(8,128)(2,1)S(1)}, bf16[128,512]{1,0:T(8,128)(2,1)S(1)}, u32[]{:S(2)}, u32[]{:S(2)}) collective-permute-start(bf16[128,512]{1,0:T(8,128)(2,1)S(1)} %get-tuple-element.30.refs_0_), channel_id=1, source_target_pairs={{0,2},{1,3},{2,0},{3,1},{4,6},{5,7},{6,4},{7,5},{8,10},{9,11},{10,... | collective-permute-start | bytes 393224 | tf_op jit(solution)/shard_map/ppermute | solution.py:35
  46.3 7.0 %collective-permute-start.21 = (bf16[64,512]{1,0:T(8,128)(2,1)S(1)}, bf16[64,512]{1,0:T(8,128)(2,1)S(1)}, u32[]{:S(2)}, u32[]{:S(2)}) collective-permute-start(bf16[64,512]{1,0:T(8,128)(2,1)S(1)} %shard_map.103.refs_0_), channel_id=1, source_target_pairs={{0,2},{1,3},{2,0},{3,1},{4,6},{5,7},{6,4},{7,5},{8,10},{9,11},{10,... | collective-permute-start | bytes 196616 | tf_op jit(solution)/shard_map/ppermute | solution.py:35
  53.3 5.5 %collective-permute-done.22.refs_2_ = bf16[64,512]{1,0:T(8,128)(2,1)S(1)} collective-permute-done((bf16[64,512]{1,0:T(8,128)(2,1)S(1)}, bf16[64,512]{1,0:T(8,128)(2,1)S(1)}, u32[]{:S(2)}, u32[]{:S(2)}) %collective-permute-start.22) | collective-permute-done | bytes 65568 | tf_op jit(solution)/shard_map/ppermute | solution.py:35
  58.8 1.4 %collective-permute-start.26 = (bf16[64,512]{1,0:T(8,128)(2,1)S(1)}, bf16[64,512]{1,0:T(8,128)(2,1)S(1)}, u32[]{:S(2)}, u32[]{:S(2)}) collective-permute-start(bf16[64,512]{1,0:T(8,128)(2,1)S(1)} %shard_map.104.refs_0_), channel_id=1, source_target_pairs={{0,24},{8,16},{16,8},{24,0},{1,25},{9,17},{17,9},{25,1},{2,26},{10... | collective-permute-start | bytes 196616 | tf_op jit(solution)/shard_map/ppermute | solution.py:35
  60.2 1.3 %collective-permute-start.25 = (bf16[64,512]{1,0:T(8,128)(2,1)S(1)}, bf16[64,512]{1,0:T(8,128)(2,1)S(1)}, u32[]{:S(2)}, u32[]{:S(2)}) collective-permute-start(bf16[64,512]{1,0:T(8,128)(2,1)S(1)} %shard_map.104.refs_0_), channel_id=1, source_target_pairs={{0,16},{8,24},{16,0},{24,8},{1,17},{9,25},{17,1},{25,9},{2,18},{10... | collective-permute-start | bytes 196616 | tf_op jit(solution)/shard_map/ppermute | solution.py:35
  66.8 1.2 %collective-permute-start.14 = (bf16[128,512]{1,0:T(8,128)(2,1)S(1)}, bf16[128,512]{1,0:T(8,128)(2,1)S(1)}, u32[]{:S(2)}, u32[]{:S(2)}) collective-permute-start(bf16[128,512]{1,0:T(8,128)(2,1)S(1)} %get-tuple-element.32), channel_id=1, source_target_pairs={{0,8},{8,0},{16,24},{24,16},{1,9},{9,1},{17,25},{25,17},{2,10},{10... | collective-permute-start | bytes 393224 | tf_op jit(solution)/shard_map/ppermute | solution.py:35
  68.8 1.6 %collective-permute-start.16 = (bf16[128,512]{1,0:T(8,128)(2,1)S(1)}, bf16[128,512]{1,0:T(8,128)(2,1)S(1)}, u32[]{:S(2)}, u32[]{:S(2)}) collective-permute-start(bf16[128,512]{1,0:T(8,128)(2,1)S(1)} %get-tuple-element.34), channel_id=1, source_target_pairs={{0,24},{8,16},{16,8},{24,0},{1,25},{9,17},{17,9},{25,1},{2,26},{10... | collective-permute-start | bytes 393224 | tf_op jit(solution)/shard_map/ppermute | solution.py:35
  70.3 2.8 %collective-permute-done.14.refs_1_ = bf16[128,512]{1,0:T(8,128)(2,1)S(1)} collective-permute-done((bf16[128,512]{1,0:T(8,128)(2,1)S(1)}, bf16[128,512]{1,0:T(8,128)(2,1)S(1)}, u32[]{:S(2)}, u32[]{:S(2)}) %collective-permute-start.14) | collective-permute-done | bytes 131104 | tf_op jit(solution)/shard_map/ppermute | solution.py:35
  73.2 2.9 %collective-permute-done.15.refs_2_ = bf16[128,512]{1,0:T(8,128)(2,1)S(1)} collective-permute-done((bf16[128,512]{1,0:T(8,128)(2,1)S(1)}, bf16[128,512]{1,0:T(8,128)(2,1)S(1)}, u32[]{:S(2)}, u32[]{:S(2)}) %collective-permute-start.15) | collective-permute-done | bytes 131104 | tf_op jit(solution)/shard_map/ppermute | solution.py:35
  (57 shorter events, 15.7 us)
Async XLA Ops:
  0.7 8.2 %collective-permute-start.2 = (bf16[128,512]{1,0:T(8,128)(2,1)}, bf16[128,512]{1,0:T(8,128)(2,1)S(1)}, u32[]{:S(2)}, u32[]{:S(2)}) collective-permute-start(bf16[128,512]{1,0:T(8,128)(2,1)} %bitcast.3), channel_id=1, source_target_pairs={{0,24},{8,16},{16,8},{24,0},{1,25},{9,17},{17,9},{25,1},{2,26},{10... | collective-permute-start | bytes 393224 | tf_op jit(solution)/shard_map/ppermute | solution.py:35
  4.6 6.5 %collective-permute-start.1 = (bf16[128,512]{1,0:T(8,128)(2,1)}, bf16[128,512]{1,0:T(8,128)(2,1)S(1)}, u32[]{:S(2)}, u32[]{:S(2)}) collective-permute-start(bf16[128,512]{1,0:T(8,128)(2,1)} %bitcast.4), channel_id=1, source_target_pairs={{0,16},{8,24},{16,0},{24,8},{1,17},{9,25},{17,1},{25,9},{2,18},{10... | collective-permute-start | bytes 393224 | tf_op jit(solution)/shard_map/ppermute | solution.py:35
  5.1 6.3 %collective-permute-start = (bf16[128,512]{1,0:T(8,128)(2,1)}, bf16[128,512]{1,0:T(8,128)(2,1)S(1)}, u32[]{:S(2)}, u32[]{:S(2)}) collective-permute-start(bf16[128,512]{1,0:T(8,128)(2,1)} %bitcast.5), channel_id=1, source_target_pairs={{0,8},{8,0},{16,24},{24,16},{1,9},{9,1},{17,25},{25,17},{2,10},{10... | collective-permute-start | bytes 393224 | tf_op jit(solution)/shard_map/ppermute | solution.py:35
  13.9 7.5 %collective-permute-start.4 = (bf16[128,512]{1,0:T(8,128)(2,1)S(1)}, bf16[128,512]{1,0:T(8,128)(2,1)S(1)}, u32[]{:S(2)}, u32[]{:S(2)}) collective-permute-start(bf16[128,512]{1,0:T(8,128)(2,1)S(1)} %get-tuple-element.25), channel_id=1, source_target_pairs={{0,2},{1,3},{2,0},{3,1},{4,6},{5,7},{6,4},{7,5},{8,10},{9,11},{10,... | collective-permute-start | bytes 393224 | tf_op jit(solution)/shard_map/ppermute | solution.py:35
  15.5 12.9 %collective-permute-start.5 = (bf16[128,512]{1,0:T(8,128)(2,1)S(1)}, bf16[128,512]{1,0:T(8,128)(2,1)S(1)}, u32[]{:S(2)}, u32[]{:S(2)}) collective-permute-start(bf16[128,512]{1,0:T(8,128)(2,1)S(1)} %get-tuple-element.26), channel_id=1, source_target_pairs={{0,4},{1,5},{2,6},{3,7},{4,0},{5,1},{6,2},{7,3},{8,12},{9,13},{10,... | collective-permute-start | bytes 393224 | tf_op jit(solution)/shard_map/ppermute | solution.py:35
  18.1 10.3 %collective-permute-start.6 = (bf16[128,512]{1,0:T(8,128)(2,1)S(1)}, bf16[128,512]{1,0:T(8,128)(2,1)S(1)}, u32[]{:S(2)}, u32[]{:S(2)}) collective-permute-start(bf16[128,512]{1,0:T(8,128)(2,1)S(1)} %get-tuple-element.27), channel_id=1, source_target_pairs={{0,6},{1,7},{2,4},{3,5},{4,2},{5,3},{6,0},{7,1},{8,14},{9,15},{10,... | collective-permute-start | bytes 393224 | tf_op jit(solution)/shard_map/ppermute | solution.py:35
  31.5 4.3 %collective-permute-start.18 = (bf16[64,512]{1,0:T(8,128)(2,1)S(1)}, bf16[64,512]{1,0:T(8,128)(2,1)S(1)}, u32[]{:S(2)}, u32[]{:S(2)}) collective-permute-start(bf16[64,512]{1,0:T(8,128)(2,1)S(1)} %get-tuple-element.40), channel_id=1, source_target_pairs={{0,8},{8,0},{16,24},{24,16},{1,9},{9,1},{17,25},{25,17},{2,10},{10... | collective-permute-start | bytes 196616 | tf_op jit(solution)/shard_map/ppermute | solution.py:35
  33.1 5.0 %collective-permute-start.19 = (bf16[64,512]{1,0:T(8,128)(2,1)S(1)}, bf16[64,512]{1,0:T(8,128)(2,1)S(1)}, u32[]{:S(2)}, u32[]{:S(2)}) collective-permute-start(bf16[64,512]{1,0:T(8,128)(2,1)S(1)} %get-tuple-element.41), channel_id=1, source_target_pairs={{0,16},{8,24},{16,0},{24,8},{1,17},{9,25},{17,1},{25,9},{2,18},{10... | collective-permute-start | bytes 196616 | tf_op jit(solution)/shard_map/ppermute | solution.py:35
  33.8 5.2 %collective-permute-start.20 = (bf16[64,512]{1,0:T(8,128)(2,1)S(1)}, bf16[64,512]{1,0:T(8,128)(2,1)S(1)}, u32[]{:S(2)}, u32[]{:S(2)}) collective-permute-start(bf16[64,512]{1,0:T(8,128)(2,1)S(1)} %get-tuple-element.42), channel_id=1, source_target_pairs={{0,24},{8,16},{16,8},{24,0},{1,25},{9,17},{17,9},{25,1},{2,26},{10... | collective-permute-start | bytes 196616 | tf_op jit(solution)/shard_map/ppermute | solution.py:35
  39.0 7.3 %collective-permute-start.23 = (bf16[64,512]{1,0:T(8,128)(2,1)S(1)}, bf16[64,512]{1,0:T(8,128)(2,1)S(1)}, u32[]{:S(2)}, u32[]{:S(2)}) collective-permute-start(bf16[64,512]{1,0:T(8,128)(2,1)S(1)} %shard_map.103.refs_0_), channel_id=1, source_target_pairs={{0,6},{1,7},{2,4},{3,5},{4,2},{5,3},{6,0},{7,1},{8,14},{9,15},{10,... | collective-permute-start | bytes 196616 | tf_op jit(solution)/shard_map/ppermute | solution.py:35
  41.5 20.0 %collective-permute-start.9 = (bf16[128,512]{1,0:T(8,128)(2,1)S(1)}, bf16[128,512]{1,0:T(8,128)(2,1)S(1)}, u32[]{:S(2)}, u32[]{:S(2)}) collective-permute-start(bf16[128,512]{1,0:T(8,128)(2,1)S(1)} %get-tuple-element.30.refs_0_), channel_id=1, source_target_pairs={{0,6},{1,7},{2,4},{3,5},{4,2},{5,3},{6,0},{7,1},{8,14},{9,15},{10,... | collective-permute-start | bytes 393224 | tf_op jit(solution)/shard_map/ppermute | solution.py:35
  42.9 19.5 %collective-permute-start.8 = (bf16[128,512]{1,0:T(8,128)(2,1)S(1)}, bf16[128,512]{1,0:T(8,128)(2,1)S(1)}, u32[]{:S(2)}, u32[]{:S(2)}) collective-permute-start(bf16[128,512]{1,0:T(8,128)(2,1)S(1)} %get-tuple-element.30.refs_0_), channel_id=1, source_target_pairs={{0,4},{1,5},{2,6},{3,7},{4,0},{5,1},{6,2},{7,3},{8,12},{9,13},{10,... | collective-permute-start | bytes 393224 | tf_op jit(solution)/shard_map/ppermute | solution.py:35
  44.4 18.0 %collective-permute-start.7 = (bf16[128,512]{1,0:T(8,128)(2,1)S(1)}, bf16[128,512]{1,0:T(8,128)(2,1)S(1)}, u32[]{:S(2)}, u32[]{:S(2)}) collective-permute-start(bf16[128,512]{1,0:T(8,128)(2,1)S(1)} %get-tuple-element.30.refs_0_), channel_id=1, source_target_pairs={{0,2},{1,3},{2,0},{3,1},{4,6},{5,7},{6,4},{7,5},{8,10},{9,11},{10,... | collective-permute-start | bytes 393224 | tf_op jit(solution)/shard_map/ppermute | solution.py:35
  45.9 12.9 %collective-permute-start.22 = (bf16[64,512]{1,0:T(8,128)(2,1)S(1)}, bf16[64,512]{1,0:T(8,128)(2,1)S(1)}, u32[]{:S(2)}, u32[]{:S(2)}) collective-permute-start(bf16[64,512]{1,0:T(8,128)(2,1)S(1)} %shard_map.103.refs_0_), channel_id=1, source_target_pairs={{0,4},{1,5},{2,6},{3,7},{4,0},{5,1},{6,2},{7,3},{8,12},{9,13},{10,... | collective-permute-start | bytes 196616 | tf_op jit(solution)/shard_map/ppermute | solution.py:35
  46.3 12.5 %collective-permute-start.21 = (bf16[64,512]{1,0:T(8,128)(2,1)S(1)}, bf16[64,512]{1,0:T(8,128)(2,1)S(1)}, u32[]{:S(2)}, u32[]{:S(2)}) collective-permute-start(bf16[64,512]{1,0:T(8,128)(2,1)S(1)} %shard_map.103.refs_0_), channel_id=1, source_target_pairs={{0,2},{1,3},{2,0},{3,1},{4,6},{5,7},{6,4},{7,5},{8,10},{9,11},{10,... | collective-permute-start | bytes 196616 | tf_op jit(solution)/shard_map/ppermute | solution.py:35
  58.8 5.3 %collective-permute-start.26 = (bf16[64,512]{1,0:T(8,128)(2,1)S(1)}, bf16[64,512]{1,0:T(8,128)(2,1)S(1)}, u32[]{:S(2)}, u32[]{:S(2)}) collective-permute-start(bf16[64,512]{1,0:T(8,128)(2,1)S(1)} %shard_map.104.refs_0_), channel_id=1, source_target_pairs={{0,24},{8,16},{16,8},{24,0},{1,25},{9,17},{17,9},{25,1},{2,26},{10... | collective-permute-start | bytes 196616 | tf_op jit(solution)/shard_map/ppermute | solution.py:35
  60.2 4.5 %collective-permute-start.25 = (bf16[64,512]{1,0:T(8,128)(2,1)S(1)}, bf16[64,512]{1,0:T(8,128)(2,1)S(1)}, u32[]{:S(2)}, u32[]{:S(2)}) collective-permute-start(bf16[64,512]{1,0:T(8,128)(2,1)S(1)} %shard_map.104.refs_0_), channel_id=1, source_target_pairs={{0,16},{8,24},{16,0},{24,8},{1,17},{9,25},{17,1},{25,9},{2,18},{10... | collective-permute-start | bytes 196616 | tf_op jit(solution)/shard_map/ppermute | solution.py:35
  61.5 4.3 %collective-permute-start.24 = (bf16[64,512]{1,0:T(8,128)(2,1)S(1)}, bf16[64,512]{1,0:T(8,128)(2,1)S(1)}, u32[]{:S(2)}, u32[]{:S(2)}) collective-permute-start(bf16[64,512]{1,0:T(8,128)(2,1)S(1)} %shard_map.104.refs_0_), channel_id=1, source_target_pairs={{0,8},{8,0},{16,24},{24,16},{1,9},{9,1},{17,25},{25,17},{2,10},{10... | collective-permute-start | bytes 196616 | tf_op jit(solution)/shard_map/ppermute | solution.py:35
  62.4 3.5 %collective-permute-start.10 = (bf16[128,512]{1,0:T(8,128)(2,1)S(1)}, bf16[128,512]{1,0:T(8,128)(2,1)S(1)}, u32[]{:S(2)}, u32[]{:S(2)}) collective-permute-start(bf16[128,512]{1,0:T(8,128)(2,1)S(1)} %get-tuple-element.30.refs_0_), channel_id=1, source_target_pairs={{0,1},{1,0},{2,3},{3,2},{4,5},{5,4},{6,7},{7,6},{8,9},{9,8},{10,11... | collective-permute-start | bytes 393224 | tf_op jit(solution)/shard_map/ppermute | solution.py:35
  62.4 3.5 %collective-permute-start.13 = (bf16[128,512]{1,0:T(8,128)(2,1)S(1)}, bf16[128,512]{1,0:T(8,128)(2,1)S(1)}, u32[]{:S(2)}, u32[]{:S(2)}) collective-permute-start(bf16[128,512]{1,0:T(8,128)(2,1)S(1)} %collective-permute-done.9.refs_3_), channel_id=1, source_target_pairs={{0,1},{1,0},{2,3},{3,2},{4,5},{5,4},{6,7},{7,6},{8,9},{9,8},{10,11... | collective-permute-start | bytes 393224 | tf_op jit(solution)/shard_map/ppermute | solution.py:35
  65.8 11.0 %collective-permute-start.27 = (bf16[256,512]{1,0:T(8,128)(2,1)S(1)}, bf16[256,512]{1,0:T(8,128)(2,1)S(1)}, u32[]{:S(2)}, u32[]{:S(2)}) collective-permute-start(bf16[256,512]{1,0:T(8,128)(2,1)S(1)} %shard_map.105.mine), channel_id=1, source_target_pairs={{0,1},{1,0},{2,3},{3,2},{4,5},{5,4},{6,7},{7,6},{8,9},{9,8},{10,11... | collective-permute-start | bytes 786440 | tf_op jit(solution)/shard_map/ppermute | solution.py:35
  66.8 6.4 %collective-permute-start.14 = (bf16[128,512]{1,0:T(8,128)(2,1)S(1)}, bf16[128,512]{1,0:T(8,128)(2,1)S(1)}, u32[]{:S(2)}, u32[]{:S(2)}) collective-permute-start(bf16[128,512]{1,0:T(8,128)(2,1)S(1)} %get-tuple-element.32), channel_id=1, source_target_pairs={{0,8},{8,0},{16,24},{24,16},{1,9},{9,1},{17,25},{25,17},{2,10},{10... | collective-permute-start | bytes 393224 | tf_op jit(solution)/shard_map/ppermute | solution.py:35
  68.0 8.1 %collective-permute-start.15 = (bf16[128,512]{1,0:T(8,128)(2,1)S(1)}, bf16[128,512]{1,0:T(8,128)(2,1)S(1)}, u32[]{:S(2)}, u32[]{:S(2)}) collective-permute-start(bf16[128,512]{1,0:T(8,128)(2,1)S(1)} %get-tuple-element.33), channel_id=1, source_target_pairs={{0,16},{8,24},{16,0},{24,8},{1,17},{9,25},{17,1},{25,9},{2,18},{10... | collective-permute-start | bytes 393224 | tf_op jit(solution)/shard_map/ppermute | solution.py:35
  68.8 7.3 %collective-permute-start.16 = (bf16[128,512]{1,0:T(8,128)(2,1)S(1)}, bf16[128,512]{1,0:T(8,128)(2,1)S(1)}, u32[]{:S(2)}, u32[]{:S(2)}) collective-permute-start(bf16[128,512]{1,0:T(8,128)(2,1)S(1)} %get-tuple-element.34), channel_id=1, source_target_pairs={{0,24},{8,16},{16,8},{24,0},{1,25},{9,17},{17,9},{25,1},{2,26},{10... | collective-permute-start | bytes 393224 | tf_op jit(solution)/shard_map/ppermute | solution.py:35
  (10 other events, 54.9 us)

commit v2 on v1

--- a/solution.py
+++ b/solution.py
@@ -14,17 +14,22 @@
 TILE = 128
 
 
-def call(kernel, outs, args, specs=None, scratch=(), work=0):
+def call(kernel, outs, args, specs=None, scratch=(), after=(), alias={}, us=0):
     held = sum(a.size * a.dtype.itemsize for a in (*args, *outs))
+
+    def body(*refs):
+        kernel(*refs[: len(args)], *refs[len(args) + len(after) :])
+
     return pl.pallas_call(
-        kernel,
+        body,
         out_shape=outs,
-        in_specs=specs or [VMEM] * len(args),
+        in_specs=(specs or [VMEM] * len(args)) + [pl.BlockSpec(memory_space=pl.ANY)] * len(after),
+        input_output_aliases=alias,
         out_specs=[VMEM] * len(outs),
         scratch_shapes=scratch,
         compiler_params=pltpu.CompilerParams(vmem_limit_bytes=12 * 2**20 + 3 * held),
-        cost_estimate=pl.CostEstimate(flops=work, bytes_accessed=held, transcendentals=0),
-    )(*args)
+        cost_estimate=pl.CostEstimate(flops=int(us * 1.15e9), bytes_accessed=0, transcendentals=0),
+    )(*args, *after)
 
 
 def like(*shape, dtype=BF16):
@@ -37,22 +42,32 @@
 
 def tree(terms):
     while len(terms) > 1:
-        terms = [terms[i] + terms[i + 1] for i in range(0, len(terms), 2)]
+        terms = [sum(terms[i + 1 : i + 2], terms[i]) for i in range(0, len(terms), 2)]
     return terms[0]
 
 
-def densify(n_z, values, rows, cols, count, dense, dense_t):
+def densify(n_z, values, rows, cols, count, dense, dense_t, other_t):
     me_row, me_col = lax.axis_index("row"), lax.axis_index("col")
     dense[...] = jnp.zeros_like(dense)
     dense_t[...] = jnp.zeros_like(dense_t)
+    other_t[...] = jnp.zeros_like(other_t)
 
     def place(s, carry):
         far = rows[0, 0, s] ^ me_col
-        at = pl.multiple_of(((far & 1) * n_z + (far >> 1)) * TILE, TILE)
+        inside = pl.multiple_of((far >> 1) * TILE, TILE)
+        at = pl.multiple_of((far & 1) * n_z * TILE + inside, TILE)
         to = pl.multiple_of((cols[0, 0, s] ^ me_row) * TILE, TILE)
         tile = values[0, 0, s]
         dense[pl.ds(at, TILE), pl.ds(to, TILE)] = tile
-        dense_t[pl.ds(to, TILE), pl.ds(at, TILE)] = tile.T
+
+        @pl.when((far & 1) == 0)
+        def _():
+            dense_t[pl.ds(to, TILE), pl.ds(inside, TILE)] = tile.T
+
+        @pl.when((far & 1) == 1)
+        def _():
+            other_t[pl.ds(to, TILE), pl.ds(inside, TILE)] = tile.T
+
         return carry
 
     lax.fori_loop(0, count[0, 0], place, 0)
@@ -74,13 +89,17 @@
         out[...] = (mine[part, :].astype(F32) + other[part, :].astype(F32)).astype(out.dtype)
 
 
+def relay(value, out):
+    pass
+
+
 def add_all(*refs):
     *terms, out = refs
     out[...] = tree([t[...].astype(F32) for t in terms]).astype(out.dtype)
 
 
-def dense_layer(n_z, weight, cotangent, *refs):
-    terms, (layer_out, summed, hidden_grad, grad_rows) = refs[:n_z], refs[n_z:]
+def dense_layer(weight, cotangent, *refs):
+    *terms, layer_out, summed, hidden_grad, grad_rows = refs
     total = tree([t[...].astype(F32) for t in terms]).astype(BF16)
     summed[...] = total
     hidden = jnp.dot(total, weight[...], preferred_element_type=F32)
@@ -112,21 +131,36 @@
         other[part, :] = whole[pl.ds(at, piece), :].astype(BF16)
 
 
-def backward(n_z, dense_t, *refs):
-    grads, outs = refs[: 2 * n_z], refs[2 * n_z :]
+def backward(dense_t, *refs):
+    *grads, out = refs
     panel = jnp.concatenate([g[...] for g in grads], axis=0)
-    total = jnp.dot(dense_t[...], panel, preferred_element_type=F32)
+    out[...] = jnp.dot(dense_t[...], panel, preferred_element_type=F32).astype(out.dtype)
+
+
+def messages(mine, other, final_w, own, *outs):
+    own[...] = mine[:TILE, :] + other[:TILE, :].astype(F32)
     for k, out in enumerate(outs):
-        out[...] = total[k * TILE : (k + 1) * TILE].astype(out.dtype)
-
-
-def join(*refs):
-    *pieces, out = refs
+        part = pl.ds((k + 1) * TILE, TILE)
+        out[:TILE, :] = (mine[part, :] + other[part, :].astype(F32)).astype(BF16)
+        out[TILE:, :] = final_w[...]
+
+
+def add_rows(own, *refs):
+    *terms, out = refs
+    total = own[...]
+    for t in terms:
+        total += t[:TILE, :].astype(F32)
+    out[...] = total.astype(BF16)
+
+
+def join(own, *refs):
+    *others, out = refs
     me_row = lax.axis_index("row")
-    piece = pieces[0].shape[0]
-    for k, ref in enumerate(pieces):
-        at = pl.multiple_of((me_row ^ k) * piece, piece)
-        out[pl.ds(at, piece), :] = ref[...]
+    piece = own.shape[0]
+    out[pl.ds(pl.multiple_of(me_row * piece, piece), piece), :] = own[...]
+    for k, ref in enumerate(others):
+        at = pl.multiple_of((me_row ^ (k + 1)) * piece, piece)
+        out[pl.ds(at, piece), :] = ref[TILE:, :]
 
 
 def spread(mine, other, out):
@@ -148,59 +182,82 @@
 
     own = feats[0]
     panel = [own] + [row_swap(own, k) for k in range(1, n_row)]
-    dense, dense_t = call(
+    dense, dense_t, other_t = call(
         functools.partial(densify, n_z),
-        [like(row_nodes, col_nodes), like(col_nodes, row_nodes)],
+        [like(row_nodes, col_nodes), like(col_nodes, half), like(col_nodes, half)],
         (tile_values, tile_rows, tile_cols, tile_count),
         specs=[VMEM, SMEM, SMEM, SMEM],
     )
-    work = 2 * half * col_nodes * width
-    (other,) = call(functools.partial(forward, half), [like(half, width)], (dense, *panel), work=work)
+    other_t = core_swap(other_t)
+    (other,) = call(functools.partial(forward, half), [like(half, width)], (dense, *panel))
     other = core_swap(other)
     (mine,) = call(
-        functools.partial(forward, 0), [like(half, width, dtype=F32)], (dense, *panel), work=work
-    )
-    parts = call(
-        add_split,
-        [like(TILE, width, dtype=F32)] + [like(TILE, width)] * (n_z - 1),
-        (mine, other),
-    )
-    terms = [parts[0]] + [z_swap(parts[k], k) for k in range(1, n_z)]
+        functools.partial(forward, 0), [like(half, width, dtype=F32)], (dense, *panel)
+    )
+    parts = list(
+        call(
+            add_split,
+            [like(TILE, width, dtype=F32)] + [like(TILE, width)] * (n_z - 1),
+            (mine, other),
+        )
+    )
+    bit, extra = 1, []
+    while bit < n_z:
+        far = [k for k in range(n_z) if k & bit and k % bit == 0]
+        for k in sorted(far, reverse=True):
+            got = z_swap(parts[k], bit)
+            if k == bit:
+                extra.append(got)
+            else:
+                (parts[k ^ bit],) = call(add_all, [like(TILE, width)], (parts[k ^ bit], got))
+        bit *= 2
+    terms = [parts[0]] + extra
     layer_out, summed, hidden_grad, grad_rows = call(
-        functools.partial(dense_layer, n_z),
+        dense_layer,
         [like(TILE, width)] * 4,
         (weight, cotangent, *terms),
-        work=4 * TILE * width * width,
-    )
-    same = [grad_rows] + [z_swap(grad_rows, k) for k in range(1, n_z)]
-    cross = [core_swap(g) for g in same]
-
+        after=(other_t,),
+    )
     piece = width // 2 // n_row
     mine_w, other_w = call(
         functools.partial(weight_term, n_row, (n_row * n_col * TILE) ** -0.5),
         [like(width // 2, width, dtype=F32), like(width // 2, width)],
         (summed, hidden_grad),
         scratch=[pltpu.VMEM((width, width), F32)],
-        work=2 * TILE * width * width,
     )
     other_w = core_swap(other_w)
     parts_w = call(add_split, [like(piece, width)] * n_row, (mine_w, other_w))
     terms_w = [parts_w[0]] + [row_swap(parts_w[k], k) for k in range(1, n_row)]
+    same = [grad_rows] + [None] * (n_z - 1)
+    bit = n_z // 2
+    while bit:
+        for k in range(0, n_z, 2 * bit):
+            same[k | bit] = z_swap(same[k], bit)
+            if bit > 1:
+                (same[k | bit],) = call(
+                    relay,
+                    [like(TILE, width)],
+                    (same[k | bit],),
+                    after=terms_w[1 : n_row - 1],
+                    alias={0: 0},
+                )
+        bit //= 2
     (plane_w,) = call(add_all, [like(piece, width)], terms_w)
     terms_w = [plane_w] + [z_swap(plane_w, k) for k in range(1, n_z)]
-    (final_w,) = call(add_all, [like(piece, width)], terms_w)
-    pieces_w = [final_w] + [row_swap(final_w, k) for k in range(1, n_row)]
-    (half_w,) = call(join, [like(width // 2, width)], pieces_w)
-    (weight_grad,) = call(spread, [like(width, width, dtype=F32)], (half_w, core_swap(half_w)))
-
-    back = call(
-        functools.partial(backward, n_z),
-        [like(TILE, width, dtype=F32)] + [like(TILE, width)] * (n_row - 1),
-        (dense_t, *same, *cross),
-        work=2 * work,
-    )
-    terms = [back[0]] + [row_swap(back[k], k) for k in range(1, n_row)]
-    (feat_grad,) = call(add_all, [like(TILE, width)], terms)
+    (final_w,) = call(add_all, [like(piece, width)], terms_w, us=5)
+    (other,) = call(backward, [like(col_nodes, width)], (other_t, *same))
+    other = core_swap(other)
+    (mine,) = call(backward, [like(col_nodes, width, dtype=F32)], (dense_t, *same))
+    back, *parts = call(
+        messages,
+        [like(TILE, width, dtype=F32)] + [like(TILE + piece, width)] * (n_row - 1),
+        (mine, other, final_w),
+    )
+    terms = [row_swap(part, k + 1) for k, part in enumerate(parts)]
+    (half_w,) = call(join, [like(width // 2, width)], (final_w, *terms))
+    other_w = core_swap(half_w)
+    (feat_grad,) = call(add_rows, [like(TILE, width)], (back, *terms), after=(half_w,))
+    (weight_grad,) = call(spread, [like(width, width, dtype=F32)], (half_w, other_w))
     return layer_out[None], feat_grad[None], weight_grad
 
 

time: 78 us -> 63.9 us (0.82)
  starting transfers between devices: 34.7 us -> 25.1 us
  waiting for transfers between devices: 34 us -> 28.2 us
  Pallas kernels: 6.46 us -> 7.86 us
    ppermute x28 -> x23, starting transfers between devices: 34.7 us -> 25.1 us  [swap(): return lax.ppermute(value, axis, [(i, i ^ mask) for i in range(size)])]
    ppermute x28 -> x23, waiting for transfers between devices: 34 us -> 28.2 us  [swap(): return lax.ppermute(value, axis, [(i, i ^ mask) for i in range(size)])]
    pallas_call x13 -> x17, Pallas kernels: 6.46 us -> 7.86 us  [call(): pl.pallas_call(body, out_shape=outs, in_specs=(specs or [VMEM] * len(args...]
  transfers between devices with their start and end apart: 28 -> 23, of which waited for: 17 -> 14; matrix products, arithmetic and copies ran while one was open for 0% -> 0% of each run, Pallas kernels for 4% -> 8%
where the time goes in v2:
time: 63.9 us; the launch traced here: 63.8 us
  waiting for transfers between devices  28.2 us (44%)
  starting transfers between devices  25.1 us (39%)
  Pallas kernels  7.86 us (12%)
  between operations  1.46 us (2%)
  local copies, waits for them, and re-layouts  1.15 us (2%)
    ppermute x23, waiting for transfers between devices, swap(): return lax.ppermute(value, axis, [(i, i ^ mask) for i in range(size)])  28.2 us
    ppermute x23, starting transfers between devices, swap(): return lax.ppermute(value, axis, [(i, i ^ mask) for i in range(size)])  25.1 us
    pallas_call x17, Pallas kernels, call(): pl.pallas_call(body, out_shape=outs, in_specs=(specs or [VMEM] * len(args...  7.86 us
  transfers between devices with their start and end apart: 23, of which 14 were waited for; matrix products, arithmetic and copies ran while one was open for 0% of the time, Pallas kernels for 8%

profile of v2, /device:TPU:0, one launch (start us, length us, event | category | flops | bytes accessed | tf_op | source)
XLA Modules:
  0.0 63.8 jit_solution(6999510174229992895)
XLA Ops:
  0.7 4.0 %collective-permute-start.2 = (bf16[128,512]{1,0:T(8,128)(2,1)}, bf16[128,512]{1,0:T(8,128)(2,1)S(1)}, u32[]{:S(2)}, u32[]{:S(2)}) collective-permute-start(bf16[128,512]{1,0:T(8,128)(2,1)} %bitcast.3), channel_id=1, source_target_pairs={{0,24},{8,16},{16,8},{24,0},{1,25},{9,17},{17,9},{25,1},{2,26},{10... | collective-permute-start | bytes 393224 | tf_op jit(solution)/shard_map/ppermute | solution.py:40
  5.9 1.1 %copy-done = bf16[1,1,24,128,128]{4,3,2,1,0:T(8,128)(2,1)S(1)} copy-done((bf16[1,1,24,128,128]{4,3,2,1,0:T(8,128)(2,1)S(1)}, bf16[1,1,24,128,128]{4,3,2,1,0:T(8,128)(2,1)}, u32[]{:S(2)}) %copy-start) | copy-done | bytes 786456
  7.1 2.6 %shard_map.94 = (bf16[1024,512]{1,0:T(8,128)(2,1)S(1)}, bf16[512,512]{1,0:T(8,128)(2,1)S(1)}, bf16[512,512]{1,0:T(8,128)(2,1)S(1)}) custom-call(bf16[1,1,24,128,128]{4,3,2,1,0:T(8,128)(2,1)S(1)} %copy-done, s32[1,1,24]{2,1,0:T(1,128)S(1)} %copy-done.4, s32[1,1,24]{2,1,0:T(1,128)S(1)} %copy-done.5, s32[1,1]{1,0:T(1,128)S(6)} %copy.12.refs_3_), custom_call_target="tpu_custom_call" | custom-call | tf_op jit(solution)/shard_map/pallas_call | solution.py:23
  9.7 1.4 %collective-permute-done.1.refs_3_ = bf16[128,512]{1,0:T(8,128)(2,1)S(1)} collective-permute-done((bf16[128,512]{1,0:T(8,128)(2,1)}, bf16[128,512]{1,0:T(8,128)(2,1)S(1)}, u32[]{:S(2)}, u32[]{:S(2)}) %collective-permute-start.1) | collective-permute-done | bytes 131104 | tf_op jit(solution)/shard_map/ppermute | solution.py:40
  12.8 1.0 %collective-permute-done.3.refs_1_ = bf16[512,512]{1,0:T(8,128)(2,1)S(1)} collective-permute-done((bf16[512,512]{1,0:T(8,128)(2,1)S(1)}, bf16[512,512]{1,0:T(8,128)(2,1)S(1)}, u32[]{:S(2)}, u32[]{:S(2)}) %collective-permute-start.3) | collective-permute-done | bytes 524320 | tf_op jit(solution)/shard_map/ppermute | solution.py:40
  13.9 1.6 %collective-permute-start.5 = (bf16[128,512]{1,0:T(8,128)(2,1)S(1)}, bf16[128,512]{1,0:T(8,128)(2,1)S(1)}, u32[]{:S(2)}, u32[]{:S(2)}) collective-permute-start(bf16[128,512]{1,0:T(8,128)(2,1)S(1)} %get-tuple-element.28), channel_id=1, source_target_pairs={{0,2},{1,3},{2,0},{3,1},{4,6},{5,7},{6,4},{7,5},{8,10},{9,11},{10,... | collective-permute-start | bytes 393224 | tf_op jit(solution)/shard_map/ppermute | solution.py:40
  16.0 4.3 %collective-permute-done.5.refs_1_ = bf16[128,512]{1,0:T(8,128)(2,1)S(1)} collective-permute-done((bf16[128,512]{1,0:T(8,128)(2,1)S(1)}, bf16[128,512]{1,0:T(8,128)(2,1)S(1)}, u32[]{:S(2)}, u32[]{:S(2)}) %collective-permute-start.5) | collective-permute-done | bytes 131104 | tf_op jit(solution)/shard_map/ppermute | solution.py:40
  20.3 2.7 %collective-permute-start.6 = (bf16[128,512]{1,0:T(8,128)(2,1)S(1)}, bf16[128,512]{1,0:T(8,128)(2,1)S(1)}, u32[]{:S(2)}, u32[]{:S(2)}) collective-permute-start(bf16[128,512]{1,0:T(8,128)(2,1)S(1)} %shard_map.98), channel_id=1, source_target_pairs={{0,4},{1,5},{2,6},{3,7},{4,0},{5,1},{6,2},{7,3},{8,12},{9,13},{10,... | collective-permute-start | bytes 393224 | tf_op jit(solution)/shard_map/ppermute | solution.py:40
  23.0 5.4 %collective-permute-done.6.refs_4_ = bf16[128,512]{1,0:T(8,128)(2,1)S(1)} collective-permute-done((bf16[128,512]{1,0:T(8,128)(2,1)S(1)}, bf16[128,512]{1,0:T(8,128)(2,1)S(1)}, u32[]{:S(2)}, u32[]{:S(2)}) %collective-permute-start.6) | collective-permute-done | bytes 131104 | tf_op jit(solution)/shard_map/ppermute | solution.py:40
  28.4 1.0 %shard_map.99 = (bf16[128,512]{1,0:T(8,128)(2,1)}, bf16[128,512]{1,0:T(8,128)(2,1)S(1)}, bf16[128,512]{1,0:T(8,128)(2,1)S(1)}, bf16[128,512]{1,0:T(8,128)(2,1)S(1)}) custom-call(bf16[512,512]{1,0:T(8,128)(2,1)S(1)} %copy-done.2, bf16[1,128,512]{2,1,0:T(8,128)(2,1)S(1)} %copy-done.3, f32[128,512]{1,0:T(8,128)S(1)} %get-tuple-element.25.refs_2_, ...), custom_call_target="tpu_custom_call" | custom-call | tf_op jit(solution)/shard_map/pallas_call | solution.py:23
  31.4 1.6 %collective-permute-start.11 = (bf16[64,512]{1,0:T(8,128)(2,1)S(1)}, bf16[64,512]{1,0:T(8,128)(2,1)S(1)}, u32[]{:S(2)}, u32[]{:S(2)}) collective-permute-start(bf16[64,512]{1,0:T(8,128)(2,1)S(1)} %get-tuple-element.37), channel_id=1, source_target_pairs={{0,8},{8,0},{16,24},{24,16},{1,9},{9,1},{17,25},{25,17},{2,10},{10... | collective-permute-start | bytes 196616 | tf_op jit(solution)/shard_map/ppermute | solution.py:40
  33.7 2.3 %collective-permute-start.8 = (bf16[128,512]{1,0:T(8,128)(2,1)S(1)}, bf16[128,512]{1,0:T(8,128)(2,1)S(1)}, u32[]{:S(2)}, u32[]{:S(2)}) collective-permute-start(bf16[128,512]{1,0:T(8,128)(2,1)S(1)} %get-tuple-element.32.refs_1_), channel_id=1, source_target_pairs={{0,2},{1,3},{2,0},{3,1},{4,6},{5,7},{6,4},{7,5},{8,10},{9,11},{10,... | collective-permute-start | bytes 393224 | tf_op jit(solution)/shard_map/ppermute | solution.py:40
  36.0 1.2 %collective-permute-start.15 = (bf16[64,512]{1,0:T(8,128)(2,1)S(1)}, bf16[64,512]{1,0:T(8,128)(2,1)S(1)}, u32[]{:S(2)}, u32[]{:S(2)}) collective-permute-start(bf16[64,512]{1,0:T(8,128)(2,1)S(1)} %get-tuple-element.40), channel_id=1, source_target_pairs={{0,24},{8,16},{16,8},{24,0},{1,25},{9,17},{17,9},{25,1},{2,26},{10... | collective-permute-start | bytes 196616 | tf_op jit(solution)/shard_map/ppermute | solution.py:40
  37.2 2.4 %collective-permute-done.9.refs_0_ = bf16[128,512]{1,0:T(8,128)(2,1)S(1)} collective-permute-done((bf16[128,512]{1,0:T(8,128)(2,1)S(1)}, bf16[128,512]{1,0:T(8,128)(2,1)S(1)}, u32[]{:S(2)}, u32[]{:S(2)}) %collective-permute-start.9) | collective-permute-done | bytes 131104 | tf_op jit(solution)/shard_map/ppermute | solution.py:40
  41.2 1.0 %collective-permute-start.18 = (bf16[64,512]{1,0:T(8,128)(2,1)S(1)}, bf16[64,512]{1,0:T(8,128)(2,1)S(1)}, u32[]{:S(2)}, u32[]{:S(2)}) collective-permute-start(bf16[64,512]{1,0:T(8,128)(2,1)S(1)} %shard_map.105.refs_0_), channel_id=1, source_target_pairs={{0,6},{1,7},{2,4},{3,5},{4,2},{5,3},{6,0},{7,1},{8,14},{9,15},{10,... | collective-permute-start | bytes 196616 | tf_op jit(solution)/shard_map/ppermute | solution.py:40
  42.1 1.1 %collective-permute-start.17 = (bf16[64,512]{1,0:T(8,128)(2,1)S(1)}, bf16[64,512]{1,0:T(8,128)(2,1)S(1)}, u32[]{:S(2)}, u32[]{:S(2)}) collective-permute-start(bf16[64,512]{1,0:T(8,128)(2,1)S(1)} %shard_map.105.refs_0_), channel_id=1, source_target_pairs={{0,4},{1,5},{2,6},{3,7},{4,0},{5,1},{6,2},{7,3},{8,12},{9,13},{10,... | collective-permute-start | bytes 196616 | tf_op jit(solution)/shard_map/ppermute | solution.py:40
  43.3 2.4 %collective-permute-start.16 = (bf16[64,512]{1,0:T(8,128)(2,1)S(1)}, bf16[64,512]{1,0:T(8,128)(2,1)S(1)}, u32[]{:S(2)}, u32[]{:S(2)}) collective-permute-start(bf16[64,512]{1,0:T(8,128)(2,1)S(1)} %shard_map.105.refs_0_), channel_id=1, source_target_pairs={{0,2},{1,3},{2,0},{3,1},{4,6},{5,7},{6,4},{7,5},{8,10},{9,11},{10,... | collective-permute-start | bytes 196616 | tf_op jit(solution)/shard_map/ppermute | solution.py:40
  46.5 1.1 %collective-permute-done.18.refs_3_ = bf16[64,512]{1,0:T(8,128)(2,1)S(1)} collective-permute-done((bf16[64,512]{1,0:T(8,128)(2,1)S(1)}, bf16[64,512]{1,0:T(8,128)(2,1)S(1)}, u32[]{:S(2)}, u32[]{:S(2)}) %collective-permute-start.18) | collective-permute-done | bytes 65568 | tf_op jit(solution)/shard_map/ppermute | solution.py:40
  47.6 1.6 %collective-permute-done.17.refs_2_ = bf16[64,512]{1,0:T(8,128)(2,1)S(1)} collective-permute-done((bf16[64,512]{1,0:T(8,128)(2,1)S(1)}, bf16[64,512]{1,0:T(8,128)(2,1)S(1)}, u32[]{:S(2)}, u32[]{:S(2)}) %collective-permute-start.17) | collective-permute-done | bytes 65568 | tf_op jit(solution)/shard_map/ppermute | solution.py:40
  49.8 1.6 %collective-permute-start.19 = (bf16[192,512]{1,0:T(8,128)(2,1)S(1)}, bf16[192,512]{1,0:T(8,128)(2,1)S(1)}, u32[]{:S(2)}, u32[]{:S(2)}) collective-permute-start(bf16[192,512]{1,0:T(8,128)(2,1)S(1)} %get-tuple-element.42), channel_id=1, source_target_pairs={{0,8},{8,0},{16,24},{24,16},{1,9},{9,1},{17,25},{25,17},{2,10},{10... | collective-permute-start | bytes 589832 | tf_op jit(solution)/shard_map/ppermute | solution.py:40
  52.1 1.2 %collective-permute-start.21 = (bf16[192,512]{1,0:T(8,128)(2,1)S(1)}, bf16[192,512]{1,0:T(8,128)(2,1)S(1)}, u32[]{:S(2)}, u32[]{:S(2)}) collective-permute-start(bf16[192,512]{1,0:T(8,128)(2,1)S(1)} %get-tuple-element.44), channel_id=1, source_target_pairs={{0,24},{8,16},{16,8},{24,0},{1,25},{9,17},{17,9},{25,1},{2,26},{10... | collective-permute-start | bytes 589832 | tf_op jit(solution)/shard_map/ppermute | solution.py:40
  53.3 4.1 %collective-permute-done.19.refs_1_ = bf16[192,512]{1,0:T(8,128)(2,1)S(1)} collective-permute-done((bf16[192,512]{1,0:T(8,128)(2,1)S(1)}, bf16[192,512]{1,0:T(8,128)(2,1)S(1)}, u32[]{:S(2)}, u32[]{:S(2)}) %collective-permute-start.19) | collective-permute-done | bytes 196640 | tf_op jit(solution)/shard_map/ppermute | solution.py:40
  57.4 3.7 %collective-permute-done.20.refs_2_ = bf16[192,512]{1,0:T(8,128)(2,1)S(1)} collective-permute-done((bf16[192,512]{1,0:T(8,128)(2,1)S(1)}, bf16[192,512]{1,0:T(8,128)(2,1)S(1)}, u32[]{:S(2)}, u32[]{:S(2)}) %collective-permute-start.20) | collective-permute-done | bytes 196640 | tf_op jit(solution)/shard_map/ppermute | solution.py:40
  62.7 1.0 %shard_map.110 = f32[512,512]{1,0:T(8,128)} custom-call(bf16[256,512]{1,0:T(8,128)(2,1)S(1)} %shard_map.108.refs_4_.refs_0_, bf16[256,512]{1,0:T(8,128)(2,1)S(1)} %collective-permute-done.22.refs_1_), custom_call_target="tpu_custom_call" | custom-call | tf_op jit(solution)/shard_map/pallas_call | solution.py:23
  (51 shorter events, 11.0 us)
Async XLA Ops:
  0.7 9.1 %collective-permute-start.2 = (bf16[128,512]{1,0:T(8,128)(2,1)}, bf16[128,512]{1,0:T(8,128)(2,1)S(1)}, u32[]{:S(2)}, u32[]{:S(2)}) collective-permute-start(bf16[128,512]{1,0:T(8,128)(2,1)} %bitcast.3), channel_id=1, source_target_pairs={{0,24},{8,16},{16,8},{24,0},{1,25},{9,17},{17,9},{25,1},{2,26},{10... | collective-permute-start | bytes 393224 | tf_op jit(solution)/shard_map/ppermute | solution.py:40
  4.6 6.5 %collective-permute-start.1 = (bf16[128,512]{1,0:T(8,128)(2,1)}, bf16[128,512]{1,0:T(8,128)(2,1)S(1)}, u32[]{:S(2)}, u32[]{:S(2)}) collective-permute-start(bf16[128,512]{1,0:T(8,128)(2,1)} %bitcast.4), channel_id=1, source_target_pairs={{0,16},{8,24},{16,0},{24,8},{1,17},{9,25},{17,1},{25,9},{2,18},{10... | collective-permute-start | bytes 393224 | tf_op jit(solution)/shard_map/ppermute | solution.py:40
  5.1 6.3 %collective-permute-start = (bf16[128,512]{1,0:T(8,128)(2,1)}, bf16[128,512]{1,0:T(8,128)(2,1)S(1)}, u32[]{:S(2)}, u32[]{:S(2)}) collective-permute-start(bf16[128,512]{1,0:T(8,128)(2,1)} %bitcast.5), channel_id=1, source_target_pairs={{0,8},{8,0},{16,24},{24,16},{1,9},{9,1},{17,25},{25,17},{2,10},{10... | collective-permute-start | bytes 393224 | tf_op jit(solution)/shard_map/ppermute | solution.py:40
  11.8 2.0 %collective-permute-start.3 = (bf16[512,512]{1,0:T(8,128)(2,1)S(1)}, bf16[512,512]{1,0:T(8,128)(2,1)S(1)}, u32[]{:S(2)}, u32[]{:S(2)}) collective-permute-start(bf16[512,512]{1,0:T(8,128)(2,1)S(1)} %shard_map.96), channel_id=1, source_target_pairs={{0,1},{1,0},{2,3},{3,2},{4,5},{5,4},{6,7},{7,6},{8,9},{9,8},{10,11... | collective-permute-start | bytes 1572872 | tf_op jit(solution)/shard_map/ppermute | solution.py:40
  11.9 11.1 %collective-permute-start.7 = (bf16[512,512]{1,0:T(8,128)(2,1)S(1)}, bf16[512,512]{1,0:T(8,128)(2,1)S(1)}, u32[]{:S(2)}, u32[]{:S(2)}) collective-permute-start(bf16[512,512]{1,0:T(8,128)(2,1)S(1)} %get-tuple-element.29), channel_id=1, source_target_pairs={{0,1},{1,0},{2,3},{3,2},{4,5},{5,4},{6,7},{7,6},{8,9},{9,8},{10,11... | collective-permute-start | bytes 1572872 | tf_op jit(solution)/shard_map/ppermute | solution.py:40
  13.8 14.6 %copy-start.2 = (bf16[512,512]{1,0:T(8,128)(2,1)S(1)}, bf16[512,512]{1,0:T(8,128)(2,1)}, u32[]{:S(2)}) copy-start(bf16[512,512]{1,0:T(8,128)(2,1)} %refs_0_.3) | copy-start | bytes 1572868
  13.9 6.4 %collective-permute-start.5 = (bf16[128,512]{1,0:T(8,128)(2,1)S(1)}, bf16[128,512]{1,0:T(8,128)(2,1)S(1)}, u32[]{:S(2)}, u32[]{:S(2)}) collective-permute-start(bf16[128,512]{1,0:T(8,128)(2,1)S(1)} %get-tuple-element.28), channel_id=1, source_target_pairs={{0,2},{1,3},{2,0},{3,1},{4,6},{5,7},{6,4},{7,5},{8,10},{9,11},{10,... | collective-permute-start | bytes 393224 | tf_op jit(solution)/shard_map/ppermute | solution.py:40
  15.5 7.5 %collective-permute-start.4 = (bf16[128,512]{1,0:T(8,128)(2,1)S(1)}, bf16[128,512]{1,0:T(8,128)(2,1)S(1)}, u32[]{:S(2)}, u32[]{:S(2)}) collective-permute-start(bf16[128,512]{1,0:T(8,128)(2,1)S(1)} %get-tuple-element.26), channel_id=1, source_target_pairs={{0,2},{1,3},{2,0},{3,1},{4,6},{5,7},{6,4},{7,5},{8,10},{9,11},{10,... | collective-permute-start | bytes 393224 | tf_op jit(solution)/shard_map/ppermute | solution.py:40
  20.3 8.1 %collective-permute-start.6 = (bf16[128,512]{1,0:T(8,128)(2,1)S(1)}, bf16[128,512]{1,0:T(8,128)(2,1)S(1)}, u32[]{:S(2)}, u32[]{:S(2)}) collective-permute-start(bf16[128,512]{1,0:T(8,128)(2,1)S(1)} %shard_map.98), channel_id=1, source_target_pairs={{0,4},{1,5},{2,6},{3,7},{4,0},{5,1},{6,2},{7,3},{8,12},{9,13},{10,... | collective-permute-start | bytes 393224 | tf_op jit(solution)/shard_map/ppermute | solution.py:40
  29.8 1.6 %collective-permute-start.10 = (bf16[256,512]{1,0:T(8,128)(2,1)S(1)}, bf16[256,512]{1,0:T(8,128)(2,1)S(1)}, u32[]{:S(2)}, u32[]{:S(2)}) collective-permute-start(bf16[256,512]{1,0:T(8,128)(2,1)S(1)} %get-tuple-element.36), channel_id=1, source_target_pairs={{0,1},{1,0},{2,3},{3,2},{4,5},{5,4},{6,7},{7,6},{8,9},{9,8},{10,11... | collective-permute-start | bytes 786440 | tf_op jit(solution)/shard_map/ppermute | solution.py:40
  29.9 9.7 %collective-permute-start.9 = (bf16[128,512]{1,0:T(8,128)(2,1)S(1)}, bf16[128,512]{1,0:T(8,128)(2,1)S(1)}, u32[]{:S(2)}, u32[]{:S(2)}) collective-permute-start(bf16[128,512]{1,0:T(8,128)(2,1)S(1)} %get-tuple-element.32.refs_1_), channel_id=1, source_target_pairs={{0,4},{1,5},{2,6},{3,7},{4,0},{5,1},{6,2},{7,3},{8,12},{9,13},{10,... | collective-permute-start | bytes 393224 | tf_op jit(solution)/shard_map/ppermute | solution.py:40
  31.4 8.2 %collective-permute-start.11 = (bf16[64,512]{1,0:T(8,128)(2,1)S(1)}, bf16[64,512]{1,0:T(8,128)(2,1)S(1)}, u32[]{:S(2)}, u32[]{:S(2)}) collective-permute-start(bf16[64,512]{1,0:T(8,128)(2,1)S(1)} %get-tuple-element.37), channel_id=1, source_target_pairs={{0,8},{8,0},{16,24},{24,16},{1,9},{9,1},{17,25},{25,17},{2,10},{10... | collective-permute-start | bytes 196616 | tf_op jit(solution)/shard_map/ppermute | solution.py:40
  33.0 6.6 %collective-permute-start.12 = (bf16[64,512]{1,0:T(8,128)(2,1)S(1)}, bf16[64,512]{1,0:T(8,128)(2,1)S(1)}, u32[]{:S(2)}, u32[]{:S(2)}) collective-permute-start(bf16[64,512]{1,0:T(8,128)(2,1)S(1)} %get-tuple-element.38), channel_id=1, source_target_pairs={{0,16},{8,24},{16,0},{24,8},{1,17},{9,25},{17,1},{25,9},{2,18},{10... | collective-permute-start | bytes 196616 | tf_op jit(solution)/shard_map/ppermute | solution.py:40
  33.7 11.9 %collective-permute-start.8 = (bf16[128,512]{1,0:T(8,128)(2,1)S(1)}, bf16[128,512]{1,0:T(8,128)(2,1)S(1)}, u32[]{:S(2)}, u32[]{:S(2)}) collective-permute-start(bf16[128,512]{1,0:T(8,128)(2,1)S(1)} %get-tuple-element.32.refs_1_), channel_id=1, source_target_pairs={{0,2},{1,3},{2,0},{3,1},{4,6},{5,7},{6,4},{7,5},{8,10},{9,11},{10,... | collective-permute-start | bytes 393224 | tf_op jit(solution)/shard_map/ppermute | solution.py:40
  36.0 5.2 %collective-permute-start.15 = (bf16[64,512]{1,0:T(8,128)(2,1)S(1)}, bf16[64,512]{1,0:T(8,128)(2,1)S(1)}, u32[]{:S(2)}, u32[]{:S(2)}) collective-permute-start(bf16[64,512]{1,0:T(8,128)(2,1)S(1)} %get-tuple-element.40), channel_id=1, source_target_pairs={{0,24},{8,16},{16,8},{24,0},{1,25},{9,17},{17,9},{25,1},{2,26},{10... | collective-permute-start | bytes 196616 | tf_op jit(solution)/shard_map/ppermute | solution.py:40
  39.6 6.4 %collective-permute-start.13 = (bf16[128,512]{1,0:T(8,128)(2,1)S(1)}, bf16[128,512]{1,0:T(8,128)(2,1)S(1)}, u32[]{:S(2)}, u32[]{:S(2)}) collective-permute-start(bf16[128,512]{1,0:T(8,128)(2,1)S(1)} %shard_map.102.refs_3_), channel_id=1, source_target_pairs={{0,2},{1,3},{2,0},{3,1},{4,6},{5,7},{6,4},{7,5},{8,10},{9,11},{10,... | collective-permute-start | bytes 393224 | tf_op jit(solution)/shard_map/ppermute | solution.py:40
  41.2 6.4 %collective-permute-start.18 = (bf16[64,512]{1,0:T(8,128)(2,1)S(1)}, bf16[64,512]{1,0:T(8,128)(2,1)S(1)}, u32[]{:S(2)}, u32[]{:S(2)}) collective-permute-start(bf16[64,512]{1,0:T(8,128)(2,1)S(1)} %shard_map.105.refs_0_), channel_id=1, source_target_pairs={{0,6},{1,7},{2,4},{3,5},{4,2},{5,3},{6,0},{7,1},{8,14},{9,15},{10,... | collective-permute-start | bytes 196616 | tf_op jit(solution)/shard_map/ppermute | solution.py:40
  42.1 7.1 %collective-permute-start.17 = (bf16[64,512]{1,0:T(8,128)(2,1)S(1)}, bf16[64,512]{1,0:T(8,128)(2,1)S(1)}, u32[]{:S(2)}, u32[]{:S(2)}) collective-permute-start(bf16[64,512]{1,0:T(8,128)(2,1)S(1)} %shard_map.105.refs_0_), channel_id=1, source_target_pairs={{0,4},{1,5},{2,6},{3,7},{4,0},{5,1},{6,2},{7,3},{8,12},{9,13},{10,... | collective-permute-start | bytes 196616 | tf_op jit(solution)/shard_map/ppermute | solution.py:40
  43.3 5.9 %collective-permute-start.16 = (bf16[64,512]{1,0:T(8,128)(2,1)S(1)}, bf16[64,512]{1,0:T(8,128)(2,1)S(1)}, u32[]{:S(2)}, u32[]{:S(2)}) collective-permute-start(bf16[64,512]{1,0:T(8,128)(2,1)S(1)} %shard_map.105.refs_0_), channel_id=1, source_target_pairs={{0,2},{1,3},{2,0},{3,1},{4,6},{5,7},{6,4},{7,5},{8,10},{9,11},{10,... | collective-permute-start | bytes 196616 | tf_op jit(solution)/shard_map/ppermute | solution.py:40
  46.4 3.3 %collective-permute-start.14 = (bf16[512,512]{1,0:T(8,128)(2,1)S(1)}, bf16[512,512]{1,0:T(8,128)(2,1)S(1)}, u32[]{:S(2)}, u32[]{:S(2)}) collective-permute-start(bf16[512,512]{1,0:T(8,128)(2,1)S(1)} %shard_map.104), channel_id=1, source_target_pairs={{0,1},{1,0},{2,3},{3,2},{4,5},{5,4},{6,7},{7,6},{8,9},{9,8},{10,11... | collective-permute-start | bytes 1572872 | tf_op jit(solution)/shard_map/ppermute | solution.py:40
  49.8 7.6 %collective-permute-start.19 = (bf16[192,512]{1,0:T(8,128)(2,1)S(1)}, bf16[192,512]{1,0:T(8,128)(2,1)S(1)}, u32[]{:S(2)}, u32[]{:S(2)}) collective-permute-start(bf16[192,512]{1,0:T(8,128)(2,1)S(1)} %get-tuple-element.42), channel_id=1, source_target_pairs={{0,8},{8,0},{16,24},{24,16},{1,9},{9,1},{17,25},{25,17},{2,10},{10... | collective-permute-start | bytes 589832 | tf_op jit(solution)/shard_map/ppermute | solution.py:40
  51.4 9.7 %collective-permute-start.20 = (bf16[192,512]{1,0:T(8,128)(2,1)S(1)}, bf16[192,512]{1,0:T(8,128)(2,1)S(1)}, u32[]{:S(2)}, u32[]{:S(2)}) collective-permute-start(bf16[192,512]{1,0:T(8,128)(2,1)S(1)} %get-tuple-element.43), channel_id=1, source_target_pairs={{0,16},{8,24},{16,0},{24,8},{1,17},{9,25},{17,1},{25,9},{2,18},{10... | collective-permute-start | bytes 589832 | tf_op jit(solution)/shard_map/ppermute | solution.py:40
  52.1 9.0 %collective-permute-start.21 = (bf16[192,512]{1,0:T(8,128)(2,1)S(1)}, bf16[192,512]{1,0:T(8,128)(2,1)S(1)}, u32[]{:S(2)}, u32[]{:S(2)}) collective-permute-start(bf16[192,512]{1,0:T(8,128)(2,1)S(1)} %get-tuple-element.44), channel_id=1, source_target_pairs={{0,24},{8,16},{16,8},{24,0},{1,25},{9,17},{17,9},{25,1},{2,26},{10... | collective-permute-start | bytes 589832 | tf_op jit(solution)/shard_map/ppermute | solution.py:40
  61.1 1.6 %collective-permute-start.22 = (bf16[256,512]{1,0:T(8,128)(2,1)S(1)}, bf16[256,512]{1,0:T(8,128)(2,1)S(1)}, u32[]{:S(2)}, u32[]{:S(2)}) collective-permute-start(bf16[256,512]{1,0:T(8,128)(2,1)S(1)} %shard_map.108.refs_4_.refs_0_), channel_id=1, source_target_pairs={{0,1},{1,0},{2,3},{3,2},{4,5},{5,4},{6,7},{7,6},{8,9},{9,8},{10,11... | collective-permute-start | bytes 786440 | tf_op jit(solution)/shard_map/ppermute | solution.py:40
  (5 other events, 24.1 us)

commit v3 on v2

--- a/solution.py
+++ b/solution.py
@@ -55,7 +55,9 @@
     def place(s, carry):
         far = rows[0, 0, s] ^ me_col
         inside = pl.multiple_of((far >> 1) * TILE, TILE)
-        at = pl.multiple_of((far & 1) * n_z * TILE + inside, TILE)
+        chip = far >> 1
+        part = (far & 1) * n_z + (1 - (chip & 1)) * (n_z // 2) + (chip >> 1)
+        at = pl.multiple_of(part * TILE, TILE)
         to = pl.multiple_of((cols[0, 0, s] ^ me_row) * TILE, TILE)
         tile = values[0, 0, s]
         dense[pl.ds(at, TILE), pl.ds(to, TILE)] = tile
@@ -99,17 +101,22 @@
 
 
 def dense_layer(weight, cotangent, *refs):
-    *terms, layer_out, summed, hidden_grad, grad_rows = refs
+    *terms, hidden_out, summed, hidden_grad, grad_rows = refs
     total = tree([t[...].astype(F32) for t in terms]).astype(BF16)
     summed[...] = total
     hidden = jnp.dot(total, weight[...], preferred_element_type=F32)
+    hidden_out[...] = hidden
     gate = jax.nn.sigmoid(hidden)
-    layer_out[...] = (hidden * gate).astype(BF16)
     grad = (cotangent[0].astype(F32) * gate * (1.0 + hidden * (1.0 - gate))).astype(BF16)
     hidden_grad[...] = grad
     grad_rows[...] = lax.dot_general(
         grad, weight[...], (((1,), (1,)), ((), ())), preferred_element_type=F32
     ).astype(BF16)
+
+
+def activation(hidden, out, done):
+    done[...] = jnp.zeros_like(done)
+    out[...] = (hidden[...] * jax.nn.sigmoid(hidden[...])).astype(BF16)
 
 
 def weight_term(n_row, scale, summed, hidden_grad, mine, other, whole):
@@ -189,18 +196,20 @@
         specs=[VMEM, SMEM, SMEM, SMEM],
     )
     other_t = core_swap(other_t)
-    (other,) = call(functools.partial(forward, half), [like(half, width)], (dense, *panel))
-    other = core_swap(other)
-    (mine,) = call(
-        functools.partial(forward, 0), [like(half, width, dtype=F32)], (dense, *panel)
-    )
-    parts = list(
-        call(
-            add_split,
-            [like(TILE, width, dtype=F32)] + [like(TILE, width)] * (n_z - 1),
-            (mine, other),
+    quarter, parts = half // 2, [None] * n_z
+    for odd in (1, 0):
+        first = (1 - odd) * quarter
+        (other,) = call(
+            functools.partial(forward, half + first),
+            [like(quarter, width)],
+            (dense, *panel),
         )
-    )
+        other = core_swap(other)
+        (mine,) = call(
+            functools.partial(forward, first), [like(quarter, width, dtype=F32)], (dense, *panel)
+        )
+        outs = [like(TILE, width, dtype=BF16 if k else F32) for k in range(odd, n_z, 2)]
+        parts[odd::2] = call(add_split, outs, (mine, other))
     bit, extra = 1, []
     while bit < n_z:
         far = [k for k in range(n_z) if k & bit and k % bit == 0]
@@ -212,11 +221,10 @@
                 (parts[k ^ bit],) = call(add_all, [like(TILE, width)], (parts[k ^ bit], got))
         bit *= 2
     terms = [parts[0]] + extra
-    layer_out, summed, hidden_grad, grad_rows = call(
+    hidden, summed, hidden_grad, grad_rows = call(
         dense_layer,
-        [like(TILE, width)] * 4,
+        [like(TILE, width, dtype=F32)] + [like(TILE, width)] * 3,
         (weight, cotangent, *terms),
-        after=(other_t,),
     )
     piece = width // 2 // n_row
     mine_w, other_w = call(
@@ -226,7 +234,7 @@
         scratch=[pltpu.VMEM((width, width), F32)],
     )
     other_w = core_swap(other_w)
-    parts_w = call(add_split, [like(piece, width)] * n_row, (mine_w, other_w))
+    parts_w = call(add_split, [like(piece, width)] * n_row, (mine_w, other_w), after=(other_t,))
     terms_w = [parts_w[0]] + [row_swap(parts_w[k], k) for k in range(1, n_row)]
     same = [grad_rows] + [None] * (n_z - 1)
     bit = n_z // 2
@@ -254,7 +262,10 @@
         (mine, other, final_w),
     )
     terms = [row_swap(part, k + 1) for k, part in enumerate(parts)]
-    (half_w,) = call(join, [like(width // 2, width)], (final_w, *terms))
+    layer_out, done = call(
+        activation, [like(TILE, width), like(8, TILE, dtype=F32)], (hidden,), us=1
+    )
+    (half_w,) = call(join, [like(width // 2, width)], (final_w, *terms), after=(done,))
     other_w = core_swap(half_w)
     (feat_grad,) = call(add_rows, [like(TILE, width)], (back, *terms), after=(half_w,))
     (weight_grad,) = call(spread, [like(width, width, dtype=F32)], (half_w, other_w))

time: 63.9 us -> 63 us (0.986)
  Pallas kernels: 7.86 us -> 6.65 us
  waiting for transfers between devices: 28.2 us -> 29 us
    pallas_call x17 -> x21, Pallas kernels: 7.86 us -> 6.65 us  [call(): pl.pallas_call(body, out_shape=outs, in_specs=(specs or [VMEM] * len(args...]
    ppermute x23 -> x24, waiting for transfers between devices: 28.2 us -> 29 us  [swap(): return lax.ppermute(value, axis, [(i, i ^ mask) for i in range(size)])]
    ppermute x23 -> x24, starting transfers between devices: 25.1 us -> 24.5 us  [swap(): return lax.ppermute(value, axis, [(i, i ^ mask) for i in range(size)])]
  transfers between devices with their start and end apart: 23 -> 24, of which waited for: 14 -> 13; matrix products, arithmetic and copies ran while one was open for 0% -> 0% of each run, Pallas kernels for 8% -> 8%
where the time goes in v3:
time: 63 us; the launch traced here: 62.8 us
  waiting for transfers between devices  29 us (46%)
  starting transfers between devices  24.5 us (39%)
  Pallas kernels  6.65 us (11%)
  between operations  1.5 us (2%)
  local copies, waits for them, and re-layouts  1.15 us (2%)
    ppermute x24, waiting for transfers between devices, swap(): return lax.ppermute(value, axis, [(i, i ^ mask) for i in range(size)])  29 us
    ppermute x24, starting transfers between devices, swap(): return lax.ppermute(value, axis, [(i, i ^ mask) for i in range(size)])  24.5 us
    pallas_call x21, Pallas kernels, call(): pl.pallas_call(body, out_shape=outs, in_specs=(specs or [VMEM] * len(args...  6.65 us
  transfers between devices with their start and end apart: 24, of which 13 were waited for; matrix products, arithmetic and copies ran while one was open for 0% of the time, Pallas kernels for 8%

profile of v3, /device:TPU:0, one launch (start us, length us, event | category | flops | bytes accessed | tf_op | source)
XLA Modules:
  0.0 62.8 jit_solution(1514410542045431883)
XLA Ops:
  0.7 3.0 %collective-permute-start = (bf16[128,512]{1,0:T(8,128)(2,1)}, bf16[128,512]{1,0:T(8,128)(2,1)S(1)}, u32[]{:S(2)}, u32[]{:S(2)}) collective-permute-start(bf16[128,512]{1,0:T(8,128)(2,1)} %bitcast.3), channel_id=1, source_target_pairs={{0,8},{8,0},{16,24},{24,16},{1,9},{9,1},{17,25},{25,17},{2,10},{10... | collective-permute-start | bytes 393224 | tf_op jit(solution)/shard_map/ppermute | solution.py:40
  3.7 1.5 %collective-permute-start.1 = (bf16[128,512]{1,0:T(8,128)(2,1)}, bf16[128,512]{1,0:T(8,128)(2,1)S(1)}, u32[]{:S(2)}, u32[]{:S(2)}) collective-permute-start(bf16[128,512]{1,0:T(8,128)(2,1)} %bitcast.4), channel_id=1, source_target_pairs={{0,16},{8,24},{16,0},{24,8},{1,17},{9,25},{17,1},{25,9},{2,18},{10... | collective-permute-start | bytes 393224 | tf_op jit(solution)/shard_map/ppermute | solution.py:40
  5.9 1.1 %copy-done.1 = bf16[1,1,24,128,128]{4,3,2,1,0:T(8,128)(2,1)S(1)} copy-done((bf16[1,1,24,128,128]{4,3,2,1,0:T(8,128)(2,1)S(1)}, bf16[1,1,24,128,128]{4,3,2,1,0:T(8,128)(2,1)}, u32[]{:S(2)}) %copy-start.1) | copy-done | bytes 786456
  7.0 0.9 %shard_map.94 = (bf16[1024,512]{1,0:T(8,128)(2,1)S(1)}, bf16[512,512]{1,0:T(8,128)(2,1)S(1)}, bf16[512,512]{1,0:T(8,128)(2,1)S(1)}) custom-call(bf16[1,1,24,128,128]{4,3,2,1,0:T(8,128)(2,1)S(1)} %copy-done.1, s32[1,1,24]{2,1,0:T(1,128)S(1)} %copy-done.4, s32[1,1,24]{2,1,0:T(1,128)S(1)} %copy-done.5, s32[1,1]{1,0:T(1,128)S(6)} %copy.12.refs_3_), custom_call_target="tpu_custom_call" | custom-call | tf_op jit(solution)/shard_map/pallas_call | solution.py:23
  7.9 3.7 %collective-permute-done.1.refs_3_ = bf16[128,512]{1,0:T(8,128)(2,1)S(1)} collective-permute-done((bf16[128,512]{1,0:T(8,128)(2,1)}, bf16[128,512]{1,0:T(8,128)(2,1)S(1)}, u32[]{:S(2)}, u32[]{:S(2)}) %collective-permute-start.1) | collective-permute-done | bytes 131104 | tf_op jit(solution)/shard_map/ppermute | solution.py:40
  13.6 1.6 %collective-permute-start.6 = (bf16[128,512]{1,0:T(8,128)(2,1)S(1)}, bf16[128,512]{1,0:T(8,128)(2,1)S(1)}, u32[]{:S(2)}, u32[]{:S(2)}) collective-permute-start(bf16[128,512]{1,0:T(8,128)(2,1)S(1)} %get-tuple-element.30), channel_id=1, source_target_pairs={{0,2},{1,3},{2,0},{3,1},{4,6},{5,7},{6,4},{7,5},{8,10},{9,11},{10,... | collective-permute-start | bytes 393224 | tf_op jit(solution)/shard_map/ppermute | solution.py:40
  16.1 3.5 %collective-permute-done.6.refs_1_ = bf16[128,512]{1,0:T(8,128)(2,1)S(1)} collective-permute-done((bf16[128,512]{1,0:T(8,128)(2,1)S(1)}, bf16[128,512]{1,0:T(8,128)(2,1)S(1)}, u32[]{:S(2)}, u32[]{:S(2)}) %collective-permute-start.6) | collective-permute-done | bytes 131104 | tf_op jit(solution)/shard_map/ppermute | solution.py:40
  19.7 2.7 %collective-permute-start.7 = (bf16[128,512]{1,0:T(8,128)(2,1)S(1)}, bf16[128,512]{1,0:T(8,128)(2,1)S(1)}, u32[]{:S(2)}, u32[]{:S(2)}) collective-permute-start(bf16[128,512]{1,0:T(8,128)(2,1)S(1)} %shard_map.101), channel_id=1, source_target_pairs={{0,4},{1,5},{2,6},{3,7},{4,0},{5,1},{6,2},{7,3},{8,12},{9,13},{10,... | collective-permute-start | bytes 393224 | tf_op jit(solution)/shard_map/ppermute | solution.py:40
  22.3 5.8 %collective-permute-done.7.refs_4_ = bf16[128,512]{1,0:T(8,128)(2,1)S(1)} collective-permute-done((bf16[128,512]{1,0:T(8,128)(2,1)S(1)}, bf16[128,512]{1,0:T(8,128)(2,1)S(1)}, u32[]{:S(2)}, u32[]{:S(2)}) %collective-permute-start.7) | collective-permute-done | bytes 131104 | tf_op jit(solution)/shard_map/ppermute | solution.py:40
  29.3 1.3 %collective-permute-done.10.refs_1_ = bf16[256,512]{1,0:T(8,128)(2,1)S(1)} collective-permute-done((bf16[256,512]{1,0:T(8,128)(2,1)S(1)}, bf16[256,512]{1,0:T(8,128)(2,1)S(1)}, u32[]{:S(2)}, u32[]{:S(2)}) %collective-permute-start.10) | collective-permute-done | bytes 262176 | tf_op jit(solution)/shard_map/ppermute | solution.py:40
  30.6 1.3 %collective-permute-start.12 = (bf16[64,512]{1,0:T(8,128)(2,1)S(1)}, bf16[64,512]{1,0:T(8,128)(2,1)S(1)}, u32[]{:S(2)}, u32[]{:S(2)}) collective-permute-start(bf16[64,512]{1,0:T(8,128)(2,1)S(1)} %get-tuple-element.40), channel_id=1, source_target_pairs={{0,8},{8,0},{16,24},{24,16},{1,9},{9,1},{17,25},{25,17},{2,10},{10... | collective-permute-start | bytes 196616 | tf_op jit(solution)/shard_map/ppermute | solution.py:40
  32.8 2.2 %collective-permute-start.8 = (bf16[128,512]{1,0:T(8,128)(2,1)S(1)}, bf16[128,512]{1,0:T(8,128)(2,1)S(1)}, u32[]{:S(2)}, u32[]{:S(2)}) collective-permute-start(bf16[128,512]{1,0:T(8,128)(2,1)S(1)} %get-tuple-element.34.refs_1_), channel_id=1, source_target_pairs={{0,2},{1,3},{2,0},{3,1},{4,6},{5,7},{6,4},{7,5},{8,10},{9,11},{10,... | collective-permute-start | bytes 393224 | tf_op jit(solution)/shard_map/ppermute | solution.py:40
  35.0 1.4 %collective-permute-start.16 = (bf16[64,512]{1,0:T(8,128)(2,1)S(1)}, bf16[64,512]{1,0:T(8,128)(2,1)S(1)}, u32[]{:S(2)}, u32[]{:S(2)}) collective-permute-start(bf16[64,512]{1,0:T(8,128)(2,1)S(1)} %get-tuple-element.43), channel_id=1, source_target_pairs={{0,24},{8,16},{16,8},{24,0},{1,25},{9,17},{17,9},{25,1},{2,26},{10... | collective-permute-start | bytes 196616 | tf_op jit(solution)/shard_map/ppermute | solution.py:40
  36.4 2.4 %collective-permute-done.9.refs_0_ = bf16[128,512]{1,0:T(8,128)(2,1)S(1)} collective-permute-done((bf16[128,512]{1,0:T(8,128)(2,1)S(1)}, bf16[128,512]{1,0:T(8,128)(2,1)S(1)}, u32[]{:S(2)}, u32[]{:S(2)}) %collective-permute-start.9) | collective-permute-done | bytes 131104 | tf_op jit(solution)/shard_map/ppermute | solution.py:40
  39.1 1.0 %collective-permute-done.16.refs_3_ = bf16[64,512]{1,0:T(8,128)(2,1)S(1)} collective-permute-done((bf16[64,512]{1,0:T(8,128)(2,1)S(1)}, bf16[64,512]{1,0:T(8,128)(2,1)S(1)}, u32[]{:S(2)}, u32[]{:S(2)}) %collective-permute-start.16) | collective-permute-done | bytes 65568 | tf_op jit(solution)/shard_map/ppermute | solution.py:40
  41.8 2.9 %collective-permute-start.19 = (bf16[64,512]{1,0:T(8,128)(2,1)S(1)}, bf16[64,512]{1,0:T(8,128)(2,1)S(1)}, u32[]{:S(2)}, u32[]{:S(2)}) collective-permute-start(bf16[64,512]{1,0:T(8,128)(2,1)S(1)} %shard_map.109.refs_0_), channel_id=1, source_target_pairs={{0,6},{1,7},{2,4},{3,5},{4,2},{5,3},{6,0},{7,1},{8,14},{9,15},{10,... | collective-permute-start | bytes 196616 | tf_op jit(solution)/shard_map/ppermute | solution.py:40
  45.8 1.0 %collective-permute-done.17.refs_1_ = bf16[64,512]{1,0:T(8,128)(2,1)S(1)} collective-permute-done((bf16[64,512]{1,0:T(8,128)(2,1)S(1)}, bf16[64,512]{1,0:T(8,128)(2,1)S(1)}, u32[]{:S(2)}, u32[]{:S(2)}) %collective-permute-start.17) | collective-permute-done | bytes 65568 | tf_op jit(solution)/shard_map/ppermute | solution.py:40
  46.8 1.6 %collective-permute-done.18.refs_2_ = bf16[64,512]{1,0:T(8,128)(2,1)S(1)} collective-permute-done((bf16[64,512]{1,0:T(8,128)(2,1)S(1)}, bf16[64,512]{1,0:T(8,128)(2,1)S(1)}, u32[]{:S(2)}, u32[]{:S(2)}) %collective-permute-start.18) | collective-permute-done | bytes 65568 | tf_op jit(solution)/shard_map/ppermute | solution.py:40
  49.1 1.3 %collective-permute-start.20 = (bf16[192,512]{1,0:T(8,128)(2,1)S(1)}, bf16[192,512]{1,0:T(8,128)(2,1)S(1)}, u32[]{:S(2)}, u32[]{:S(2)}) collective-permute-start(bf16[192,512]{1,0:T(8,128)(2,1)S(1)} %get-tuple-element.45), channel_id=1, source_target_pairs={{0,8},{8,0},{16,24},{24,16},{1,9},{9,1},{17,25},{25,17},{2,10},{10... | collective-permute-start | bytes 589832 | tf_op jit(solution)/shard_map/ppermute | solution.py:40
  50.3 0.8 %collective-permute-start.21 = (bf16[192,512]{1,0:T(8,128)(2,1)S(1)}, bf16[192,512]{1,0:T(8,128)(2,1)S(1)}, u32[]{:S(2)}, u32[]{:S(2)}) collective-permute-start(bf16[192,512]{1,0:T(8,128)(2,1)S(1)} %get-tuple-element.46), channel_id=1, source_target_pairs={{0,16},{8,24},{16,0},{24,8},{1,17},{9,25},{17,1},{25,9},{2,18},{10... | collective-permute-start | bytes 589832 | tf_op jit(solution)/shard_map/ppermute | solution.py:40
  51.2 1.4 %collective-permute-start.22 = (bf16[192,512]{1,0:T(8,128)(2,1)S(1)}, bf16[192,512]{1,0:T(8,128)(2,1)S(1)}, u32[]{:S(2)}, u32[]{:S(2)}) collective-permute-start(bf16[192,512]{1,0:T(8,128)(2,1)S(1)} %get-tuple-element.47), channel_id=1, source_target_pairs={{0,24},{8,16},{16,8},{24,0},{1,25},{9,17},{17,9},{25,1},{2,26},{10... | collective-permute-start | bytes 589832 | tf_op jit(solution)/shard_map/ppermute | solution.py:40
  53.3 3.4 %collective-permute-done.20.refs_1_ = bf16[192,512]{1,0:T(8,128)(2,1)S(1)} collective-permute-done((bf16[192,512]{1,0:T(8,128)(2,1)S(1)}, bf16[192,512]{1,0:T(8,128)(2,1)S(1)}, u32[]{:S(2)}, u32[]{:S(2)}) %collective-permute-start.20) | collective-permute-done | bytes 196640 | tf_op jit(solution)/shard_map/ppermute | solution.py:40
  56.7 3.4 %collective-permute-done.21.refs_2_ = bf16[192,512]{1,0:T(8,128)(2,1)S(1)} collective-permute-done((bf16[192,512]{1,0:T(8,128)(2,1)S(1)}, bf16[192,512]{1,0:T(8,128)(2,1)S(1)}, u32[]{:S(2)}, u32[]{:S(2)}) %collective-permute-start.21) | collective-permute-done | bytes 196640 | tf_op jit(solution)/shard_map/ppermute | solution.py:40
  61.8 1.0 %shard_map.114 = f32[512,512]{1,0:T(8,128)} custom-call(bf16[256,512]{1,0:T(8,128)(2,1)S(1)} %shard_map.112.refs_4_.refs_0_, bf16[256,512]{1,0:T(8,128)(2,1)S(1)} %collective-permute-done.23.refs_1_), custom_call_target="tpu_custom_call" | custom-call | tf_op jit(solution)/shard_map/pallas_call | solution.py:23
  (57 shorter events, 10.9 us)
Async XLA Ops:
  0.7 7.3 %collective-permute-start = (bf16[128,512]{1,0:T(8,128)(2,1)}, bf16[128,512]{1,0:T(8,128)(2,1)S(1)}, u32[]{:S(2)}, u32[]{:S(2)}) collective-permute-start(bf16[128,512]{1,0:T(8,128)(2,1)} %bitcast.3), channel_id=1, source_target_pairs={{0,8},{8,0},{16,24},{24,16},{1,9},{9,1},{17,25},{25,17},{2,10},{10... | collective-permute-start | bytes 393224 | tf_op jit(solution)/shard_map/ppermute | solution.py:40
  3.7 8.0 %collective-permute-start.1 = (bf16[128,512]{1,0:T(8,128)(2,1)}, bf16[128,512]{1,0:T(8,128)(2,1)S(1)}, u32[]{:S(2)}, u32[]{:S(2)}) collective-permute-start(bf16[128,512]{1,0:T(8,128)(2,1)} %bitcast.4), channel_id=1, source_target_pairs={{0,16},{8,24},{16,0},{24,8},{1,17},{9,25},{17,1},{25,9},{2,18},{10... | collective-permute-start | bytes 393224 | tf_op jit(solution)/shard_map/ppermute | solution.py:40
  5.2 6.5 %collective-permute-start.2 = (bf16[128,512]{1,0:T(8,128)(2,1)}, bf16[128,512]{1,0:T(8,128)(2,1)S(1)}, u32[]{:S(2)}, u32[]{:S(2)}) collective-permute-start(bf16[128,512]{1,0:T(8,128)(2,1)} %bitcast.5), channel_id=1, source_target_pairs={{0,24},{8,16},{16,8},{24,0},{1,25},{9,17},{17,9},{25,1},{2,26},{10... | collective-permute-start | bytes 393224 | tf_op jit(solution)/shard_map/ppermute | solution.py:40
  12.0 1.6 %collective-permute-start.4 = (bf16[256,512]{1,0:T(8,128)(2,1)S(1)}, bf16[256,512]{1,0:T(8,128)(2,1)S(1)}, u32[]{:S(2)}, u32[]{:S(2)}) collective-permute-start(bf16[256,512]{1,0:T(8,128)(2,1)S(1)} %shard_map.99), channel_id=1, source_target_pairs={{0,1},{1,0},{2,3},{3,2},{4,5},{5,4},{6,7},{7,6},{8,9},{9,8},{10,11... | collective-permute-start | bytes 786440 | tf_op jit(solution)/shard_map/ppermute | solution.py:40
  12.3 3.8 %collective-permute-start.3 = (bf16[256,512]{1,0:T(8,128)(2,1)S(1)}, bf16[256,512]{1,0:T(8,128)(2,1)S(1)}, u32[]{:S(2)}, u32[]{:S(2)}) collective-permute-start(bf16[256,512]{1,0:T(8,128)(2,1)S(1)} %shard_map.96), channel_id=1, source_target_pairs={{0,1},{1,0},{2,3},{3,2},{4,5},{5,4},{6,7},{7,6},{8,9},{9,8},{10,11... | collective-permute-start | bytes 786440 | tf_op jit(solution)/shard_map/ppermute | solution.py:40
  13.6 6.0 %collective-permute-start.6 = (bf16[128,512]{1,0:T(8,128)(2,1)S(1)}, bf16[128,512]{1,0:T(8,128)(2,1)S(1)}, u32[]{:S(2)}, u32[]{:S(2)}) collective-permute-start(bf16[128,512]{1,0:T(8,128)(2,1)S(1)} %get-tuple-element.30), channel_id=1, source_target_pairs={{0,2},{1,3},{2,0},{3,1},{4,6},{5,7},{6,4},{7,5},{8,10},{9,11},{10,... | collective-permute-start | bytes 393224 | tf_op jit(solution)/shard_map/ppermute | solution.py:40
  15.3 14.0 %collective-permute-start.11 = (bf16[512,512]{1,0:T(8,128)(2,1)S(1)}, bf16[512,512]{1,0:T(8,128)(2,1)S(1)}, u32[]{:S(2)}, u32[]{:S(2)}) collective-permute-start(bf16[512,512]{1,0:T(8,128)(2,1)S(1)} %get-tuple-element.39), channel_id=1, source_target_pairs={{0,1},{1,0},{2,3},{3,2},{4,5},{5,4},{6,7},{7,6},{8,9},{9,8},{10,11... | collective-permute-start | bytes 1572872 | tf_op jit(solution)/shard_map/ppermute | solution.py:40
  15.6 6.8 %collective-permute-start.5 = (bf16[128,512]{1,0:T(8,128)(2,1)S(1)}, bf16[128,512]{1,0:T(8,128)(2,1)S(1)}, u32[]{:S(2)}, u32[]{:S(2)}) collective-permute-start(bf16[128,512]{1,0:T(8,128)(2,1)S(1)} %get-tuple-element.28), channel_id=1, source_target_pairs={{0,2},{1,3},{2,0},{3,1},{4,6},{5,7},{6,4},{7,5},{8,10},{9,11},{10,... | collective-permute-start | bytes 393224 | tf_op jit(solution)/shard_map/ppermute | solution.py:40
  19.7 8.5 %collective-permute-start.7 = (bf16[128,512]{1,0:T(8,128)(2,1)S(1)}, bf16[128,512]{1,0:T(8,128)(2,1)S(1)}, u32[]{:S(2)}, u32[]{:S(2)}) collective-permute-start(bf16[128,512]{1,0:T(8,128)(2,1)S(1)} %shard_map.101), channel_id=1, source_target_pairs={{0,4},{1,5},{2,6},{3,7},{4,0},{5,1},{6,2},{7,3},{8,12},{9,13},{10,... | collective-permute-start | bytes 393224 | tf_op jit(solution)/shard_map/ppermute | solution.py:40
  29.0 1.6 %collective-permute-start.10 = (bf16[256,512]{1,0:T(8,128)(2,1)S(1)}, bf16[256,512]{1,0:T(8,128)(2,1)S(1)}, u32[]{:S(2)}, u32[]{:S(2)}) collective-permute-start(bf16[256,512]{1,0:T(8,128)(2,1)S(1)} %get-tuple-element.38), channel_id=1, source_target_pairs={{0,1},{1,0},{2,3},{3,2},{4,5},{5,4},{6,7},{7,6},{8,9},{9,8},{10,11... | collective-permute-start | bytes 786440 | tf_op jit(solution)/shard_map/ppermute | solution.py:40
  29.1 9.7 %collective-permute-start.9 = (bf16[128,512]{1,0:T(8,128)(2,1)S(1)}, bf16[128,512]{1,0:T(8,128)(2,1)S(1)}, u32[]{:S(2)}, u32[]{:S(2)}) collective-permute-start(bf16[128,512]{1,0:T(8,128)(2,1)S(1)} %get-tuple-element.34.refs_1_), channel_id=1, source_target_pairs={{0,4},{1,5},{2,6},{3,7},{4,0},{5,1},{6,2},{7,3},{8,12},{9,13},{10,... | collective-permute-start | bytes 393224 | tf_op jit(solution)/shard_map/ppermute | solution.py:40
  30.6 8.2 %collective-permute-start.12 = (bf16[64,512]{1,0:T(8,128)(2,1)S(1)}, bf16[64,512]{1,0:T(8,128)(2,1)S(1)}, u32[]{:S(2)}, u32[]{:S(2)}) collective-permute-start(bf16[64,512]{1,0:T(8,128)(2,1)S(1)} %get-tuple-element.40), channel_id=1, source_target_pairs={{0,8},{8,0},{16,24},{24,16},{1,9},{9,1},{17,25},{25,17},{2,10},{10... | collective-permute-start | bytes 196616 | tf_op jit(solution)/shard_map/ppermute | solution.py:40
  31.9 6.9 %collective-permute-start.13 = (bf16[64,512]{1,0:T(8,128)(2,1)S(1)}, bf16[64,512]{1,0:T(8,128)(2,1)S(1)}, u32[]{:S(2)}, u32[]{:S(2)}) collective-permute-start(bf16[64,512]{1,0:T(8,128)(2,1)S(1)} %get-tuple-element.41), channel_id=1, source_target_pairs={{0,16},{8,24},{16,0},{24,8},{1,17},{9,25},{17,1},{25,9},{2,18},{10... | collective-permute-start | bytes 196616 | tf_op jit(solution)/shard_map/ppermute | solution.py:40
  32.8 11.9 %collective-permute-start.8 = (bf16[128,512]{1,0:T(8,128)(2,1)S(1)}, bf16[128,512]{1,0:T(8,128)(2,1)S(1)}, u32[]{:S(2)}, u32[]{:S(2)}) collective-permute-start(bf16[128,512]{1,0:T(8,128)(2,1)S(1)} %get-tuple-element.34.refs_1_), channel_id=1, source_target_pairs={{0,2},{1,3},{2,0},{3,1},{4,6},{5,7},{6,4},{7,5},{8,10},{9,11},{10,... | collective-permute-start | bytes 393224 | tf_op jit(solution)/shard_map/ppermute | solution.py:40
  35.0 5.2 %collective-permute-start.16 = (bf16[64,512]{1,0:T(8,128)(2,1)S(1)}, bf16[64,512]{1,0:T(8,128)(2,1)S(1)}, u32[]{:S(2)}, u32[]{:S(2)}) collective-permute-start(bf16[64,512]{1,0:T(8,128)(2,1)S(1)} %get-tuple-element.43), channel_id=1, source_target_pairs={{0,24},{8,16},{16,8},{24,0},{1,25},{9,17},{17,9},{25,1},{2,26},{10... | collective-permute-start | bytes 196616 | tf_op jit(solution)/shard_map/ppermute | solution.py:40
  38.8 6.5 %collective-permute-start.14 = (bf16[128,512]{1,0:T(8,128)(2,1)S(1)}, bf16[128,512]{1,0:T(8,128)(2,1)S(1)}, u32[]{:S(2)}, u32[]{:S(2)}) collective-permute-start(bf16[128,512]{1,0:T(8,128)(2,1)S(1)} %shard_map.106.refs_3_), channel_id=1, source_target_pairs={{0,2},{1,3},{2,0},{3,1},{4,6},{5,7},{6,4},{7,5},{8,10},{9,11},{10,... | collective-permute-start | bytes 393224 | tf_op jit(solution)/shard_map/ppermute | solution.py:40
  40.2 6.7 %collective-permute-start.17 = (bf16[64,512]{1,0:T(8,128)(2,1)S(1)}, bf16[64,512]{1,0:T(8,128)(2,1)S(1)}, u32[]{:S(2)}, u32[]{:S(2)}) collective-permute-start(bf16[64,512]{1,0:T(8,128)(2,1)S(1)} %shard_map.109.refs_0_), channel_id=1, source_target_pairs={{0,2},{1,3},{2,0},{3,1},{4,6},{5,7},{6,4},{7,5},{8,10},{9,11},{10,... | collective-permute-start | bytes 196616 | tf_op jit(solution)/shard_map/ppermute | solution.py:40
  41.0 7.5 %collective-permute-start.18 = (bf16[64,512]{1,0:T(8,128)(2,1)S(1)}, bf16[64,512]{1,0:T(8,128)(2,1)S(1)}, u32[]{:S(2)}, u32[]{:S(2)}) collective-permute-start(bf16[64,512]{1,0:T(8,128)(2,1)S(1)} %shard_map.109.refs_0_), channel_id=1, source_target_pairs={{0,4},{1,5},{2,6},{3,7},{4,0},{5,1},{6,2},{7,3},{8,12},{9,13},{10,... | collective-permute-start | bytes 196616 | tf_op jit(solution)/shard_map/ppermute | solution.py:40
  41.8 6.7 %collective-permute-start.19 = (bf16[64,512]{1,0:T(8,128)(2,1)S(1)}, bf16[64,512]{1,0:T(8,128)(2,1)S(1)}, u32[]{:S(2)}, u32[]{:S(2)}) collective-permute-start(bf16[64,512]{1,0:T(8,128)(2,1)S(1)} %shard_map.109.refs_0_), channel_id=1, source_target_pairs={{0,6},{1,7},{2,4},{3,5},{4,2},{5,3},{6,0},{7,1},{8,14},{9,15},{10,... | collective-permute-start | bytes 196616 | tf_op jit(solution)/shard_map/ppermute | solution.py:40
  45.7 3.2 %collective-permute-start.15 = (bf16[512,512]{1,0:T(8,128)(2,1)S(1)}, bf16[512,512]{1,0:T(8,128)(2,1)S(1)}, u32[]{:S(2)}, u32[]{:S(2)}) collective-permute-start(bf16[512,512]{1,0:T(8,128)(2,1)S(1)} %shard_map.108), channel_id=1, source_target_pairs={{0,1},{1,0},{2,3},{3,2},{4,5},{5,4},{6,7},{7,6},{8,9},{9,8},{10,11... | collective-permute-start | bytes 1572872 | tf_op jit(solution)/shard_map/ppermute | solution.py:40
  49.1 7.7 %collective-permute-start.20 = (bf16[192,512]{1,0:T(8,128)(2,1)S(1)}, bf16[192,512]{1,0:T(8,128)(2,1)S(1)}, u32[]{:S(2)}, u32[]{:S(2)}) collective-permute-start(bf16[192,512]{1,0:T(8,128)(2,1)S(1)} %get-tuple-element.45), channel_id=1, source_target_pairs={{0,8},{8,0},{16,24},{24,16},{1,9},{9,1},{17,25},{25,17},{2,10},{10... | collective-permute-start | bytes 589832 | tf_op jit(solution)/shard_map/ppermute | solution.py:40
  50.3 9.8 %collective-permute-start.21 = (bf16[192,512]{1,0:T(8,128)(2,1)S(1)}, bf16[192,512]{1,0:T(8,128)(2,1)S(1)}, u32[]{:S(2)}, u32[]{:S(2)}) collective-permute-start(bf16[192,512]{1,0:T(8,128)(2,1)S(1)} %get-tuple-element.46), channel_id=1, source_target_pairs={{0,16},{8,24},{16,0},{24,8},{1,17},{9,25},{17,1},{25,9},{2,18},{10... | collective-permute-start | bytes 589832 | tf_op jit(solution)/shard_map/ppermute | solution.py:40
  51.2 9.0 %collective-permute-start.22 = (bf16[192,512]{1,0:T(8,128)(2,1)S(1)}, bf16[192,512]{1,0:T(8,128)(2,1)S(1)}, u32[]{:S(2)}, u32[]{:S(2)}) collective-permute-start(bf16[192,512]{1,0:T(8,128)(2,1)S(1)} %get-tuple-element.47), channel_id=1, source_target_pairs={{0,24},{8,16},{16,8},{24,0},{1,25},{9,17},{17,9},{25,1},{2,26},{10... | collective-permute-start | bytes 589832 | tf_op jit(solution)/shard_map/ppermute | solution.py:40
  60.2 1.6 %collective-permute-start.23 = (bf16[256,512]{1,0:T(8,128)(2,1)S(1)}, bf16[256,512]{1,0:T(8,128)(2,1)S(1)}, u32[]{:S(2)}, u32[]{:S(2)}) collective-permute-start(bf16[256,512]{1,0:T(8,128)(2,1)S(1)} %shard_map.112.refs_4_.refs_0_), channel_id=1, source_target_pairs={{0,1},{1,0},{2,3},{3,2},{4,5},{5,4},{6,7},{7,6},{8,9},{9,8},{10,11... | collective-permute-start | bytes 786440 | tf_op jit(solution)/shard_map/ppermute | solution.py:40
  (6 other events, 37.3 us)

commit v4 on v3

--- a/solution.py
+++ b/solution.py
@@ -14,7 +14,7 @@
 TILE = 128
 
 
-def call(kernel, outs, args, specs=None, scratch=(), after=(), alias={}, us=0):
+def call(kernel, outs, args, specs=None, scratch=(), after=(), us=0):
     held = sum(a.size * a.dtype.itemsize for a in (*args, *outs))
 
     def body(*refs):
@@ -24,7 +24,6 @@
         body,
         out_shape=outs,
         in_specs=(specs or [VMEM] * len(args)) + [pl.BlockSpec(memory_space=pl.ANY)] * len(after),
-        input_output_aliases=alias,
         out_specs=[VMEM] * len(outs),
         scratch_shapes=scratch,
         compiler_params=pltpu.CompilerParams(vmem_limit_bytes=12 * 2**20 + 3 * held),
@@ -92,7 +91,7 @@
 
 
 def relay(value, out):
-    pass
+    out[...] = value[...]
 
 
 def add_all(*refs):
@@ -235,7 +234,9 @@
     )
     other_w = core_swap(other_w)
     parts_w = call(add_split, [like(piece, width)] * n_row, (mine_w, other_w), after=(other_t,))
-    terms_w = [parts_w[0]] + [row_swap(parts_w[k], k) for k in range(1, n_row)]
+    terms_w = {k: row_swap(parts_w[k], k) for k in reversed(range(1, n_row))}
+    terms_w[0] = parts_w[0]
+    terms_w = [terms_w[k] for k in range(n_row)]
     same = [grad_rows] + [None] * (n_z - 1)
     bit = n_z // 2
     while bit:
@@ -243,11 +244,7 @@
             same[k | bit] = z_swap(same[k], bit)
             if bit > 1:
                 (same[k | bit],) = call(
-                    relay,
-                    [like(TILE, width)],
-                    (same[k | bit],),
-                    after=terms_w[1 : n_row - 1],
-                    alias={0: 0},
+                    relay, [like(TILE, width)], (same[k | bit],), after=tuple(terms_w[2:])
                 )
         bit //= 2
     (plane_w,) = call(add_all, [like(piece, width)], terms_w)
@@ -261,7 +258,7 @@
         [like(TILE, width, dtype=F32)] + [like(TILE + piece, width)] * (n_row - 1),
         (mine, other, final_w),
     )
-    terms = [row_swap(part, k + 1) for k, part in enumerate(parts)]
+    terms = [row_swap(parts[k - 1], k) for k in reversed(range(1, n_row))][::-1]
     layer_out, done = call(
         activation, [like(TILE, width), like(8, TILE, dtype=F32)], (hidden,), us=1
     )

time: 63 us -> 63.1 us (level)
  starting transfers between devices: 24.5 us -> 25.4 us
  waiting for transfers between devices: 29 us -> 28.2 us
    ppermute x24, starting transfers between devices: 24.5 us -> 25.4 us  [swap(): return lax.ppermute(value, axis, [(i, i ^ mask) for i in range(size)])]
    ppermute x24, waiting for transfers between devices: 29 us -> 28.2 us  [swap(): return lax.ppermute(value, axis, [(i, i ^ mask) for i in range(size)])]
  transfers between devices with their start and end apart: 24 -> 24, of which waited for: 13 -> 12; matrix products, arithmetic and copies ran while one was open for 0% -> 0% of each run, Pallas kernels for 8% -> 8%
where the time goes in v4:
time: 63.1 us; the launch traced here: 62.9 us
  waiting for transfers between devices  28.2 us (45%)
  starting transfers between devices  25.4 us (40%)
  Pallas kernels  6.66 us (11%)
  between operations  1.51 us (2%)
  local copies, waits for them, and re-layouts  1.15 us (2%)
    ppermute x24, waiting for transfers between devices, swap(): return lax.ppermute(value, axis, [(i, i ^ mask) for i in range(size)])  28.2 us
    ppermute x24, starting transfers between devices, swap(): return lax.ppermute(value, axis, [(i, i ^ mask) for i in range(size)])  25.4 us
    pallas_call x21, Pallas kernels, call(): pl.pallas_call(body, out_shape=outs, in_specs=(specs or [VMEM] * len(args...  6.66 us
  transfers between devices with their start and end apart: 24, of which 12 were waited for; matrix products, arithmetic and copies ran while one was open for 0% of the time, Pallas kernels for 8%

profile of v4, /device:TPU:0, one launch (start us, length us, event | category | flops | bytes accessed | tf_op | source)
XLA Modules:
  0.0 62.9 jit_solution(17482359325869550531)
XLA Ops:
  0.7 3.0 %collective-permute-start = (bf16[128,512]{1,0:T(8,128)(2,1)}, bf16[128,512]{1,0:T(8,128)(2,1)S(1)}, u32[]{:S(2)}, u32[]{:S(2)}) collective-permute-start(bf16[128,512]{1,0:T(8,128)(2,1)} %bitcast.3), channel_id=1, source_target_pairs={{0,8},{8,0},{16,24},{24,16},{1,9},{9,1},{17,25},{25,17},{2,10},{10... | collective-permute-start | bytes 393224 | tf_op jit(solution)/shard_map/ppermute | solution.py:39
  3.7 1.5 %collective-permute-start.1 = (bf16[128,512]{1,0:T(8,128)(2,1)}, bf16[128,512]{1,0:T(8,128)(2,1)S(1)}, u32[]{:S(2)}, u32[]{:S(2)}) collective-permute-start(bf16[128,512]{1,0:T(8,128)(2,1)} %bitcast.4), channel_id=1, source_target_pairs={{0,16},{8,24},{16,0},{24,8},{1,17},{9,25},{17,1},{25,9},{2,18},{10... | collective-permute-start | bytes 393224 | tf_op jit(solution)/shard_map/ppermute | solution.py:39
  5.9 1.1 %copy-done.1 = bf16[1,1,24,128,128]{4,3,2,1,0:T(8,128)(2,1)S(1)} copy-done((bf16[1,1,24,128,128]{4,3,2,1,0:T(8,128)(2,1)S(1)}, bf16[1,1,24,128,128]{4,3,2,1,0:T(8,128)(2,1)}, u32[]{:S(2)}) %copy-start.1) | copy-done | bytes 786456
  8.0 3.7 %collective-permute-done.1.refs_3_ = bf16[128,512]{1,0:T(8,128)(2,1)S(1)} collective-permute-done((bf16[128,512]{1,0:T(8,128)(2,1)}, bf16[128,512]{1,0:T(8,128)(2,1)S(1)}, u32[]{:S(2)}, u32[]{:S(2)}) %collective-permute-start.1) | collective-permute-done | bytes 131104 | tf_op jit(solution)/shard_map/ppermute | solution.py:39
  13.6 1.6 %collective-permute-start.6 = (bf16[128,512]{1,0:T(8,128)(2,1)S(1)}, bf16[128,512]{1,0:T(8,128)(2,1)S(1)}, u32[]{:S(2)}, u32[]{:S(2)}) collective-permute-start(bf16[128,512]{1,0:T(8,128)(2,1)S(1)} %get-tuple-element.30), channel_id=1, source_target_pairs={{0,2},{1,3},{2,0},{3,1},{4,6},{5,7},{6,4},{7,5},{8,10},{9,11},{10,... | collective-permute-start | bytes 393224 | tf_op jit(solution)/shard_map/ppermute | solution.py:39
  16.1 3.5 %collective-permute-done.6.refs_1_ = bf16[128,512]{1,0:T(8,128)(2,1)S(1)} collective-permute-done((bf16[128,512]{1,0:T(8,128)(2,1)S(1)}, bf16[128,512]{1,0:T(8,128)(2,1)S(1)}, u32[]{:S(2)}, u32[]{:S(2)}) %collective-permute-start.6) | collective-permute-done | bytes 131104 | tf_op jit(solution)/shard_map/ppermute | solution.py:39
  19.7 2.7 %collective-permute-start.7 = (bf16[128,512]{1,0:T(8,128)(2,1)S(1)}, bf16[128,512]{1,0:T(8,128)(2,1)S(1)}, u32[]{:S(2)}, u32[]{:S(2)}) collective-permute-start(bf16[128,512]{1,0:T(8,128)(2,1)S(1)} %shard_map.101), channel_id=1, source_target_pairs={{0,4},{1,5},{2,6},{3,7},{4,0},{5,1},{6,2},{7,3},{8,12},{9,13},{10,... | collective-permute-start | bytes 393224 | tf_op jit(solution)/shard_map/ppermute | solution.py:39
  22.3 5.8 %collective-permute-done.7.refs_4_ = bf16[128,512]{1,0:T(8,128)(2,1)S(1)} collective-permute-done((bf16[128,512]{1,0:T(8,128)(2,1)S(1)}, bf16[128,512]{1,0:T(8,128)(2,1)S(1)}, u32[]{:S(2)}, u32[]{:S(2)}) %collective-permute-start.7) | collective-permute-done | bytes 131104 | tf_op jit(solution)/shard_map/ppermute | solution.py:39
  29.3 1.3 %collective-permute-done.10.refs_1_ = bf16[256,512]{1,0:T(8,128)(2,1)S(1)} collective-permute-done((bf16[256,512]{1,0:T(8,128)(2,1)S(1)}, bf16[256,512]{1,0:T(8,128)(2,1)S(1)}, u32[]{:S(2)}, u32[]{:S(2)}) %collective-permute-start.10) | collective-permute-done | bytes 262176 | tf_op jit(solution)/shard_map/ppermute | solution.py:39
  30.6 1.6 %collective-permute-start.12 = (bf16[64,512]{1,0:T(8,128)(2,1)S(1)}, bf16[64,512]{1,0:T(8,128)(2,1)S(1)}, u32[]{:S(2)}, u32[]{:S(2)}) collective-permute-start(bf16[64,512]{1,0:T(8,128)(2,1)S(1)} %get-tuple-element.40), channel_id=1, source_target_pairs={{0,16},{8,24},{16,0},{24,8},{1,17},{9,25},{17,1},{25,9},{2,18},{10... | collective-permute-start | bytes 196616 | tf_op jit(solution)/shard_map/ppermute | solution.py:39
  32.2 1.2 %collective-permute-start.13 = (bf16[64,512]{1,0:T(8,128)(2,1)S(1)}, bf16[64,512]{1,0:T(8,128)(2,1)S(1)}, u32[]{:S(2)}, u32[]{:S(2)}) collective-permute-start(bf16[64,512]{1,0:T(8,128)(2,1)S(1)} %get-tuple-element.41), channel_id=1, source_target_pairs={{0,24},{8,16},{16,8},{24,0},{1,25},{9,17},{17,9},{25,1},{2,26},{10... | collective-permute-start | bytes 196616 | tf_op jit(solution)/shard_map/ppermute | solution.py:39
  33.4 2.2 %collective-permute-start.8 = (bf16[128,512]{1,0:T(8,128)(2,1)S(1)}, bf16[128,512]{1,0:T(8,128)(2,1)S(1)}, u32[]{:S(2)}, u32[]{:S(2)}) collective-permute-start(bf16[128,512]{1,0:T(8,128)(2,1)S(1)} %get-tuple-element.34.refs_1_), channel_id=1, source_target_pairs={{0,2},{1,3},{2,0},{3,1},{4,6},{5,7},{6,4},{7,5},{8,10},{9,11},{10,... | collective-permute-start | bytes 393224 | tf_op jit(solution)/shard_map/ppermute | solution.py:39
  36.4 2.4 %collective-permute-done.9.refs_0_ = bf16[128,512]{1,0:T(8,128)(2,1)S(1)} collective-permute-done((bf16[128,512]{1,0:T(8,128)(2,1)S(1)}, bf16[128,512]{1,0:T(8,128)(2,1)S(1)}, u32[]{:S(2)}, u32[]{:S(2)}) %collective-permute-start.9) | collective-permute-done | bytes 131104 | tf_op jit(solution)/shard_map/ppermute | solution.py:39
  38.8 1.2 %collective-permute-start.14 = (bf16[128,512]{1,0:T(8,128)(2,1)S(1)}, bf16[128,512]{1,0:T(8,128)(2,1)S(1)}, u32[]{:S(2)}, u32[]{:S(2)}) collective-permute-start(bf16[128,512]{1,0:T(8,128)(2,1)S(1)} %shard_map.106.refs_3_), channel_id=1, source_target_pairs={{0,2},{1,3},{2,0},{3,1},{4,6},{5,7},{6,4},{7,5},{8,10},{9,11},{10,... | collective-permute-start | bytes 393224 | tf_op jit(solution)/shard_map/ppermute | solution.py:39
  40.0 1.0 %collective-permute-start.17 = (bf16[64,512]{1,0:T(8,128)(2,1)S(1)}, bf16[64,512]{1,0:T(8,128)(2,1)S(1)}, u32[]{:S(2)}, u32[]{:S(2)}) collective-permute-start(bf16[64,512]{1,0:T(8,128)(2,1)S(1)} %shard_map.109.refs_0_), channel_id=1, source_target_pairs={{0,2},{1,3},{2,0},{3,1},{4,6},{5,7},{6,4},{7,5},{8,10},{9,11},{10,... | collective-permute-start | bytes 196616 | tf_op jit(solution)/shard_map/ppermute | solution.py:39
  41.6 2.9 %collective-permute-start.19 = (bf16[64,512]{1,0:T(8,128)(2,1)S(1)}, bf16[64,512]{1,0:T(8,128)(2,1)S(1)}, u32[]{:S(2)}, u32[]{:S(2)}) collective-permute-start(bf16[64,512]{1,0:T(8,128)(2,1)S(1)} %shard_map.109.refs_0_), channel_id=1, source_target_pairs={{0,6},{1,7},{2,4},{3,5},{4,2},{5,3},{6,0},{7,1},{8,14},{9,15},{10,... | collective-permute-start | bytes 196616 | tf_op jit(solution)/shard_map/ppermute | solution.py:39
  44.5 1.0 %collective-permute-done.14.refs_4_ = bf16[128,512]{1,0:T(8,128)(2,1)S(1)} collective-permute-done((bf16[128,512]{1,0:T(8,128)(2,1)S(1)}, bf16[128,512]{1,0:T(8,128)(2,1)S(1)}, u32[]{:S(2)}, u32[]{:S(2)}) %collective-permute-start.14) | collective-permute-done | bytes 131104 | tf_op jit(solution)/shard_map/ppermute | solution.py:39
  46.0 1.1 %collective-permute-done.17.refs_1_ = bf16[64,512]{1,0:T(8,128)(2,1)S(1)} collective-permute-done((bf16[64,512]{1,0:T(8,128)(2,1)S(1)}, bf16[64,512]{1,0:T(8,128)(2,1)S(1)}, u32[]{:S(2)}, u32[]{:S(2)}) %collective-permute-start.17) | collective-permute-done | bytes 65568 | tf_op jit(solution)/shard_map/ppermute | solution.py:39
  47.1 1.4 %collective-permute-done.18.refs_2_ = bf16[64,512]{1,0:T(8,128)(2,1)S(1)} collective-permute-done((bf16[64,512]{1,0:T(8,128)(2,1)S(1)}, bf16[64,512]{1,0:T(8,128)(2,1)S(1)}, u32[]{:S(2)}, u32[]{:S(2)}) %collective-permute-start.18) | collective-permute-done | bytes 65568 | tf_op jit(solution)/shard_map/ppermute | solution.py:39
  49.1 1.3 %collective-permute-start.20 = (bf16[192,512]{1,0:T(8,128)(2,1)S(1)}, bf16[192,512]{1,0:T(8,128)(2,1)S(1)}, u32[]{:S(2)}, u32[]{:S(2)}) collective-permute-start(bf16[192,512]{1,0:T(8,128)(2,1)S(1)} %get-tuple-element.45), channel_id=1, source_target_pairs={{0,8},{8,0},{16,24},{24,16},{1,9},{9,1},{17,25},{25,17},{2,10},{10... | collective-permute-start | bytes 589832 | tf_op jit(solution)/shard_map/ppermute | solution.py:39
  51.2 1.4 %collective-permute-start.22 = (bf16[192,512]{1,0:T(8,128)(2,1)S(1)}, bf16[192,512]{1,0:T(8,128)(2,1)S(1)}, u32[]{:S(2)}, u32[]{:S(2)}) collective-permute-start(bf16[192,512]{1,0:T(8,128)(2,1)S(1)} %get-tuple-element.47), channel_id=1, source_target_pairs={{0,24},{8,16},{16,8},{24,0},{1,25},{9,17},{17,9},{25,1},{2,26},{10... | collective-permute-start | bytes 589832 | tf_op jit(solution)/shard_map/ppermute | solution.py:39
  53.3 3.6 %collective-permute-done.20.refs_1_ = bf16[192,512]{1,0:T(8,128)(2,1)S(1)} collective-permute-done((bf16[192,512]{1,0:T(8,128)(2,1)S(1)}, bf16[192,512]{1,0:T(8,128)(2,1)S(1)}, u32[]{:S(2)}, u32[]{:S(2)}) %collective-permute-start.20) | collective-permute-done | bytes 196640 | tf_op jit(solution)/shard_map/ppermute | solution.py:39
  57.0 3.3 %collective-permute-done.21.refs_2_ = bf16[192,512]{1,0:T(8,128)(2,1)S(1)} collective-permute-done((bf16[192,512]{1,0:T(8,128)(2,1)S(1)}, bf16[192,512]{1,0:T(8,128)(2,1)S(1)}, u32[]{:S(2)}, u32[]{:S(2)}) %collective-permute-start.21) | collective-permute-done | bytes 196640 | tf_op jit(solution)/shard_map/ppermute | solution.py:39
  61.9 1.0 %shard_map.114 = f32[512,512]{1,0:T(8,128)} custom-call(bf16[256,512]{1,0:T(8,128)(2,1)S(1)} %shard_map.112.refs_4_.refs_0_, bf16[256,512]{1,0:T(8,128)(2,1)S(1)} %collective-permute-done.23.refs_1_), custom_call_target="tpu_custom_call" | custom-call | tf_op jit(solution)/shard_map/pallas_call | solution.py:23
  (57 shorter events, 10.7 us)
Async XLA Ops:
  0.7 7.3 %collective-permute-start = (bf16[128,512]{1,0:T(8,128)(2,1)}, bf16[128,512]{1,0:T(8,128)(2,1)S(1)}, u32[]{:S(2)}, u32[]{:S(2)}) collective-permute-start(bf16[128,512]{1,0:T(8,128)(2,1)} %bitcast.3), channel_id=1, source_target_pairs={{0,8},{8,0},{16,24},{24,16},{1,9},{9,1},{17,25},{25,17},{2,10},{10... | collective-permute-start | bytes 393224 | tf_op jit(solution)/shard_map/ppermute | solution.py:39
  3.7 8.0 %collective-permute-start.1 = (bf16[128,512]{1,0:T(8,128)(2,1)}, bf16[128,512]{1,0:T(8,128)(2,1)S(1)}, u32[]{:S(2)}, u32[]{:S(2)}) collective-permute-start(bf16[128,512]{1,0:T(8,128)(2,1)} %bitcast.4), channel_id=1, source_target_pairs={{0,16},{8,24},{16,0},{24,8},{1,17},{9,25},{17,1},{25,9},{2,18},{10... | collective-permute-start | bytes 393224 | tf_op jit(solution)/shard_map/ppermute | solution.py:39
  5.2 6.5 %collective-permute-start.2 = (bf16[128,512]{1,0:T(8,128)(2,1)}, bf16[128,512]{1,0:T(8,128)(2,1)S(1)}, u32[]{:S(2)}, u32[]{:S(2)}) collective-permute-start(bf16[128,512]{1,0:T(8,128)(2,1)} %bitcast.5), channel_id=1, source_target_pairs={{0,24},{8,16},{16,8},{24,0},{1,25},{9,17},{17,9},{25,1},{2,26},{10... | collective-permute-start | bytes 393224 | tf_op jit(solution)/shard_map/ppermute | solution.py:39
  12.0 1.6 %collective-permute-start.4 = (bf16[256,512]{1,0:T(8,128)(2,1)S(1)}, bf16[256,512]{1,0:T(8,128)(2,1)S(1)}, u32[]{:S(2)}, u32[]{:S(2)}) collective-permute-start(bf16[256,512]{1,0:T(8,128)(2,1)S(1)} %shard_map.99), channel_id=1, source_target_pairs={{0,1},{1,0},{2,3},{3,2},{4,5},{5,4},{6,7},{7,6},{8,9},{9,8},{10,11... | collective-permute-start | bytes 786440 | tf_op jit(solution)/shard_map/ppermute | solution.py:39
  12.3 3.8 %collective-permute-start.3 = (bf16[256,512]{1,0:T(8,128)(2,1)S(1)}, bf16[256,512]{1,0:T(8,128)(2,1)S(1)}, u32[]{:S(2)}, u32[]{:S(2)}) collective-permute-start(bf16[256,512]{1,0:T(8,128)(2,1)S(1)} %shard_map.96), channel_id=1, source_target_pairs={{0,1},{1,0},{2,3},{3,2},{4,5},{5,4},{6,7},{7,6},{8,9},{9,8},{10,11... | collective-permute-start | bytes 786440 | tf_op jit(solution)/shard_map/ppermute | solution.py:39
  13.6 6.0 %collective-permute-start.6 = (bf16[128,512]{1,0:T(8,128)(2,1)S(1)}, bf16[128,512]{1,0:T(8,128)(2,1)S(1)}, u32[]{:S(2)}, u32[]{:S(2)}) collective-permute-start(bf16[128,512]{1,0:T(8,128)(2,1)S(1)} %get-tuple-element.30), channel_id=1, source_target_pairs={{0,2},{1,3},{2,0},{3,1},{4,6},{5,7},{6,4},{7,5},{8,10},{9,11},{10,... | collective-permute-start | bytes 393224 | tf_op jit(solution)/shard_map/ppermute | solution.py:39
  15.3 14.0 %collective-permute-start.11 = (bf16[512,512]{1,0:T(8,128)(2,1)S(1)}, bf16[512,512]{1,0:T(8,128)(2,1)S(1)}, u32[]{:S(2)}, u32[]{:S(2)}) collective-permute-start(bf16[512,512]{1,0:T(8,128)(2,1)S(1)} %get-tuple-element.39), channel_id=1, source_target_pairs={{0,1},{1,0},{2,3},{3,2},{4,5},{5,4},{6,7},{7,6},{8,9},{9,8},{10,11... | collective-permute-start | bytes 1572872 | tf_op jit(solution)/shard_map/ppermute | solution.py:39
  15.6 6.8 %collective-permute-start.5 = (bf16[128,512]{1,0:T(8,128)(2,1)S(1)}, bf16[128,512]{1,0:T(8,128)(2,1)S(1)}, u32[]{:S(2)}, u32[]{:S(2)}) collective-permute-start(bf16[128,512]{1,0:T(8,128)(2,1)S(1)} %get-tuple-element.28), channel_id=1, source_target_pairs={{0,2},{1,3},{2,0},{3,1},{4,6},{5,7},{6,4},{7,5},{8,10},{9,11},{10,... | collective-permute-start | bytes 393224 | tf_op jit(solution)/shard_map/ppermute | solution.py:39
  19.7 8.5 %collective-permute-start.7 = (bf16[128,512]{1,0:T(8,128)(2,1)S(1)}, bf16[128,512]{1,0:T(8,128)(2,1)S(1)}, u32[]{:S(2)}, u32[]{:S(2)}) collective-permute-start(bf16[128,512]{1,0:T(8,128)(2,1)S(1)} %shard_map.101), channel_id=1, source_target_pairs={{0,4},{1,5},{2,6},{3,7},{4,0},{5,1},{6,2},{7,3},{8,12},{9,13},{10,... | collective-permute-start | bytes 393224 | tf_op jit(solution)/shard_map/ppermute | solution.py:39
  29.0 1.6 %collective-permute-start.10 = (bf16[256,512]{1,0:T(8,128)(2,1)S(1)}, bf16[256,512]{1,0:T(8,128)(2,1)S(1)}, u32[]{:S(2)}, u32[]{:S(2)}) collective-permute-start(bf16[256,512]{1,0:T(8,128)(2,1)S(1)} %get-tuple-element.38), channel_id=1, source_target_pairs={{0,1},{1,0},{2,3},{3,2},{4,5},{5,4},{6,7},{7,6},{8,9},{9,8},{10,11... | collective-permute-start | bytes 786440 | tf_op jit(solution)/shard_map/ppermute | solution.py:39
  29.1 9.7 %collective-permute-start.9 = (bf16[128,512]{1,0:T(8,128)(2,1)S(1)}, bf16[128,512]{1,0:T(8,128)(2,1)S(1)}, u32[]{:S(2)}, u32[]{:S(2)}) collective-permute-start(bf16[128,512]{1,0:T(8,128)(2,1)S(1)} %get-tuple-element.34.refs_1_), channel_id=1, source_target_pairs={{0,4},{1,5},{2,6},{3,7},{4,0},{5,1},{6,2},{7,3},{8,12},{9,13},{10,... | collective-permute-start | bytes 393224 | tf_op jit(solution)/shard_map/ppermute | solution.py:39
  30.6 8.2 %collective-permute-start.12 = (bf16[64,512]{1,0:T(8,128)(2,1)S(1)}, bf16[64,512]{1,0:T(8,128)(2,1)S(1)}, u32[]{:S(2)}, u32[]{:S(2)}) collective-permute-start(bf16[64,512]{1,0:T(8,128)(2,1)S(1)} %get-tuple-element.40), channel_id=1, source_target_pairs={{0,16},{8,24},{16,0},{24,8},{1,17},{9,25},{17,1},{25,9},{2,18},{10... | collective-permute-start | bytes 196616 | tf_op jit(solution)/shard_map/ppermute | solution.py:39
  32.2 6.6 %collective-permute-start.13 = (bf16[64,512]{1,0:T(8,128)(2,1)S(1)}, bf16[64,512]{1,0:T(8,128)(2,1)S(1)}, u32[]{:S(2)}, u32[]{:S(2)}) collective-permute-start(bf16[64,512]{1,0:T(8,128)(2,1)S(1)} %get-tuple-element.41), channel_id=1, source_target_pairs={{0,24},{8,16},{16,8},{24,0},{1,25},{9,17},{17,9},{25,1},{2,26},{10... | collective-permute-start | bytes 196616 | tf_op jit(solution)/shard_map/ppermute | solution.py:39
  33.4 11.1 %collective-permute-start.8 = (bf16[128,512]{1,0:T(8,128)(2,1)S(1)}, bf16[128,512]{1,0:T(8,128)(2,1)S(1)}, u32[]{:S(2)}, u32[]{:S(2)}) collective-permute-start(bf16[128,512]{1,0:T(8,128)(2,1)S(1)} %get-tuple-element.34.refs_1_), channel_id=1, source_target_pairs={{0,2},{1,3},{2,0},{3,1},{4,6},{5,7},{6,4},{7,5},{8,10},{9,11},{10,... | collective-permute-start | bytes 393224 | tf_op jit(solution)/shard_map/ppermute | solution.py:39
  35.6 4.4 %collective-permute-start.16 = (bf16[64,512]{1,0:T(8,128)(2,1)S(1)}, bf16[64,512]{1,0:T(8,128)(2,1)S(1)}, u32[]{:S(2)}, u32[]{:S(2)}) collective-permute-start(bf16[64,512]{1,0:T(8,128)(2,1)S(1)} %get-tuple-element.43), channel_id=1, source_target_pairs={{0,8},{8,0},{16,24},{24,16},{1,9},{9,1},{17,25},{25,17},{2,10},{10... | collective-permute-start | bytes 196616 | tf_op jit(solution)/shard_map/ppermute | solution.py:39
  38.8 6.6 %collective-permute-start.14 = (bf16[128,512]{1,0:T(8,128)(2,1)S(1)}, bf16[128,512]{1,0:T(8,128)(2,1)S(1)}, u32[]{:S(2)}, u32[]{:S(2)}) collective-permute-start(bf16[128,512]{1,0:T(8,128)(2,1)S(1)} %shard_map.106.refs_3_), channel_id=1, source_target_pairs={{0,2},{1,3},{2,0},{3,1},{4,6},{5,7},{6,4},{7,5},{8,10},{9,11},{10,... | collective-permute-start | bytes 393224 | tf_op jit(solution)/shard_map/ppermute | solution.py:39
  40.0 7.1 %collective-permute-start.17 = (bf16[64,512]{1,0:T(8,128)(2,1)S(1)}, bf16[64,512]{1,0:T(8,128)(2,1)S(1)}, u32[]{:S(2)}, u32[]{:S(2)}) collective-permute-start(bf16[64,512]{1,0:T(8,128)(2,1)S(1)} %shard_map.109.refs_0_), channel_id=1, source_target_pairs={{0,2},{1,3},{2,0},{3,1},{4,6},{5,7},{6,4},{7,5},{8,10},{9,11},{10,... | collective-permute-start | bytes 196616 | tf_op jit(solution)/shard_map/ppermute | solution.py:39
  41.0 7.5 %collective-permute-start.18 = (bf16[64,512]{1,0:T(8,128)(2,1)S(1)}, bf16[64,512]{1,0:T(8,128)(2,1)S(1)}, u32[]{:S(2)}, u32[]{:S(2)}) collective-permute-start(bf16[64,512]{1,0:T(8,128)(2,1)S(1)} %shard_map.109.refs_0_), channel_id=1, source_target_pairs={{0,4},{1,5},{2,6},{3,7},{4,0},{5,1},{6,2},{7,3},{8,12},{9,13},{10,... | collective-permute-start | bytes 196616 | tf_op jit(solution)/shard_map/ppermute | solution.py:39
  41.6 6.9 %collective-permute-start.19 = (bf16[64,512]{1,0:T(8,128)(2,1)S(1)}, bf16[64,512]{1,0:T(8,128)(2,1)S(1)}, u32[]{:S(2)}, u32[]{:S(2)}) collective-permute-start(bf16[64,512]{1,0:T(8,128)(2,1)S(1)} %shard_map.109.refs_0_), channel_id=1, source_target_pairs={{0,6},{1,7},{2,4},{3,5},{4,2},{5,3},{6,0},{7,1},{8,14},{9,15},{10,... | collective-permute-start | bytes 196616 | tf_op jit(solution)/shard_map/ppermute | solution.py:39
  45.9 3.1 %collective-permute-start.15 = (bf16[512,512]{1,0:T(8,128)(2,1)S(1)}, bf16[512,512]{1,0:T(8,128)(2,1)S(1)}, u32[]{:S(2)}, u32[]{:S(2)}) collective-permute-start(bf16[512,512]{1,0:T(8,128)(2,1)S(1)} %shard_map.108), channel_id=1, source_target_pairs={{0,1},{1,0},{2,3},{3,2},{4,5},{5,4},{6,7},{7,6},{8,9},{9,8},{10,11... | collective-permute-start | bytes 1572872 | tf_op jit(solution)/shard_map/ppermute | solution.py:39
  49.1 7.9 %collective-permute-start.20 = (bf16[192,512]{1,0:T(8,128)(2,1)S(1)}, bf16[192,512]{1,0:T(8,128)(2,1)S(1)}, u32[]{:S(2)}, u32[]{:S(2)}) collective-permute-start(bf16[192,512]{1,0:T(8,128)(2,1)S(1)} %get-tuple-element.45), channel_id=1, source_target_pairs={{0,8},{8,0},{16,24},{24,16},{1,9},{9,1},{17,25},{25,17},{2,10},{10... | collective-permute-start | bytes 589832 | tf_op jit(solution)/shard_map/ppermute | solution.py:39
  50.4 9.9 %collective-permute-start.21 = (bf16[192,512]{1,0:T(8,128)(2,1)S(1)}, bf16[192,512]{1,0:T(8,128)(2,1)S(1)}, u32[]{:S(2)}, u32[]{:S(2)}) collective-permute-start(bf16[192,512]{1,0:T(8,128)(2,1)S(1)} %get-tuple-element.46), channel_id=1, source_target_pairs={{0,16},{8,24},{16,0},{24,8},{1,17},{9,25},{17,1},{25,9},{2,18},{10... | collective-permute-start | bytes 589832 | tf_op jit(solution)/shard_map/ppermute | solution.py:39
  51.2 9.1 %collective-permute-start.22 = (bf16[192,512]{1,0:T(8,128)(2,1)S(1)}, bf16[192,512]{1,0:T(8,128)(2,1)S(1)}, u32[]{:S(2)}, u32[]{:S(2)}) collective-permute-start(bf16[192,512]{1,0:T(8,128)(2,1)S(1)} %get-tuple-element.47), channel_id=1, source_target_pairs={{0,24},{8,16},{16,8},{24,0},{1,25},{9,17},{17,9},{25,1},{2,26},{10... | collective-permute-start | bytes 589832 | tf_op jit(solution)/shard_map/ppermute | solution.py:39
  60.3 1.6 %collective-permute-start.23 = (bf16[256,512]{1,0:T(8,128)(2,1)S(1)}, bf16[256,512]{1,0:T(8,128)(2,1)S(1)}, u32[]{:S(2)}, u32[]{:S(2)}) collective-permute-start(bf16[256,512]{1,0:T(8,128)(2,1)S(1)} %shard_map.112.refs_4_.refs_0_), channel_id=1, source_target_pairs={{0,1},{1,0},{2,3},{3,2},{4,5},{5,4},{6,7},{7,6},{8,9},{9,8},{10,11... | collective-permute-start | bytes 786440 | tf_op jit(solution)/shard_map/ppermute | solution.py:39
  (6 other events, 37.3 us)

commit v5 on v4

--- a/solution.py
+++ b/solution.py
@@ -234,9 +234,7 @@
     )
     other_w = core_swap(other_w)
     parts_w = call(add_split, [like(piece, width)] * n_row, (mine_w, other_w), after=(other_t,))
-    terms_w = {k: row_swap(parts_w[k], k) for k in reversed(range(1, n_row))}
-    terms_w[0] = parts_w[0]
-    terms_w = [terms_w[k] for k in range(n_row)]
+    terms_w = [parts_w[0]] + [row_swap(parts_w[k], k) for k in range(1, n_row)]
     same = [grad_rows] + [None] * (n_z - 1)
     bit = n_z // 2
     while bit:
@@ -244,7 +242,7 @@
             same[k | bit] = z_swap(same[k], bit)
             if bit > 1:
                 (same[k | bit],) = call(
-                    relay, [like(TILE, width)], (same[k | bit],), after=tuple(terms_w[2:])
+                    relay, [like(TILE, width)], (same[k | bit],), after=terms_w[1 : n_row - 1]
                 )
         bit //= 2
     (plane_w,) = call(add_all, [like(piece, width)], terms_w)
@@ -258,7 +256,7 @@
         [like(TILE, width, dtype=F32)] + [like(TILE + piece, width)] * (n_row - 1),
         (mine, other, final_w),
     )
-    terms = [row_swap(parts[k - 1], k) for k in reversed(range(1, n_row))][::-1]
+    terms = [row_swap(part, k + 1) for k, part in enumerate(parts)]
     layer_out, done = call(
         activation, [like(TILE, width), like(8, TILE, dtype=F32)], (hidden,), us=1
     )

time: 63.1 us -> 63 us (level)
  starting transfers between devices: 25.4 us -> 24.6 us
    ppermute x24, starting transfers between devices: 25.4 us -> 24.6 us  [swap(): return lax.ppermute(value, axis, [(i, i ^ mask) for i in range(size)])]
  transfers between devices with their start and end apart: 24 -> 24, of which waited for: 12 -> 13; matrix products, arithmetic and copies ran while one was open for 0% -> 0% of each run, Pallas kernels for 8% -> 9%
where the time goes in v5:
time: 63 us; the launch traced here: 62.8 us
  waiting for transfers between devices  28.7 us (46%)
  starting transfers between devices  24.6 us (39%)
  Pallas kernels  6.91 us (11%)
  between operations  1.5 us (2%)
  local copies, waits for them, and re-layouts  1.15 us (2%)
    ppermute x24, waiting for transfers between devices, swap(): return lax.ppermute(value, axis, [(i, i ^ mask) for i in range(size)])  28.7 us
    ppermute x24, starting transfers between devices, swap(): return lax.ppermute(value, axis, [(i, i ^ mask) for i in range(size)])  24.6 us
    pallas_call x21, Pallas kernels, call(): pl.pallas_call(body, out_shape=outs, in_specs=(specs or [VMEM] * len(args...  6.91 us
  transfers between devices with their start and end apart: 24, of which 13 were waited for; matrix products, arithmetic and copies ran while one was open for 0% of the time, Pallas kernels for 9%

profile of v5, /device:TPU:0, one launch (start us, length us, event | category | flops | bytes accessed | tf_op | source)
XLA Modules:
  0.0 62.8 jit_solution(12264347549809036369)
XLA Ops:
  0.7 3.0 %collective-permute-start = (bf16[128,512]{1,0:T(8,128)(2,1)}, bf16[128,512]{1,0:T(8,128)(2,1)S(1)}, u32[]{:S(2)}, u32[]{:S(2)}) collective-permute-start(bf16[128,512]{1,0:T(8,128)(2,1)} %bitcast.3), channel_id=1, source_target_pairs={{0,8},{8,0},{16,24},{24,16},{1,9},{9,1},{17,25},{25,17},{2,10},{10... | collective-permute-start | bytes 393224 | tf_op jit(solution)/shard_map/ppermute | solution.py:39
  3.7 1.5 %collective-permute-start.1 = (bf16[128,512]{1,0:T(8,128)(2,1)}, bf16[128,512]{1,0:T(8,128)(2,1)S(1)}, u32[]{:S(2)}, u32[]{:S(2)}) collective-permute-start(bf16[128,512]{1,0:T(8,128)(2,1)} %bitcast.4), channel_id=1, source_target_pairs={{0,16},{8,24},{16,0},{24,8},{1,17},{9,25},{17,1},{25,9},{2,18},{10... | collective-permute-start | bytes 393224 | tf_op jit(solution)/shard_map/ppermute | solution.py:39
  5.9 1.1 %copy-done.1 = bf16[1,1,24,128,128]{4,3,2,1,0:T(8,128)(2,1)S(1)} copy-done((bf16[1,1,24,128,128]{4,3,2,1,0:T(8,128)(2,1)S(1)}, bf16[1,1,24,128,128]{4,3,2,1,0:T(8,128)(2,1)}, u32[]{:S(2)}) %copy-start.1) | copy-done | bytes 786456
  7.0 1.2 %shard_map.94 = (bf16[1024,512]{1,0:T(8,128)(2,1)S(1)}, bf16[512,512]{1,0:T(8,128)(2,1)S(1)}, bf16[512,512]{1,0:T(8,128)(2,1)S(1)}) custom-call(bf16[1,1,24,128,128]{4,3,2,1,0:T(8,128)(2,1)S(1)} %copy-done.1, s32[1,1,24]{2,1,0:T(1,128)S(1)} %copy-done.4, s32[1,1,24]{2,1,0:T(1,128)S(1)} %copy-done.5, s32[1,1]{1,0:T(1,128)S(6)} %copy.10.refs_3_), custom_call_target="tpu_custom_call" | custom-call | tf_op jit(solution)/shard_map/pallas_call | solution.py:23
  8.2 3.4 %collective-permute-done.1.refs_3_ = bf16[128,512]{1,0:T(8,128)(2,1)S(1)} collective-permute-done((bf16[128,512]{1,0:T(8,128)(2,1)}, bf16[128,512]{1,0:T(8,128)(2,1)S(1)}, u32[]{:S(2)}, u32[]{:S(2)}) %collective-permute-start.1) | collective-permute-done | bytes 131104 | tf_op jit(solution)/shard_map/ppermute | solution.py:39
  13.6 1.6 %collective-permute-start.6 = (bf16[128,512]{1,0:T(8,128)(2,1)S(1)}, bf16[128,512]{1,0:T(8,128)(2,1)S(1)}, u32[]{:S(2)}, u32[]{:S(2)}) collective-permute-start(bf16[128,512]{1,0:T(8,128)(2,1)S(1)} %get-tuple-element.30), channel_id=1, source_target_pairs={{0,2},{1,3},{2,0},{3,1},{4,6},{5,7},{6,4},{7,5},{8,10},{9,11},{10,... | collective-permute-start | bytes 393224 | tf_op jit(solution)/shard_map/ppermute | solution.py:39
  16.1 3.5 %collective-permute-done.6.refs_1_ = bf16[128,512]{1,0:T(8,128)(2,1)S(1)} collective-permute-done((bf16[128,512]{1,0:T(8,128)(2,1)S(1)}, bf16[128,512]{1,0:T(8,128)(2,1)S(1)}, u32[]{:S(2)}, u32[]{:S(2)}) %collective-permute-start.6) | collective-permute-done | bytes 131104 | tf_op jit(solution)/shard_map/ppermute | solution.py:39
  19.7 2.7 %collective-permute-start.7 = (bf16[128,512]{1,0:T(8,128)(2,1)S(1)}, bf16[128,512]{1,0:T(8,128)(2,1)S(1)}, u32[]{:S(2)}, u32[]{:S(2)}) collective-permute-start(bf16[128,512]{1,0:T(8,128)(2,1)S(1)} %shard_map.101), channel_id=1, source_target_pairs={{0,4},{1,5},{2,6},{3,7},{4,0},{5,1},{6,2},{7,3},{8,12},{9,13},{10,... | collective-permute-start | bytes 393224 | tf_op jit(solution)/shard_map/ppermute | solution.py:39
  22.3 5.8 %collective-permute-done.7.refs_4_ = bf16[128,512]{1,0:T(8,128)(2,1)S(1)} collective-permute-done((bf16[128,512]{1,0:T(8,128)(2,1)S(1)}, bf16[128,512]{1,0:T(8,128)(2,1)S(1)}, u32[]{:S(2)}, u32[]{:S(2)}) %collective-permute-start.7) | collective-permute-done | bytes 131104 | tf_op jit(solution)/shard_map/ppermute | solution.py:39
  29.3 1.3 %collective-permute-done.10.refs_1_ = bf16[256,512]{1,0:T(8,128)(2,1)S(1)} collective-permute-done((bf16[256,512]{1,0:T(8,128)(2,1)S(1)}, bf16[256,512]{1,0:T(8,128)(2,1)S(1)}, u32[]{:S(2)}, u32[]{:S(2)}) %collective-permute-start.10) | collective-permute-done | bytes 262176 | tf_op jit(solution)/shard_map/ppermute | solution.py:39
  30.6 1.3 %collective-permute-start.12 = (bf16[64,512]{1,0:T(8,128)(2,1)S(1)}, bf16[64,512]{1,0:T(8,128)(2,1)S(1)}, u32[]{:S(2)}, u32[]{:S(2)}) collective-permute-start(bf16[64,512]{1,0:T(8,128)(2,1)S(1)} %get-tuple-element.40), channel_id=1, source_target_pairs={{0,8},{8,0},{16,24},{24,16},{1,9},{9,1},{17,25},{25,17},{2,10},{10... | collective-permute-start | bytes 196616 | tf_op jit(solution)/shard_map/ppermute | solution.py:39
  32.8 2.2 %collective-permute-start.8 = (bf16[128,512]{1,0:T(8,128)(2,1)S(1)}, bf16[128,512]{1,0:T(8,128)(2,1)S(1)}, u32[]{:S(2)}, u32[]{:S(2)}) collective-permute-start(bf16[128,512]{1,0:T(8,128)(2,1)S(1)} %get-tuple-element.34.refs_1_), channel_id=1, source_target_pairs={{0,2},{1,3},{2,0},{3,1},{4,6},{5,7},{6,4},{7,5},{8,10},{9,11},{10,... | collective-permute-start | bytes 393224 | tf_op jit(solution)/shard_map/ppermute | solution.py:39
  35.0 1.4 %collective-permute-start.16 = (bf16[64,512]{1,0:T(8,128)(2,1)S(1)}, bf16[64,512]{1,0:T(8,128)(2,1)S(1)}, u32[]{:S(2)}, u32[]{:S(2)}) collective-permute-start(bf16[64,512]{1,0:T(8,128)(2,1)S(1)} %get-tuple-element.43), channel_id=1, source_target_pairs={{0,24},{8,16},{16,8},{24,0},{1,25},{9,17},{17,9},{25,1},{2,26},{10... | collective-permute-start | bytes 196616 | tf_op jit(solution)/shard_map/ppermute | solution.py:39
  36.4 2.4 %collective-permute-done.9.refs_0_ = bf16[128,512]{1,0:T(8,128)(2,1)S(1)} collective-permute-done((bf16[128,512]{1,0:T(8,128)(2,1)S(1)}, bf16[128,512]{1,0:T(8,128)(2,1)S(1)}, u32[]{:S(2)}, u32[]{:S(2)}) %collective-permute-start.9) | collective-permute-done | bytes 131104 | tf_op jit(solution)/shard_map/ppermute | solution.py:39
  39.2 0.9 %collective-permute-done.16.refs_3_ = bf16[64,512]{1,0:T(8,128)(2,1)S(1)} collective-permute-done((bf16[64,512]{1,0:T(8,128)(2,1)S(1)}, bf16[64,512]{1,0:T(8,128)(2,1)S(1)}, u32[]{:S(2)}, u32[]{:S(2)}) %collective-permute-start.16) | collective-permute-done | bytes 65568 | tf_op jit(solution)/shard_map/ppermute | solution.py:39
  40.2 0.8 %collective-permute-start.17 = (bf16[64,512]{1,0:T(8,128)(2,1)S(1)}, bf16[64,512]{1,0:T(8,128)(2,1)S(1)}, u32[]{:S(2)}, u32[]{:S(2)}) collective-permute-start(bf16[64,512]{1,0:T(8,128)(2,1)S(1)} %shard_map.109.refs_0_), channel_id=1, source_target_pairs={{0,2},{1,3},{2,0},{3,1},{4,6},{5,7},{6,4},{7,5},{8,10},{9,11},{10,... | collective-permute-start | bytes 196616 | tf_op jit(solution)/shard_map/ppermute | solution.py:39
  41.8 2.9 %collective-permute-start.19 = (bf16[64,512]{1,0:T(8,128)(2,1)S(1)}, bf16[64,512]{1,0:T(8,128)(2,1)S(1)}, u32[]{:S(2)}, u32[]{:S(2)}) collective-permute-start(bf16[64,512]{1,0:T(8,128)(2,1)S(1)} %shard_map.109.refs_0_), channel_id=1, source_target_pairs={{0,6},{1,7},{2,4},{3,5},{4,2},{5,3},{6,0},{7,1},{8,14},{9,15},{10,... | collective-permute-start | bytes 196616 | tf_op jit(solution)/shard_map/ppermute | solution.py:39
  45.8 1.0 %collective-permute-done.17.refs_1_ = bf16[64,512]{1,0:T(8,128)(2,1)S(1)} collective-permute-done((bf16[64,512]{1,0:T(8,128)(2,1)S(1)}, bf16[64,512]{1,0:T(8,128)(2,1)S(1)}, u32[]{:S(2)}, u32[]{:S(2)}) %collective-permute-start.17) | collective-permute-done | bytes 65568 | tf_op jit(solution)/shard_map/ppermute | solution.py:39
  46.9 1.6 %collective-permute-done.18.refs_2_ = bf16[64,512]{1,0:T(8,128)(2,1)S(1)} collective-permute-done((bf16[64,512]{1,0:T(8,128)(2,1)S(1)}, bf16[64,512]{1,0:T(8,128)(2,1)S(1)}, u32[]{:S(2)}, u32[]{:S(2)}) %collective-permute-start.18) | collective-permute-done | bytes 65568 | tf_op jit(solution)/shard_map/ppermute | solution.py:39
  49.1 1.3 %collective-permute-start.20 = (bf16[192,512]{1,0:T(8,128)(2,1)S(1)}, bf16[192,512]{1,0:T(8,128)(2,1)S(1)}, u32[]{:S(2)}, u32[]{:S(2)}) collective-permute-start(bf16[192,512]{1,0:T(8,128)(2,1)S(1)} %get-tuple-element.45), channel_id=1, source_target_pairs={{0,8},{8,0},{16,24},{24,16},{1,9},{9,1},{17,25},{25,17},{2,10},{10... | collective-permute-start | bytes 589832 | tf_op jit(solution)/shard_map/ppermute | solution.py:39
  51.2 1.4 %collective-permute-start.22 = (bf16[192,512]{1,0:T(8,128)(2,1)S(1)}, bf16[192,512]{1,0:T(8,128)(2,1)S(1)}, u32[]{:S(2)}, u32[]{:S(2)}) collective-permute-start(bf16[192,512]{1,0:T(8,128)(2,1)S(1)} %get-tuple-element.47), channel_id=1, source_target_pairs={{0,24},{8,16},{16,8},{24,0},{1,25},{9,17},{17,9},{25,1},{2,26},{10... | collective-permute-start | bytes 589832 | tf_op jit(solution)/shard_map/ppermute | solution.py:39
  53.3 3.4 %collective-permute-done.20.refs_1_ = bf16[192,512]{1,0:T(8,128)(2,1)S(1)} collective-permute-done((bf16[192,512]{1,0:T(8,128)(2,1)S(1)}, bf16[192,512]{1,0:T(8,128)(2,1)S(1)}, u32[]{:S(2)}, u32[]{:S(2)}) %collective-permute-start.20) | collective-permute-done | bytes 196640 | tf_op jit(solution)/shard_map/ppermute | solution.py:39
  56.7 3.4 %collective-permute-done.21.refs_2_ = bf16[192,512]{1,0:T(8,128)(2,1)S(1)} collective-permute-done((bf16[192,512]{1,0:T(8,128)(2,1)S(1)}, bf16[192,512]{1,0:T(8,128)(2,1)S(1)}, u32[]{:S(2)}, u32[]{:S(2)}) %collective-permute-start.21) | collective-permute-done | bytes 196640 | tf_op jit(solution)/shard_map/ppermute | solution.py:39
  61.8 1.0 %shard_map.114 = f32[512,512]{1,0:T(8,128)} custom-call(bf16[256,512]{1,0:T(8,128)(2,1)S(1)} %shard_map.112.refs_4_.refs_0_, bf16[256,512]{1,0:T(8,128)(2,1)S(1)} %collective-permute-done.23.refs_1_), custom_call_target="tpu_custom_call" | custom-call | tf_op jit(solution)/shard_map/pallas_call | solution.py:23
  (57 shorter events, 11.0 us)
Async XLA Ops:
  0.7 7.5 %collective-permute-start = (bf16[128,512]{1,0:T(8,128)(2,1)}, bf16[128,512]{1,0:T(8,128)(2,1)S(1)}, u32[]{:S(2)}, u32[]{:S(2)}) collective-permute-start(bf16[128,512]{1,0:T(8,128)(2,1)} %bitcast.3), channel_id=1, source_target_pairs={{0,8},{8,0},{16,24},{24,16},{1,9},{9,1},{17,25},{25,17},{2,10},{10... | collective-permute-start | bytes 393224 | tf_op jit(solution)/shard_map/ppermute | solution.py:39
  3.7 8.0 %collective-permute-start.1 = (bf16[128,512]{1,0:T(8,128)(2,1)}, bf16[128,512]{1,0:T(8,128)(2,1)S(1)}, u32[]{:S(2)}, u32[]{:S(2)}) collective-permute-start(bf16[128,512]{1,0:T(8,128)(2,1)} %bitcast.4), channel_id=1, source_target_pairs={{0,16},{8,24},{16,0},{24,8},{1,17},{9,25},{17,1},{25,9},{2,18},{10... | collective-permute-start | bytes 393224 | tf_op jit(solution)/shard_map/ppermute | solution.py:39
  5.2 6.5 %collective-permute-start.2 = (bf16[128,512]{1,0:T(8,128)(2,1)}, bf16[128,512]{1,0:T(8,128)(2,1)S(1)}, u32[]{:S(2)}, u32[]{:S(2)}) collective-permute-start(bf16[128,512]{1,0:T(8,128)(2,1)} %bitcast.5), channel_id=1, source_target_pairs={{0,24},{8,16},{16,8},{24,0},{1,25},{9,17},{17,9},{25,1},{2,26},{10... | collective-permute-start | bytes 393224 | tf_op jit(solution)/shard_map/ppermute | solution.py:39
  12.0 1.6 %collective-permute-start.4 = (bf16[256,512]{1,0:T(8,128)(2,1)S(1)}, bf16[256,512]{1,0:T(8,128)(2,1)S(1)}, u32[]{:S(2)}, u32[]{:S(2)}) collective-permute-start(bf16[256,512]{1,0:T(8,128)(2,1)S(1)} %shard_map.99), channel_id=1, source_target_pairs={{0,1},{1,0},{2,3},{3,2},{4,5},{5,4},{6,7},{7,6},{8,9},{9,8},{10,11... | collective-permute-start | bytes 786440 | tf_op jit(solution)/shard_map/ppermute | solution.py:39
  12.3 3.8 %collective-permute-start.3 = (bf16[256,512]{1,0:T(8,128)(2,1)S(1)}, bf16[256,512]{1,0:T(8,128)(2,1)S(1)}, u32[]{:S(2)}, u32[]{:S(2)}) collective-permute-start(bf16[256,512]{1,0:T(8,128)(2,1)S(1)} %shard_map.96), channel_id=1, source_target_pairs={{0,1},{1,0},{2,3},{3,2},{4,5},{5,4},{6,7},{7,6},{8,9},{9,8},{10,11... | collective-permute-start | bytes 786440 | tf_op jit(solution)/shard_map/ppermute | solution.py:39
  13.6 6.0 %collective-permute-start.6 = (bf16[128,512]{1,0:T(8,128)(2,1)S(1)}, bf16[128,512]{1,0:T(8,128)(2,1)S(1)}, u32[]{:S(2)}, u32[]{:S(2)}) collective-permute-start(bf16[128,512]{1,0:T(8,128)(2,1)S(1)} %get-tuple-element.30), channel_id=1, source_target_pairs={{0,2},{1,3},{2,0},{3,1},{4,6},{5,7},{6,4},{7,5},{8,10},{9,11},{10,... | collective-permute-start | bytes 393224 | tf_op jit(solution)/shard_map/ppermute | solution.py:39
  15.3 14.0 %collective-permute-start.11 = (bf16[512,512]{1,0:T(8,128)(2,1)S(1)}, bf16[512,512]{1,0:T(8,128)(2,1)S(1)}, u32[]{:S(2)}, u32[]{:S(2)}) collective-permute-start(bf16[512,512]{1,0:T(8,128)(2,1)S(1)} %get-tuple-element.39), channel_id=1, source_target_pairs={{0,1},{1,0},{2,3},{3,2},{4,5},{5,4},{6,7},{7,6},{8,9},{9,8},{10,11... | collective-permute-start | bytes 1572872 | tf_op jit(solution)/shard_map/ppermute | solution.py:39
  15.6 6.8 %collective-permute-start.5 = (bf16[128,512]{1,0:T(8,128)(2,1)S(1)}, bf16[128,512]{1,0:T(8,128)(2,1)S(1)}, u32[]{:S(2)}, u32[]{:S(2)}) collective-permute-start(bf16[128,512]{1,0:T(8,128)(2,1)S(1)} %get-tuple-element.28), channel_id=1, source_target_pairs={{0,2},{1,3},{2,0},{3,1},{4,6},{5,7},{6,4},{7,5},{8,10},{9,11},{10,... | collective-permute-start | bytes 393224 | tf_op jit(solution)/shard_map/ppermute | solution.py:39
  19.7 8.5 %collective-permute-start.7 = (bf16[128,512]{1,0:T(8,128)(2,1)S(1)}, bf16[128,512]{1,0:T(8,128)(2,1)S(1)}, u32[]{:S(2)}, u32[]{:S(2)}) collective-permute-start(bf16[128,512]{1,0:T(8,128)(2,1)S(1)} %shard_map.101), channel_id=1, source_target_pairs={{0,4},{1,5},{2,6},{3,7},{4,0},{5,1},{6,2},{7,3},{8,12},{9,13},{10,... | collective-permute-start | bytes 393224 | tf_op jit(solution)/shard_map/ppermute | solution.py:39
  29.0 1.6 %collective-permute-start.10 = (bf16[256,512]{1,0:T(8,128)(2,1)S(1)}, bf16[256,512]{1,0:T(8,128)(2,1)S(1)}, u32[]{:S(2)}, u32[]{:S(2)}) collective-permute-start(bf16[256,512]{1,0:T(8,128)(2,1)S(1)} %get-tuple-element.38), channel_id=1, source_target_pairs={{0,1},{1,0},{2,3},{3,2},{4,5},{5,4},{6,7},{7,6},{8,9},{9,8},{10,11... | collective-permute-start | bytes 786440 | tf_op jit(solution)/shard_map/ppermute | solution.py:39
  29.1 9.7 %collective-permute-start.9 = (bf16[128,512]{1,0:T(8,128)(2,1)S(1)}, bf16[128,512]{1,0:T(8,128)(2,1)S(1)}, u32[]{:S(2)}, u32[]{:S(2)}) collective-permute-start(bf16[128,512]{1,0:T(8,128)(2,1)S(1)} %get-tuple-element.34.refs_1_), channel_id=1, source_target_pairs={{0,4},{1,5},{2,6},{3,7},{4,0},{5,1},{6,2},{7,3},{8,12},{9,13},{10,... | collective-permute-start | bytes 393224 | tf_op jit(solution)/shard_map/ppermute | solution.py:39
  30.6 8.2 %collective-permute-start.12 = (bf16[64,512]{1,0:T(8,128)(2,1)S(1)}, bf16[64,512]{1,0:T(8,128)(2,1)S(1)}, u32[]{:S(2)}, u32[]{:S(2)}) collective-permute-start(bf16[64,512]{1,0:T(8,128)(2,1)S(1)} %get-tuple-element.40), channel_id=1, source_target_pairs={{0,8},{8,0},{16,24},{24,16},{1,9},{9,1},{17,25},{25,17},{2,10},{10... | collective-permute-start | bytes 196616 | tf_op jit(solution)/shard_map/ppermute | solution.py:39
  31.9 6.9 %collective-permute-start.13 = (bf16[64,512]{1,0:T(8,128)(2,1)S(1)}, bf16[64,512]{1,0:T(8,128)(2,1)S(1)}, u32[]{:S(2)}, u32[]{:S(2)}) collective-permute-start(bf16[64,512]{1,0:T(8,128)(2,1)S(1)} %get-tuple-element.41), channel_id=1, source_target_pairs={{0,16},{8,24},{16,0},{24,8},{1,17},{9,25},{17,1},{25,9},{2,18},{10... | collective-permute-start | bytes 196616 | tf_op jit(solution)/shard_map/ppermute | solution.py:39
  32.8 11.9 %collective-permute-start.8 = (bf16[128,512]{1,0:T(8,128)(2,1)S(1)}, bf16[128,512]{1,0:T(8,128)(2,1)S(1)}, u32[]{:S(2)}, u32[]{:S(2)}) collective-permute-start(bf16[128,512]{1,0:T(8,128)(2,1)S(1)} %get-tuple-element.34.refs_1_), channel_id=1, source_target_pairs={{0,2},{1,3},{2,0},{3,1},{4,6},{5,7},{6,4},{7,5},{8,10},{9,11},{10,... | collective-permute-start | bytes 393224 | tf_op jit(solution)/shard_map/ppermute | solution.py:39
  35.0 5.2 %collective-permute-start.16 = (bf16[64,512]{1,0:T(8,128)(2,1)S(1)}, bf16[64,512]{1,0:T(8,128)(2,1)S(1)}, u32[]{:S(2)}, u32[]{:S(2)}) collective-permute-start(bf16[64,512]{1,0:T(8,128)(2,1)S(1)} %get-tuple-element.43), channel_id=1, source_target_pairs={{0,24},{8,16},{16,8},{24,0},{1,25},{9,17},{17,9},{25,1},{2,26},{10... | collective-permute-start | bytes 196616 | tf_op jit(solution)/shard_map/ppermute | solution.py:39
  38.8 6.5 %collective-permute-start.14 = (bf16[128,512]{1,0:T(8,128)(2,1)S(1)}, bf16[128,512]{1,0:T(8,128)(2,1)S(1)}, u32[]{:S(2)}, u32[]{:S(2)}) collective-permute-start(bf16[128,512]{1,0:T(8,128)(2,1)S(1)} %shard_map.106.refs_3_), channel_id=1, source_target_pairs={{0,2},{1,3},{2,0},{3,1},{4,6},{5,7},{6,4},{7,5},{8,10},{9,11},{10,... | collective-permute-start | bytes 393224 | tf_op jit(solution)/shard_map/ppermute | solution.py:39
  40.2 6.7 %collective-permute-start.17 = (bf16[64,512]{1,0:T(8,128)(2,1)S(1)}, bf16[64,512]{1,0:T(8,128)(2,1)S(1)}, u32[]{:S(2)}, u32[]{:S(2)}) collective-permute-start(bf16[64,512]{1,0:T(8,128)(2,1)S(1)} %shard_map.109.refs_0_), channel_id=1, source_target_pairs={{0,2},{1,3},{2,0},{3,1},{4,6},{5,7},{6,4},{7,5},{8,10},{9,11},{10,... | collective-permute-start | bytes 196616 | tf_op jit(solution)/shard_map/ppermute | solution.py:39
  41.0 7.5 %collective-permute-start.18 = (bf16[64,512]{1,0:T(8,128)(2,1)S(1)}, bf16[64,512]{1,0:T(8,128)(2,1)S(1)}, u32[]{:S(2)}, u32[]{:S(2)}) collective-permute-start(bf16[64,512]{1,0:T(8,128)(2,1)S(1)} %shard_map.109.refs_0_), channel_id=1, source_target_pairs={{0,4},{1,5},{2,6},{3,7},{4,0},{5,1},{6,2},{7,3},{8,12},{9,13},{10,... | collective-permute-start | bytes 196616 | tf_op jit(solution)/shard_map/ppermute | solution.py:39
  41.8 6.7 %collective-permute-start.19 = (bf16[64,512]{1,0:T(8,128)(2,1)S(1)}, bf16[64,512]{1,0:T(8,128)(2,1)S(1)}, u32[]{:S(2)}, u32[]{:S(2)}) collective-permute-start(bf16[64,512]{1,0:T(8,128)(2,1)S(1)} %shard_map.109.refs_0_), channel_id=1, source_target_pairs={{0,6},{1,7},{2,4},{3,5},{4,2},{5,3},{6,0},{7,1},{8,14},{9,15},{10,... | collective-permute-start | bytes 196616 | tf_op jit(solution)/shard_map/ppermute | solution.py:39
  45.7 3.2 %collective-permute-start.15 = (bf16[512,512]{1,0:T(8,128)(2,1)S(1)}, bf16[512,512]{1,0:T(8,128)(2,1)S(1)}, u32[]{:S(2)}, u32[]{:S(2)}) collective-permute-start(bf16[512,512]{1,0:T(8,128)(2,1)S(1)} %shard_map.108), channel_id=1, source_target_pairs={{0,1},{1,0},{2,3},{3,2},{4,5},{5,4},{6,7},{7,6},{8,9},{9,8},{10,11... | collective-permute-start | bytes 1572872 | tf_op jit(solution)/shard_map/ppermute | solution.py:39
  49.1 7.7 %collective-permute-start.20 = (bf16[192,512]{1,0:T(8,128)(2,1)S(1)}, bf16[192,512]{1,0:T(8,128)(2,1)S(1)}, u32[]{:S(2)}, u32[]{:S(2)}) collective-permute-start(bf16[192,512]{1,0:T(8,128)(2,1)S(1)} %get-tuple-element.45), channel_id=1, source_target_pairs={{0,8},{8,0},{16,24},{24,16},{1,9},{9,1},{17,25},{25,17},{2,10},{10... | collective-permute-start | bytes 589832 | tf_op jit(solution)/shard_map/ppermute | solution.py:39
  50.4 9.8 %collective-permute-start.21 = (bf16[192,512]{1,0:T(8,128)(2,1)S(1)}, bf16[192,512]{1,0:T(8,128)(2,1)S(1)}, u32[]{:S(2)}, u32[]{:S(2)}) collective-permute-start(bf16[192,512]{1,0:T(8,128)(2,1)S(1)} %get-tuple-element.46), channel_id=1, source_target_pairs={{0,16},{8,24},{16,0},{24,8},{1,17},{9,25},{17,1},{25,9},{2,18},{10... | collective-permute-start | bytes 589832 | tf_op jit(solution)/shard_map/ppermute | solution.py:39
  51.2 9.0 %collective-permute-start.22 = (bf16[192,512]{1,0:T(8,128)(2,1)S(1)}, bf16[192,512]{1,0:T(8,128)(2,1)S(1)}, u32[]{:S(2)}, u32[]{:S(2)}) collective-permute-start(bf16[192,512]{1,0:T(8,128)(2,1)S(1)} %get-tuple-element.47), channel_id=1, source_target_pairs={{0,24},{8,16},{16,8},{24,0},{1,25},{9,17},{17,9},{25,1},{2,26},{10... | collective-permute-start | bytes 589832 | tf_op jit(solution)/shard_map/ppermute | solution.py:39
  60.2 1.6 %collective-permute-start.23 = (bf16[256,512]{1,0:T(8,128)(2,1)S(1)}, bf16[256,512]{1,0:T(8,128)(2,1)S(1)}, u32[]{:S(2)}, u32[]{:S(2)}) collective-permute-start(bf16[256,512]{1,0:T(8,128)(2,1)S(1)} %shard_map.112.refs_4_.refs_0_), channel_id=1, source_target_pairs={{0,1},{1,0},{2,3},{3,2},{4,5},{5,4},{6,7},{7,6},{8,9},{9,8},{10,11... | collective-permute-start | bytes 786440 | tf_op jit(solution)/shard_map/ppermute | solution.py:39
  (6 other events, 37.3 us)

commit v6 on v5

--- a/solution.py
+++ b/solution.py
@@ -118,23 +118,23 @@
     out[...] = (hidden[...] * jax.nn.sigmoid(hidden[...])).astype(BF16)
 
 
-def weight_term(n_row, scale, summed, hidden_grad, mine, other, whole):
+def weight_half(n_row, flip, scale, summed, hidden_grad, out, whole):
+    me_row, side = lax.axis_index("row"), (lax.axis_index("col") & 1) ^ flip
+    half = out.shape[0]
+    at = pl.multiple_of(side * half, half)
     whole[...] = (
         lax.dot_general(
-            summed[...], hidden_grad[...], (((0,), (0,)), ((), ())), preferred_element_type=F32
+            summed[:, pl.ds(at, half)],
+            hidden_grad[...],
+            (((0,), (0,)), ((), ())),
+            preferred_element_type=F32,
         )
         * scale
     )
-    me_row, core = lax.axis_index("row"), lax.axis_index("col") & 1
-    half = mine.shape[0]
     piece = half // n_row
     for k in range(n_row):
-        inside = (me_row ^ k) * piece
-        part = pl.ds(k * piece, piece)
-        at = pl.multiple_of(core * half + inside, piece)
-        mine[part, :] = whole[pl.ds(at, piece), :]
-        at = pl.multiple_of((1 - core) * half + inside, piece)
-        other[part, :] = whole[pl.ds(at, piece), :].astype(BF16)
+        rows = pl.ds(pl.multiple_of((me_row ^ k) * piece, piece), piece)
+        out[k * piece : (k + 1) * piece, :] = whole[rows, :].astype(out.dtype)
 
 
 def backward(dense_t, *refs):
@@ -226,13 +226,21 @@
         (weight, cotangent, *terms),
     )
     piece = width // 2 // n_row
-    mine_w, other_w = call(
-        functools.partial(weight_term, n_row, (n_row * n_col * TILE) ** -0.5),
-        [like(width // 2, width, dtype=F32), like(width // 2, width)],
+    scale = (n_row * n_col * TILE) ** -0.5
+    scratch = [pltpu.VMEM((width // 2, width), F32)]
+    (other_w,) = call(
+        functools.partial(weight_half, n_row, 1, scale),
+        [like(width // 2, width)],
         (summed, hidden_grad),
-        scratch=[pltpu.VMEM((width, width), F32)],
+        scratch=scratch,
     )
     other_w = core_swap(other_w)
+    (mine_w,) = call(
+        functools.partial(weight_half, n_row, 0, scale),
+        [like(width // 2, width, dtype=F32)],
+        (summed, hidden_grad),
+        scratch=scratch,
+    )
     parts_w = call(add_split, [like(piece, width)] * n_row, (mine_w, other_w), after=(other_t,))
     terms_w = [parts_w[0]] + [row_swap(parts_w[k], k) for k in range(1, n_row)]
     same = [grad_rows] + [None] * (n_z - 1)

time: 63 us -> 62.9 us (level)
  waiting for transfers between devices: 28.7 us -> 27.2 us
  Pallas kernels: 6.91 us -> 7.63 us
    ppermute x24, waiting for transfers between devices: 28.7 us -> 27.2 us  [swap(): return lax.ppermute(value, axis, [(i, i ^ mask) for i in range(size)])]
    pallas_call x21 -> x22, Pallas kernels: 6.91 us -> 7.63 us  [call(): pl.pallas_call(body, out_shape=outs, in_specs=(specs or [VMEM] * len(args...]
    ppermute x24, starting transfers between devices: 24.6 us -> 25.2 us  [swap(): return lax.ppermute(value, axis, [(i, i ^ mask) for i in range(size)])]
  transfers between devices with their start and end apart: 24 -> 24, of which waited for: 13 -> 13; matrix products, arithmetic and copies ran while one was open for 0% -> 0% of each run, Pallas kernels for 9% -> 10%
where the time goes in v6:
time: 62.9 us; the launch traced here: 62.7 us
  waiting for transfers between devices  27.2 us (43%)
  starting transfers between devices  25.2 us (40%)
  Pallas kernels  7.63 us (12%)
  between operations  1.52 us (2%)
  local copies, waits for them, and re-layouts  1.15 us (2%)
    ppermute x24, waiting for transfers between devices, swap(): return lax.ppermute(value, axis, [(i, i ^ mask) for i in range(size)])  27.2 us
    ppermute x24, starting transfers between devices, swap(): return lax.ppermute(value, axis, [(i, i ^ mask) for i in range(size)])  25.2 us
    pallas_call x22, Pallas kernels, call(): pl.pallas_call(body, out_shape=outs, in_specs=(specs or [VMEM] * len(args...  7.63 us
  transfers between devices with their start and end apart: 24, of which 13 were waited for; matrix products, arithmetic and copies ran while one was open for 0% of the time, Pallas kernels for 10%

profile of v6, /device:TPU:0, one launch (start us, length us, event | category | flops | bytes accessed | tf_op | source)
XLA Modules:
  0.0 62.7 jit_solution(16479275357048569601)
XLA Ops:
  0.7 3.0 %collective-permute-start = (bf16[128,512]{1,0:T(8,128)(2,1)}, bf16[128,512]{1,0:T(8,128)(2,1)S(1)}, u32[]{:S(2)}, u32[]{:S(2)}) collective-permute-start(bf16[128,512]{1,0:T(8,128)(2,1)} %bitcast.3), channel_id=1, source_target_pairs={{0,8},{8,0},{16,24},{24,16},{1,9},{9,1},{17,25},{25,17},{2,10},{10... | collective-permute-start | bytes 393224 | tf_op jit(solution)/shard_map/ppermute | solution.py:39
  3.7 1.5 %collective-permute-start.1 = (bf16[128,512]{1,0:T(8,128)(2,1)}, bf16[128,512]{1,0:T(8,128)(2,1)S(1)}, u32[]{:S(2)}, u32[]{:S(2)}) collective-permute-start(bf16[128,512]{1,0:T(8,128)(2,1)} %bitcast.4), channel_id=1, source_target_pairs={{0,16},{8,24},{16,0},{24,8},{1,17},{9,25},{17,1},{25,9},{2,18},{10... | collective-permute-start | bytes 393224 | tf_op jit(solution)/shard_map/ppermute | solution.py:39
  5.9 1.1 %copy-done.1 = bf16[1,1,24,128,128]{4,3,2,1,0:T(8,128)(2,1)S(1)} copy-done((bf16[1,1,24,128,128]{4,3,2,1,0:T(8,128)(2,1)S(1)}, bf16[1,1,24,128,128]{4,3,2,1,0:T(8,128)(2,1)}, u32[]{:S(2)}) %copy-start.1) | copy-done | bytes 786456
  7.0 1.7 %shard_map.94 = (bf16[1024,512]{1,0:T(8,128)(2,1)S(1)}, bf16[512,512]{1,0:T(8,128)(2,1)S(1)}, bf16[512,512]{1,0:T(8,128)(2,1)S(1)}) custom-call(bf16[1,1,24,128,128]{4,3,2,1,0:T(8,128)(2,1)S(1)} %copy-done.1, s32[1,1,24]{2,1,0:T(1,128)S(1)} %copy-done.4, s32[1,1,24]{2,1,0:T(1,128)S(1)} %copy-done.5, s32[1,1]{1,0:T(1,128)S(6)} %copy.10.refs_3_), custom_call_target="tpu_custom_call" | custom-call | tf_op jit(solution)/shard_map/pallas_call | solution.py:23
  8.7 2.9 %collective-permute-done.1.refs_3_ = bf16[128,512]{1,0:T(8,128)(2,1)S(1)} collective-permute-done((bf16[128,512]{1,0:T(8,128)(2,1)}, bf16[128,512]{1,0:T(8,128)(2,1)S(1)}, u32[]{:S(2)}, u32[]{:S(2)}) %collective-permute-start.1) | collective-permute-done | bytes 131104 | tf_op jit(solution)/shard_map/ppermute | solution.py:39
  13.6 1.6 %collective-permute-start.6 = (bf16[128,512]{1,0:T(8,128)(2,1)S(1)}, bf16[128,512]{1,0:T(8,128)(2,1)S(1)}, u32[]{:S(2)}, u32[]{:S(2)}) collective-permute-start(bf16[128,512]{1,0:T(8,128)(2,1)S(1)} %get-tuple-element.28), channel_id=1, source_target_pairs={{0,2},{1,3},{2,0},{3,1},{4,6},{5,7},{6,4},{7,5},{8,10},{9,11},{10,... | collective-permute-start | bytes 393224 | tf_op jit(solution)/shard_map/ppermute | solution.py:39
  16.1 3.5 %collective-permute-done.6.refs_1_ = bf16[128,512]{1,0:T(8,128)(2,1)S(1)} collective-permute-done((bf16[128,512]{1,0:T(8,128)(2,1)S(1)}, bf16[128,512]{1,0:T(8,128)(2,1)S(1)}, u32[]{:S(2)}, u32[]{:S(2)}) %collective-permute-start.6) | collective-permute-done | bytes 131104 | tf_op jit(solution)/shard_map/ppermute | solution.py:39
  19.7 2.7 %collective-permute-start.7 = (bf16[128,512]{1,0:T(8,128)(2,1)S(1)}, bf16[128,512]{1,0:T(8,128)(2,1)S(1)}, u32[]{:S(2)}, u32[]{:S(2)}) collective-permute-start(bf16[128,512]{1,0:T(8,128)(2,1)S(1)} %shard_map.101), channel_id=1, source_target_pairs={{0,4},{1,5},{2,6},{3,7},{4,0},{5,1},{6,2},{7,3},{8,12},{9,13},{10,... | collective-permute-start | bytes 393224 | tf_op jit(solution)/shard_map/ppermute | solution.py:39
  22.3 5.8 %collective-permute-done.7.refs_4_ = bf16[128,512]{1,0:T(8,128)(2,1)S(1)} collective-permute-done((bf16[128,512]{1,0:T(8,128)(2,1)S(1)}, bf16[128,512]{1,0:T(8,128)(2,1)S(1)}, u32[]{:S(2)}, u32[]{:S(2)}) %collective-permute-start.7) | collective-permute-done | bytes 131104 | tf_op jit(solution)/shard_map/ppermute | solution.py:39
  29.5 1.0 %collective-permute-done.10.refs_1_ = bf16[256,512]{1,0:T(8,128)(2,1)S(1)} collective-permute-done((bf16[256,512]{1,0:T(8,128)(2,1)S(1)}, bf16[256,512]{1,0:T(8,128)(2,1)S(1)}, u32[]{:S(2)}, u32[]{:S(2)}) %collective-permute-start.10) | collective-permute-done | bytes 262176 | tf_op jit(solution)/shard_map/ppermute | solution.py:39
  30.6 1.3 %collective-permute-start.12 = (bf16[64,512]{1,0:T(8,128)(2,1)S(1)}, bf16[64,512]{1,0:T(8,128)(2,1)S(1)}, u32[]{:S(2)}, u32[]{:S(2)}) collective-permute-start(bf16[64,512]{1,0:T(8,128)(2,1)S(1)} %get-tuple-element.36), channel_id=1, source_target_pairs={{0,8},{8,0},{16,24},{24,16},{1,9},{9,1},{17,25},{25,17},{2,10},{10... | collective-permute-start | bytes 196616 | tf_op jit(solution)/shard_map/ppermute | solution.py:39
  32.7 2.5 %collective-permute-start.8 = (bf16[128,512]{1,0:T(8,128)(2,1)S(1)}, bf16[128,512]{1,0:T(8,128)(2,1)S(1)}, u32[]{:S(2)}, u32[]{:S(2)}) collective-permute-start(bf16[128,512]{1,0:T(8,128)(2,1)S(1)} %get-tuple-element.32.refs_1_), channel_id=1, source_target_pairs={{0,2},{1,3},{2,0},{3,1},{4,6},{5,7},{6,4},{7,5},{8,10},{9,11},{10,... | collective-permute-start | bytes 393224 | tf_op jit(solution)/shard_map/ppermute | solution.py:39
  35.2 1.4 %collective-permute-start.16 = (bf16[64,512]{1,0:T(8,128)(2,1)S(1)}, bf16[64,512]{1,0:T(8,128)(2,1)S(1)}, u32[]{:S(2)}, u32[]{:S(2)}) collective-permute-start(bf16[64,512]{1,0:T(8,128)(2,1)S(1)} %get-tuple-element.39), channel_id=1, source_target_pairs={{0,24},{8,16},{16,8},{24,0},{1,25},{9,17},{17,9},{25,1},{2,26},{10... | collective-permute-start | bytes 196616 | tf_op jit(solution)/shard_map/ppermute | solution.py:39
  36.7 2.1 %collective-permute-done.9.refs_0_ = bf16[128,512]{1,0:T(8,128)(2,1)S(1)} collective-permute-done((bf16[128,512]{1,0:T(8,128)(2,1)S(1)}, bf16[128,512]{1,0:T(8,128)(2,1)S(1)}, u32[]{:S(2)}, u32[]{:S(2)}) %collective-permute-start.9) | collective-permute-done | bytes 131104 | tf_op jit(solution)/shard_map/ppermute | solution.py:39
  39.4 1.0 %collective-permute-done.16.refs_3_ = bf16[64,512]{1,0:T(8,128)(2,1)S(1)} collective-permute-done((bf16[64,512]{1,0:T(8,128)(2,1)S(1)}, bf16[64,512]{1,0:T(8,128)(2,1)S(1)}, u32[]{:S(2)}, u32[]{:S(2)}) %collective-permute-start.16) | collective-permute-done | bytes 65568 | tf_op jit(solution)/shard_map/ppermute | solution.py:39
  40.9 0.8 %collective-permute-start.18 = (bf16[64,512]{1,0:T(8,128)(2,1)S(1)}, bf16[64,512]{1,0:T(8,128)(2,1)S(1)}, u32[]{:S(2)}, u32[]{:S(2)}) collective-permute-start(bf16[64,512]{1,0:T(8,128)(2,1)S(1)} %shard_map.110.refs_0_), channel_id=1, source_target_pairs={{0,4},{1,5},{2,6},{3,7},{4,0},{5,1},{6,2},{7,3},{8,12},{9,13},{10,... | collective-permute-start | bytes 196616 | tf_op jit(solution)/shard_map/ppermute | solution.py:39
  41.8 3.1 %collective-permute-start.19 = (bf16[64,512]{1,0:T(8,128)(2,1)S(1)}, bf16[64,512]{1,0:T(8,128)(2,1)S(1)}, u32[]{:S(2)}, u32[]{:S(2)}) collective-permute-start(bf16[64,512]{1,0:T(8,128)(2,1)S(1)} %shard_map.110.refs_0_), channel_id=1, source_target_pairs={{0,6},{1,7},{2,4},{3,5},{4,2},{5,3},{6,0},{7,1},{8,14},{9,15},{10,... | collective-permute-start | bytes 196616 | tf_op jit(solution)/shard_map/ppermute | solution.py:39
  45.7 1.0 %collective-permute-done.17.refs_1_ = bf16[64,512]{1,0:T(8,128)(2,1)S(1)} collective-permute-done((bf16[64,512]{1,0:T(8,128)(2,1)S(1)}, bf16[64,512]{1,0:T(8,128)(2,1)S(1)}, u32[]{:S(2)}, u32[]{:S(2)}) %collective-permute-start.17) | collective-permute-done | bytes 65568 | tf_op jit(solution)/shard_map/ppermute | solution.py:39
  46.8 1.6 %collective-permute-done.18.refs_2_ = bf16[64,512]{1,0:T(8,128)(2,1)S(1)} collective-permute-done((bf16[64,512]{1,0:T(8,128)(2,1)S(1)}, bf16[64,512]{1,0:T(8,128)(2,1)S(1)}, u32[]{:S(2)}, u32[]{:S(2)}) %collective-permute-start.18) | collective-permute-done | bytes 65568 | tf_op jit(solution)/shard_map/ppermute | solution.py:39
  49.0 1.3 %collective-permute-start.20 = (bf16[192,512]{1,0:T(8,128)(2,1)S(1)}, bf16[192,512]{1,0:T(8,128)(2,1)S(1)}, u32[]{:S(2)}, u32[]{:S(2)}) collective-permute-start(bf16[192,512]{1,0:T(8,128)(2,1)S(1)} %get-tuple-element.41), channel_id=1, source_target_pairs={{0,8},{8,0},{16,24},{24,16},{1,9},{9,1},{17,25},{25,17},{2,10},{10... | collective-permute-start | bytes 589832 | tf_op jit(solution)/shard_map/ppermute | solution.py:39
  51.1 1.4 %collective-permute-start.22 = (bf16[192,512]{1,0:T(8,128)(2,1)S(1)}, bf16[192,512]{1,0:T(8,128)(2,1)S(1)}, u32[]{:S(2)}, u32[]{:S(2)}) collective-permute-start(bf16[192,512]{1,0:T(8,128)(2,1)S(1)} %get-tuple-element.43), channel_id=1, source_target_pairs={{0,24},{8,16},{16,8},{24,0},{1,25},{9,17},{17,9},{25,1},{2,26},{10... | collective-permute-start | bytes 589832 | tf_op jit(solution)/shard_map/ppermute | solution.py:39
  53.2 3.4 %collective-permute-done.20.refs_1_ = bf16[192,512]{1,0:T(8,128)(2,1)S(1)} collective-permute-done((bf16[192,512]{1,0:T(8,128)(2,1)S(1)}, bf16[192,512]{1,0:T(8,128)(2,1)S(1)}, u32[]{:S(2)}, u32[]{:S(2)}) %collective-permute-start.20) | collective-permute-done | bytes 196640 | tf_op jit(solution)/shard_map/ppermute | solution.py:39
  56.7 3.4 %collective-permute-done.21.refs_2_ = bf16[192,512]{1,0:T(8,128)(2,1)S(1)} collective-permute-done((bf16[192,512]{1,0:T(8,128)(2,1)S(1)}, bf16[192,512]{1,0:T(8,128)(2,1)S(1)}, u32[]{:S(2)}, u32[]{:S(2)}) %collective-permute-start.21) | collective-permute-done | bytes 196640 | tf_op jit(solution)/shard_map/ppermute | solution.py:39
  61.7 1.0 %shard_map.115 = f32[512,512]{1,0:T(8,128)} custom-call(bf16[256,512]{1,0:T(8,128)(2,1)S(1)} %shard_map.113.refs_4_.refs_0_, bf16[256,512]{1,0:T(8,128)(2,1)S(1)} %collective-permute-done.23.refs_1_), custom_call_target="tpu_custom_call" | custom-call | tf_op jit(solution)/shard_map/pallas_call | solution.py:23
  (58 shorter events, 10.9 us)
Async XLA Ops:
  0.7 8.0 %collective-permute-start = (bf16[128,512]{1,0:T(8,128)(2,1)}, bf16[128,512]{1,0:T(8,128)(2,1)S(1)}, u32[]{:S(2)}, u32[]{:S(2)}) collective-permute-start(bf16[128,512]{1,0:T(8,128)(2,1)} %bitcast.3), channel_id=1, source_target_pairs={{0,8},{8,0},{16,24},{24,16},{1,9},{9,1},{17,25},{25,17},{2,10},{10... | collective-permute-start | bytes 393224 | tf_op jit(solution)/shard_map/ppermute | solution.py:39
  3.7 8.0 %collective-permute-start.1 = (bf16[128,512]{1,0:T(8,128)(2,1)}, bf16[128,512]{1,0:T(8,128)(2,1)S(1)}, u32[]{:S(2)}, u32[]{:S(2)}) collective-permute-start(bf16[128,512]{1,0:T(8,128)(2,1)} %bitcast.4), channel_id=1, source_target_pairs={{0,16},{8,24},{16,0},{24,8},{1,17},{9,25},{17,1},{25,9},{2,18},{10... | collective-permute-start | bytes 393224 | tf_op jit(solution)/shard_map/ppermute | solution.py:39
  5.2 6.5 %collective-permute-start.2 = (bf16[128,512]{1,0:T(8,128)(2,1)}, bf16[128,512]{1,0:T(8,128)(2,1)S(1)}, u32[]{:S(2)}, u32[]{:S(2)}) collective-permute-start(bf16[128,512]{1,0:T(8,128)(2,1)} %bitcast.5), channel_id=1, source_target_pairs={{0,24},{8,16},{16,8},{24,0},{1,25},{9,17},{17,9},{25,1},{2,26},{10... | collective-permute-start | bytes 393224 | tf_op jit(solution)/shard_map/ppermute | solution.py:39
  12.0 1.6 %collective-permute-start.4 = (bf16[256,512]{1,0:T(8,128)(2,1)S(1)}, bf16[256,512]{1,0:T(8,128)(2,1)S(1)}, u32[]{:S(2)}, u32[]{:S(2)}) collective-permute-start(bf16[256,512]{1,0:T(8,128)(2,1)S(1)} %shard_map.99), channel_id=1, source_target_pairs={{0,1},{1,0},{2,3},{3,2},{4,5},{5,4},{6,7},{7,6},{8,9},{9,8},{10,11... | collective-permute-start | bytes 786440 | tf_op jit(solution)/shard_map/ppermute | solution.py:39
  12.3 3.8 %collective-permute-start.3 = (bf16[256,512]{1,0:T(8,128)(2,1)S(1)}, bf16[256,512]{1,0:T(8,128)(2,1)S(1)}, u32[]{:S(2)}, u32[]{:S(2)}) collective-permute-start(bf16[256,512]{1,0:T(8,128)(2,1)S(1)} %shard_map.96), channel_id=1, source_target_pairs={{0,1},{1,0},{2,3},{3,2},{4,5},{5,4},{6,7},{7,6},{8,9},{9,8},{10,11... | collective-permute-start | bytes 786440 | tf_op jit(solution)/shard_map/ppermute | solution.py:39
  13.6 6.0 %collective-permute-start.6 = (bf16[128,512]{1,0:T(8,128)(2,1)S(1)}, bf16[128,512]{1,0:T(8,128)(2,1)S(1)}, u32[]{:S(2)}, u32[]{:S(2)}) collective-permute-start(bf16[128,512]{1,0:T(8,128)(2,1)S(1)} %get-tuple-element.28), channel_id=1, source_target_pairs={{0,2},{1,3},{2,0},{3,1},{4,6},{5,7},{6,4},{7,5},{8,10},{9,11},{10,... | collective-permute-start | bytes 393224 | tf_op jit(solution)/shard_map/ppermute | solution.py:39
  15.3 14.3 %collective-permute-start.11 = (bf16[512,512]{1,0:T(8,128)(2,1)S(1)}, bf16[512,512]{1,0:T(8,128)(2,1)S(1)}, u32[]{:S(2)}, u32[]{:S(2)}) collective-permute-start(bf16[512,512]{1,0:T(8,128)(2,1)S(1)} %get-tuple-element.35), channel_id=1, source_target_pairs={{0,1},{1,0},{2,3},{3,2},{4,5},{5,4},{6,7},{7,6},{8,9},{9,8},{10,11... | collective-permute-start | bytes 1572872 | tf_op jit(solution)/shard_map/ppermute | solution.py:39
  15.6 6.8 %collective-permute-start.5 = (bf16[128,512]{1,0:T(8,128)(2,1)S(1)}, bf16[128,512]{1,0:T(8,128)(2,1)S(1)}, u32[]{:S(2)}, u32[]{:S(2)}) collective-permute-start(bf16[128,512]{1,0:T(8,128)(2,1)S(1)} %get-tuple-element.26), channel_id=1, source_target_pairs={{0,2},{1,3},{2,0},{3,1},{4,6},{5,7},{6,4},{7,5},{8,10},{9,11},{10,... | collective-permute-start | bytes 393224 | tf_op jit(solution)/shard_map/ppermute | solution.py:39
  19.7 8.5 %collective-permute-start.7 = (bf16[128,512]{1,0:T(8,128)(2,1)S(1)}, bf16[128,512]{1,0:T(8,128)(2,1)S(1)}, u32[]{:S(2)}, u32[]{:S(2)}) collective-permute-start(bf16[128,512]{1,0:T(8,128)(2,1)S(1)} %shard_map.101), channel_id=1, source_target_pairs={{0,4},{1,5},{2,6},{3,7},{4,0},{5,1},{6,2},{7,3},{8,12},{9,13},{10,... | collective-permute-start | bytes 393224 | tf_op jit(solution)/shard_map/ppermute | solution.py:39
  28.9 1.6 %collective-permute-start.10 = (bf16[256,512]{1,0:T(8,128)(2,1)S(1)}, bf16[256,512]{1,0:T(8,128)(2,1)S(1)}, u32[]{:S(2)}, u32[]{:S(2)}) collective-permute-start(bf16[256,512]{1,0:T(8,128)(2,1)S(1)} %shard_map.105), channel_id=1, source_target_pairs={{0,1},{1,0},{2,3},{3,2},{4,5},{5,4},{6,7},{7,6},{8,9},{9,8},{10,11... | collective-permute-start | bytes 786440 | tf_op jit(solution)/shard_map/ppermute | solution.py:39
  29.0 9.7 %collective-permute-start.9 = (bf16[128,512]{1,0:T(8,128)(2,1)S(1)}, bf16[128,512]{1,0:T(8,128)(2,1)S(1)}, u32[]{:S(2)}, u32[]{:S(2)}) collective-permute-start(bf16[128,512]{1,0:T(8,128)(2,1)S(1)} %get-tuple-element.32.refs_1_), channel_id=1, source_target_pairs={{0,4},{1,5},{2,6},{3,7},{4,0},{5,1},{6,2},{7,3},{8,12},{9,13},{10,... | collective-permute-start | bytes 393224 | tf_op jit(solution)/shard_map/ppermute | solution.py:39
  30.6 8.2 %collective-permute-start.12 = (bf16[64,512]{1,0:T(8,128)(2,1)S(1)}, bf16[64,512]{1,0:T(8,128)(2,1)S(1)}, u32[]{:S(2)}, u32[]{:S(2)}) collective-permute-start(bf16[64,512]{1,0:T(8,128)(2,1)S(1)} %get-tuple-element.36), channel_id=1, source_target_pairs={{0,8},{8,0},{16,24},{24,16},{1,9},{9,1},{17,25},{25,17},{2,10},{10... | collective-permute-start | bytes 196616 | tf_op jit(solution)/shard_map/ppermute | solution.py:39
  31.9 6.9 %collective-permute-start.13 = (bf16[64,512]{1,0:T(8,128)(2,1)S(1)}, bf16[64,512]{1,0:T(8,128)(2,1)S(1)}, u32[]{:S(2)}, u32[]{:S(2)}) collective-permute-start(bf16[64,512]{1,0:T(8,128)(2,1)S(1)} %get-tuple-element.37), channel_id=1, source_target_pairs={{0,16},{8,24},{16,0},{24,8},{1,17},{9,25},{17,1},{25,9},{2,18},{10... | collective-permute-start | bytes 196616 | tf_op jit(solution)/shard_map/ppermute | solution.py:39
  32.7 12.2 %collective-permute-start.8 = (bf16[128,512]{1,0:T(8,128)(2,1)S(1)}, bf16[128,512]{1,0:T(8,128)(2,1)S(1)}, u32[]{:S(2)}, u32[]{:S(2)}) collective-permute-start(bf16[128,512]{1,0:T(8,128)(2,1)S(1)} %get-tuple-element.32.refs_1_), channel_id=1, source_target_pairs={{0,2},{1,3},{2,0},{3,1},{4,6},{5,7},{6,4},{7,5},{8,10},{9,11},{10,... | collective-permute-start | bytes 393224 | tf_op jit(solution)/shard_map/ppermute | solution.py:39
  35.2 5.2 %collective-permute-start.16 = (bf16[64,512]{1,0:T(8,128)(2,1)S(1)}, bf16[64,512]{1,0:T(8,128)(2,1)S(1)}, u32[]{:S(2)}, u32[]{:S(2)}) collective-permute-start(bf16[64,512]{1,0:T(8,128)(2,1)S(1)} %get-tuple-element.39), channel_id=1, source_target_pairs={{0,24},{8,16},{16,8},{24,0},{1,25},{9,17},{17,9},{25,1},{2,26},{10... | collective-permute-start | bytes 196616 | tf_op jit(solution)/shard_map/ppermute | solution.py:39
  38.7 6.5 %collective-permute-start.14 = (bf16[128,512]{1,0:T(8,128)(2,1)S(1)}, bf16[128,512]{1,0:T(8,128)(2,1)S(1)}, u32[]{:S(2)}, u32[]{:S(2)}) collective-permute-start(bf16[128,512]{1,0:T(8,128)(2,1)S(1)} %shard_map.107.refs_3_), channel_id=1, source_target_pairs={{0,2},{1,3},{2,0},{3,1},{4,6},{5,7},{6,4},{7,5},{8,10},{9,11},{10,... | collective-permute-start | bytes 393224 | tf_op jit(solution)/shard_map/ppermute | solution.py:39
  40.4 6.3 %collective-permute-start.17 = (bf16[64,512]{1,0:T(8,128)(2,1)S(1)}, bf16[64,512]{1,0:T(8,128)(2,1)S(1)}, u32[]{:S(2)}, u32[]{:S(2)}) collective-permute-start(bf16[64,512]{1,0:T(8,128)(2,1)S(1)} %shard_map.110.refs_0_), channel_id=1, source_target_pairs={{0,2},{1,3},{2,0},{3,1},{4,6},{5,7},{6,4},{7,5},{8,10},{9,11},{10,... | collective-permute-start | bytes 196616 | tf_op jit(solution)/shard_map/ppermute | solution.py:39
  40.9 7.5 %collective-permute-start.18 = (bf16[64,512]{1,0:T(8,128)(2,1)S(1)}, bf16[64,512]{1,0:T(8,128)(2,1)S(1)}, u32[]{:S(2)}, u32[]{:S(2)}) collective-permute-start(bf16[64,512]{1,0:T(8,128)(2,1)S(1)} %shard_map.110.refs_0_), channel_id=1, source_target_pairs={{0,4},{1,5},{2,6},{3,7},{4,0},{5,1},{6,2},{7,3},{8,12},{9,13},{10,... | collective-permute-start | bytes 196616 | tf_op jit(solution)/shard_map/ppermute | solution.py:39
  41.8 6.6 %collective-permute-start.19 = (bf16[64,512]{1,0:T(8,128)(2,1)S(1)}, bf16[64,512]{1,0:T(8,128)(2,1)S(1)}, u32[]{:S(2)}, u32[]{:S(2)}) collective-permute-start(bf16[64,512]{1,0:T(8,128)(2,1)S(1)} %shard_map.110.refs_0_), channel_id=1, source_target_pairs={{0,6},{1,7},{2,4},{3,5},{4,2},{5,3},{6,0},{7,1},{8,14},{9,15},{10,... | collective-permute-start | bytes 196616 | tf_op jit(solution)/shard_map/ppermute | solution.py:39
  45.7 3.2 %collective-permute-start.15 = (bf16[512,512]{1,0:T(8,128)(2,1)S(1)}, bf16[512,512]{1,0:T(8,128)(2,1)S(1)}, u32[]{:S(2)}, u32[]{:S(2)}) collective-permute-start(bf16[512,512]{1,0:T(8,128)(2,1)S(1)} %shard_map.109), channel_id=1, source_target_pairs={{0,1},{1,0},{2,3},{3,2},{4,5},{5,4},{6,7},{7,6},{8,9},{9,8},{10,11... | collective-permute-start | bytes 1572872 | tf_op jit(solution)/shard_map/ppermute | solution.py:39
  49.0 7.7 %collective-permute-start.20 = (bf16[192,512]{1,0:T(8,128)(2,1)S(1)}, bf16[192,512]{1,0:T(8,128)(2,1)S(1)}, u32[]{:S(2)}, u32[]{:S(2)}) collective-permute-start(bf16[192,512]{1,0:T(8,128)(2,1)S(1)} %get-tuple-element.41), channel_id=1, source_target_pairs={{0,8},{8,0},{16,24},{24,16},{1,9},{9,1},{17,25},{25,17},{2,10},{10... | collective-permute-start | bytes 589832 | tf_op jit(solution)/shard_map/ppermute | solution.py:39
  50.3 9.8 %collective-permute-start.21 = (bf16[192,512]{1,0:T(8,128)(2,1)S(1)}, bf16[192,512]{1,0:T(8,128)(2,1)S(1)}, u32[]{:S(2)}, u32[]{:S(2)}) collective-permute-start(bf16[192,512]{1,0:T(8,128)(2,1)S(1)} %get-tuple-element.42), channel_id=1, source_target_pairs={{0,16},{8,24},{16,0},{24,8},{1,17},{9,25},{17,1},{25,9},{2,18},{10... | collective-permute-start | bytes 589832 | tf_op jit(solution)/shard_map/ppermute | solution.py:39
  51.1 8.9 %collective-permute-start.22 = (bf16[192,512]{1,0:T(8,128)(2,1)S(1)}, bf16[192,512]{1,0:T(8,128)(2,1)S(1)}, u32[]{:S(2)}, u32[]{:S(2)}) collective-permute-start(bf16[192,512]{1,0:T(8,128)(2,1)S(1)} %get-tuple-element.43), channel_id=1, source_target_pairs={{0,24},{8,16},{16,8},{24,0},{1,25},{9,17},{17,9},{25,1},{2,26},{10... | collective-permute-start | bytes 589832 | tf_op jit(solution)/shard_map/ppermute | solution.py:39
  60.1 1.6 %collective-permute-start.23 = (bf16[256,512]{1,0:T(8,128)(2,1)S(1)}, bf16[256,512]{1,0:T(8,128)(2,1)S(1)}, u32[]{:S(2)}, u32[]{:S(2)}) collective-permute-start(bf16[256,512]{1,0:T(8,128)(2,1)S(1)} %shard_map.113.refs_4_.refs_0_), channel_id=1, source_target_pairs={{0,1},{1,0},{2,3},{3,2},{4,5},{5,4},{6,7},{7,6},{8,9},{9,8},{10,11... | collective-permute-start | bytes 786440 | tf_op jit(solution)/shard_map/ppermute | solution.py:39
  (6 other events, 37.3 us)

commit v7 on v5

--- a/solution.py
+++ b/solution.py
@@ -242,15 +242,15 @@
             same[k | bit] = z_swap(same[k], bit)
             if bit > 1:
                 (same[k | bit],) = call(
-                    relay, [like(TILE, width)], (same[k | bit],), after=terms_w[1 : n_row - 1]
+                    relay, [like(TILE, width)], (same[k | bit],), us=3
                 )
         bit //= 2
-    (plane_w,) = call(add_all, [like(piece, width)], terms_w)
+    (plane_w,) = call(add_all, [like(piece, width)], terms_w, us=1)
     terms_w = [plane_w] + [z_swap(plane_w, k) for k in range(1, n_z)]
-    (final_w,) = call(add_all, [like(piece, width)], terms_w, us=5)
     (other,) = call(backward, [like(col_nodes, width)], (other_t, *same))
     other = core_swap(other)
     (mine,) = call(backward, [like(col_nodes, width, dtype=F32)], (dense_t, *same))
+    (final_w,) = call(add_all, [like(piece, width)], terms_w, after=(mine,), us=5)
     back, *parts = call(
         messages,
         [like(TILE, width, dtype=F32)] + [like(TILE + piece, width)] * (n_row - 1),

time: 63 us -> 62.8 us (level)
  waiting for transfers between devices: 28.7 us -> 27 us
  starting transfers between devices: 24.6 us -> 25.6 us
    ppermute x24, waiting for transfers between devices: 28.7 us -> 27 us  [swap(): return lax.ppermute(value, axis, [(i, i ^ mask) for i in range(size)])]
    ppermute x24, starting transfers between devices: 24.6 us -> 25.6 us  [swap(): return lax.ppermute(value, axis, [(i, i ^ mask) for i in range(size)])]
  transfers between devices with their start and end apart: 24 -> 24, of which waited for: 13 -> 14; matrix products, arithmetic and copies ran while one was open for 0% -> 0% of each run, Pallas kernels for 9% -> 9%
where the time goes in v7:
time: 62.8 us; the launch traced here: 62.7 us
  waiting for transfers between devices  27 us (43%)
  starting transfers between devices  25.6 us (41%)
  Pallas kernels  7.41 us (12%)
  between operations  1.52 us (2%)
  local copies, waits for them, and re-layouts  1.15 us (2%)
    ppermute x24, waiting for transfers between devices, swap(): return lax.ppermute(value, axis, [(i, i ^ mask) for i in range(size)])  27 us
    ppermute x24, starting transfers between devices, swap(): return lax.ppermute(value, axis, [(i, i ^ mask) for i in range(size)])  25.6 us
    pallas_call x21, Pallas kernels, call(): pl.pallas_call(body, out_shape=outs, in_specs=(specs or [VMEM] * len(args...  7.41 us
  transfers between devices with their start and end apart: 24, of which 14 were waited for; matrix products, arithmetic and copies ran while one was open for 0% of the time, Pallas kernels for 9%

profile of v7, /device:TPU:0, one launch (start us, length us, event | category | flops | bytes accessed | tf_op | source)
XLA Modules:
  0.0 62.7 jit_solution(7370760145304843367)
XLA Ops:
  0.7 3.0 %collective-permute-start = (bf16[128,512]{1,0:T(8,128)(2,1)}, bf16[128,512]{1,0:T(8,128)(2,1)S(1)}, u32[]{:S(2)}, u32[]{:S(2)}) collective-permute-start(bf16[128,512]{1,0:T(8,128)(2,1)} %bitcast.3), channel_id=1, source_target_pairs={{0,8},{8,0},{16,24},{24,16},{1,9},{9,1},{17,25},{25,17},{2,10},{10... | collective-permute-start | bytes 393224 | tf_op jit(solution)/shard_map/ppermute | solution.py:39
  3.7 1.5 %collective-permute-start.1 = (bf16[128,512]{1,0:T(8,128)(2,1)}, bf16[128,512]{1,0:T(8,128)(2,1)S(1)}, u32[]{:S(2)}, u32[]{:S(2)}) collective-permute-start(bf16[128,512]{1,0:T(8,128)(2,1)} %bitcast.4), channel_id=1, source_target_pairs={{0,16},{8,24},{16,0},{24,8},{1,17},{9,25},{17,1},{25,9},{2,18},{10... | collective-permute-start | bytes 393224 | tf_op jit(solution)/shard_map/ppermute | solution.py:39
  5.9 1.1 %copy-done.1 = bf16[1,1,24,128,128]{4,3,2,1,0:T(8,128)(2,1)S(1)} copy-done((bf16[1,1,24,128,128]{4,3,2,1,0:T(8,128)(2,1)S(1)}, bf16[1,1,24,128,128]{4,3,2,1,0:T(8,128)(2,1)}, u32[]{:S(2)}) %copy-start.1) | copy-done | bytes 786456
  7.0 1.7 %shard_map.94 = (bf16[1024,512]{1,0:T(8,128)(2,1)S(1)}, bf16[512,512]{1,0:T(8,128)(2,1)S(1)}, bf16[512,512]{1,0:T(8,128)(2,1)S(1)}) custom-call(bf16[1,1,24,128,128]{4,3,2,1,0:T(8,128)(2,1)S(1)} %copy-done.1, s32[1,1,24]{2,1,0:T(1,128)S(1)} %copy-done.4, s32[1,1,24]{2,1,0:T(1,128)S(1)} %copy-done.5, s32[1,1]{1,0:T(1,128)S(6)} %copy.10.refs_3_), custom_call_target="tpu_custom_call" | custom-call | tf_op jit(solution)/shard_map/pallas_call | solution.py:23
  8.7 2.9 %collective-permute-done.1.refs_3_ = bf16[128,512]{1,0:T(8,128)(2,1)S(1)} collective-permute-done((bf16[128,512]{1,0:T(8,128)(2,1)}, bf16[128,512]{1,0:T(8,128)(2,1)S(1)}, u32[]{:S(2)}, u32[]{:S(2)}) %collective-permute-start.1) | collective-permute-done | bytes 131104 | tf_op jit(solution)/shard_map/ppermute | solution.py:39
  13.6 1.6 %collective-permute-start.6 = (bf16[128,512]{1,0:T(8,128)(2,1)S(1)}, bf16[128,512]{1,0:T(8,128)(2,1)S(1)}, u32[]{:S(2)}, u32[]{:S(2)}) collective-permute-start(bf16[128,512]{1,0:T(8,128)(2,1)S(1)} %get-tuple-element.30), channel_id=1, source_target_pairs={{0,2},{1,3},{2,0},{3,1},{4,6},{5,7},{6,4},{7,5},{8,10},{9,11},{10,... | collective-permute-start | bytes 393224 | tf_op jit(solution)/shard_map/ppermute | solution.py:39
  16.1 3.5 %collective-permute-done.6.refs_1_ = bf16[128,512]{1,0:T(8,128)(2,1)S(1)} collective-permute-done((bf16[128,512]{1,0:T(8,128)(2,1)S(1)}, bf16[128,512]{1,0:T(8,128)(2,1)S(1)}, u32[]{:S(2)}, u32[]{:S(2)}) %collective-permute-start.6) | collective-permute-done | bytes 131104 | tf_op jit(solution)/shard_map/ppermute | solution.py:39
  19.7 2.7 %collective-permute-start.7 = (bf16[128,512]{1,0:T(8,128)(2,1)S(1)}, bf16[128,512]{1,0:T(8,128)(2,1)S(1)}, u32[]{:S(2)}, u32[]{:S(2)}) collective-permute-start(bf16[128,512]{1,0:T(8,128)(2,1)S(1)} %shard_map.101), channel_id=1, source_target_pairs={{0,4},{1,5},{2,6},{3,7},{4,0},{5,1},{6,2},{7,3},{8,12},{9,13},{10,... | collective-permute-start | bytes 393224 | tf_op jit(solution)/shard_map/ppermute | solution.py:39
  22.3 5.8 %collective-permute-done.7.refs_4_ = bf16[128,512]{1,0:T(8,128)(2,1)S(1)} collective-permute-done((bf16[128,512]{1,0:T(8,128)(2,1)S(1)}, bf16[128,512]{1,0:T(8,128)(2,1)S(1)}, u32[]{:S(2)}, u32[]{:S(2)}) %collective-permute-start.7) | collective-permute-done | bytes 131104 | tf_op jit(solution)/shard_map/ppermute | solution.py:39
  29.3 3.5 %collective-permute-start.8 = (bf16[128,512]{1,0:T(8,128)(2,1)S(1)}, bf16[128,512]{1,0:T(8,128)(2,1)S(1)}, u32[]{:S(2)}, u32[]{:S(2)}) collective-permute-start(bf16[128,512]{1,0:T(8,128)(2,1)S(1)} %get-tuple-element.34.refs_1_), channel_id=1, source_target_pairs={{0,2},{1,3},{2,0},{3,1},{4,6},{5,7},{6,4},{7,5},{8,10},{9,11},{10,... | collective-permute-start | bytes 393224 | tf_op jit(solution)/shard_map/ppermute | solution.py:39
  32.9 1.3 %collective-permute-start.14 = (bf16[64,512]{1,0:T(8,128)(2,1)S(1)}, bf16[64,512]{1,0:T(8,128)(2,1)S(1)}, u32[]{:S(2)}, u32[]{:S(2)}) collective-permute-start(bf16[64,512]{1,0:T(8,128)(2,1)S(1)} %get-tuple-element.41), channel_id=1, source_target_pairs={{0,8},{8,0},{16,24},{24,16},{1,9},{9,1},{17,25},{25,17},{2,10},{10... | collective-permute-start | bytes 196616 | tf_op jit(solution)/shard_map/ppermute | solution.py:39
  34.1 0.8 %collective-permute-start.15 = (bf16[64,512]{1,0:T(8,128)(2,1)S(1)}, bf16[64,512]{1,0:T(8,128)(2,1)S(1)}, u32[]{:S(2)}, u32[]{:S(2)}) collective-permute-start(bf16[64,512]{1,0:T(8,128)(2,1)S(1)} %get-tuple-element.42), channel_id=1, source_target_pairs={{0,16},{8,24},{16,0},{24,8},{1,17},{9,25},{17,1},{25,9},{2,18},{10... | collective-permute-start | bytes 196616 | tf_op jit(solution)/shard_map/ppermute | solution.py:39
  35.0 1.4 %collective-permute-start.16 = (bf16[64,512]{1,0:T(8,128)(2,1)S(1)}, bf16[64,512]{1,0:T(8,128)(2,1)S(1)}, u32[]{:S(2)}, u32[]{:S(2)}) collective-permute-start(bf16[64,512]{1,0:T(8,128)(2,1)S(1)} %get-tuple-element.43), channel_id=1, source_target_pairs={{0,24},{8,16},{16,8},{24,0},{1,25},{9,17},{17,9},{25,1},{2,26},{10... | collective-permute-start | bytes 196616 | tf_op jit(solution)/shard_map/ppermute | solution.py:39
  36.4 2.4 %collective-permute-done.9.refs_0_ = bf16[128,512]{1,0:T(8,128)(2,1)S(1)} collective-permute-done((bf16[128,512]{1,0:T(8,128)(2,1)S(1)}, bf16[128,512]{1,0:T(8,128)(2,1)S(1)}, u32[]{:S(2)}, u32[]{:S(2)}) %collective-permute-start.9) | collective-permute-done | bytes 131104 | tf_op jit(solution)/shard_map/ppermute | solution.py:39
  39.1 1.0 %collective-permute-done.16.refs_3_ = bf16[64,512]{1,0:T(8,128)(2,1)S(1)} collective-permute-done((bf16[64,512]{1,0:T(8,128)(2,1)S(1)}, bf16[64,512]{1,0:T(8,128)(2,1)S(1)}, u32[]{:S(2)}, u32[]{:S(2)}) %collective-permute-start.16) | collective-permute-done | bytes 65568 | tf_op jit(solution)/shard_map/ppermute | solution.py:39
  40.2 0.8 %collective-permute-start.17 = (bf16[64,512]{1,0:T(8,128)(2,1)S(1)}, bf16[64,512]{1,0:T(8,128)(2,1)S(1)}, u32[]{:S(2)}, u32[]{:S(2)}) collective-permute-start(bf16[64,512]{1,0:T(8,128)(2,1)S(1)} %shard_map.109.refs_0_), channel_id=1, source_target_pairs={{0,2},{1,3},{2,0},{3,1},{4,6},{5,7},{6,4},{7,5},{8,10},{9,11},{10,... | collective-permute-start | bytes 196616 | tf_op jit(solution)/shard_map/ppermute | solution.py:39
  41.7 2.9 %collective-permute-start.19 = (bf16[64,512]{1,0:T(8,128)(2,1)S(1)}, bf16[64,512]{1,0:T(8,128)(2,1)S(1)}, u32[]{:S(2)}, u32[]{:S(2)}) collective-permute-start(bf16[64,512]{1,0:T(8,128)(2,1)S(1)} %shard_map.109.refs_0_), channel_id=1, source_target_pairs={{0,6},{1,7},{2,4},{3,5},{4,2},{5,3},{6,0},{7,1},{8,14},{9,15},{10,... | collective-permute-start | bytes 196616 | tf_op jit(solution)/shard_map/ppermute | solution.py:39
  46.9 1.6 %collective-permute-done.18.refs_2_ = bf16[64,512]{1,0:T(8,128)(2,1)S(1)} collective-permute-done((bf16[64,512]{1,0:T(8,128)(2,1)S(1)}, bf16[64,512]{1,0:T(8,128)(2,1)S(1)}, u32[]{:S(2)}, u32[]{:S(2)}) %collective-permute-start.18) | collective-permute-done | bytes 65568 | tf_op jit(solution)/shard_map/ppermute | solution.py:39
  48.6 1.3 %collective-permute-start.20 = (bf16[192,512]{1,0:T(8,128)(2,1)S(1)}, bf16[192,512]{1,0:T(8,128)(2,1)S(1)}, u32[]{:S(2)}, u32[]{:S(2)}) collective-permute-start(bf16[192,512]{1,0:T(8,128)(2,1)S(1)} %get-tuple-element.45), channel_id=1, source_target_pairs={{0,8},{8,0},{16,24},{24,16},{1,9},{9,1},{17,25},{25,17},{2,10},{10... | collective-permute-start | bytes 589832 | tf_op jit(solution)/shard_map/ppermute | solution.py:39
  50.8 1.4 %collective-permute-start.22 = (bf16[192,512]{1,0:T(8,128)(2,1)S(1)}, bf16[192,512]{1,0:T(8,128)(2,1)S(1)}, u32[]{:S(2)}, u32[]{:S(2)}) collective-permute-start(bf16[192,512]{1,0:T(8,128)(2,1)S(1)} %get-tuple-element.47), channel_id=1, source_target_pairs={{0,24},{8,16},{16,8},{24,0},{1,25},{9,17},{17,9},{25,1},{2,26},{10... | collective-permute-start | bytes 589832 | tf_op jit(solution)/shard_map/ppermute | solution.py:39
  52.9 3.7 %collective-permute-done.20.refs_1_ = bf16[192,512]{1,0:T(8,128)(2,1)S(1)} collective-permute-done((bf16[192,512]{1,0:T(8,128)(2,1)S(1)}, bf16[192,512]{1,0:T(8,128)(2,1)S(1)}, u32[]{:S(2)}, u32[]{:S(2)}) %collective-permute-start.20) | collective-permute-done | bytes 196640 | tf_op jit(solution)/shard_map/ppermute | solution.py:39
  56.6 1.8 %collective-permute-done.21.refs_2_ = bf16[192,512]{1,0:T(8,128)(2,1)S(1)} collective-permute-done((bf16[192,512]{1,0:T(8,128)(2,1)S(1)}, bf16[192,512]{1,0:T(8,128)(2,1)S(1)}, u32[]{:S(2)}, u32[]{:S(2)}) %collective-permute-start.21) | collective-permute-done | bytes 196640 | tf_op jit(solution)/shard_map/ppermute | solution.py:39
  58.3 1.6 %collective-permute-done.22.refs_3_ = bf16[192,512]{1,0:T(8,128)(2,1)S(1)} collective-permute-done((bf16[192,512]{1,0:T(8,128)(2,1)S(1)}, bf16[192,512]{1,0:T(8,128)(2,1)S(1)}, u32[]{:S(2)}, u32[]{:S(2)}) %collective-permute-start.22) | collective-permute-done | bytes 196640 | tf_op jit(solution)/shard_map/ppermute | solution.py:39
  61.6 1.0 %shard_map.114 = f32[512,512]{1,0:T(8,128)} custom-call(bf16[256,512]{1,0:T(8,128)(2,1)S(1)} %shard_map.112.refs_4_.refs_0_, bf16[256,512]{1,0:T(8,128)(2,1)S(1)} %collective-permute-done.23.refs_1_), custom_call_target="tpu_custom_call" | custom-call | tf_op jit(solution)/shard_map/pallas_call | solution.py:23
  (57 shorter events, 10.6 us)
Async XLA Ops:
  0.7 8.0 %collective-permute-start = (bf16[128,512]{1,0:T(8,128)(2,1)}, bf16[128,512]{1,0:T(8,128)(2,1)S(1)}, u32[]{:S(2)}, u32[]{:S(2)}) collective-permute-start(bf16[128,512]{1,0:T(8,128)(2,1)} %bitcast.3), channel_id=1, source_target_pairs={{0,8},{8,0},{16,24},{24,16},{1,9},{9,1},{17,25},{25,17},{2,10},{10... | collective-permute-start | bytes 393224 | tf_op jit(solution)/shard_map/ppermute | solution.py:39
  3.7 8.0 %collective-permute-start.1 = (bf16[128,512]{1,0:T(8,128)(2,1)}, bf16[128,512]{1,0:T(8,128)(2,1)S(1)}, u32[]{:S(2)}, u32[]{:S(2)}) collective-permute-start(bf16[128,512]{1,0:T(8,128)(2,1)} %bitcast.4), channel_id=1, source_target_pairs={{0,16},{8,24},{16,0},{24,8},{1,17},{9,25},{17,1},{25,9},{2,18},{10... | collective-permute-start | bytes 393224 | tf_op jit(solution)/shard_map/ppermute | solution.py:39
  5.2 6.5 %collective-permute-start.2 = (bf16[128,512]{1,0:T(8,128)(2,1)}, bf16[128,512]{1,0:T(8,128)(2,1)S(1)}, u32[]{:S(2)}, u32[]{:S(2)}) collective-permute-start(bf16[128,512]{1,0:T(8,128)(2,1)} %bitcast.5), channel_id=1, source_target_pairs={{0,24},{8,16},{16,8},{24,0},{1,25},{9,17},{17,9},{25,1},{2,26},{10... | collective-permute-start | bytes 393224 | tf_op jit(solution)/shard_map/ppermute | solution.py:39
  12.0 1.6 %collective-permute-start.4 = (bf16[256,512]{1,0:T(8,128)(2,1)S(1)}, bf16[256,512]{1,0:T(8,128)(2,1)S(1)}, u32[]{:S(2)}, u32[]{:S(2)}) collective-permute-start(bf16[256,512]{1,0:T(8,128)(2,1)S(1)} %shard_map.99), channel_id=1, source_target_pairs={{0,1},{1,0},{2,3},{3,2},{4,5},{5,4},{6,7},{7,6},{8,9},{9,8},{10,11... | collective-permute-start | bytes 786440 | tf_op jit(solution)/shard_map/ppermute | solution.py:39
  12.3 3.8 %collective-permute-start.3 = (bf16[256,512]{1,0:T(8,128)(2,1)S(1)}, bf16[256,512]{1,0:T(8,128)(2,1)S(1)}, u32[]{:S(2)}, u32[]{:S(2)}) collective-permute-start(bf16[256,512]{1,0:T(8,128)(2,1)S(1)} %shard_map.96), channel_id=1, source_target_pairs={{0,1},{1,0},{2,3},{3,2},{4,5},{5,4},{6,7},{7,6},{8,9},{9,8},{10,11... | collective-permute-start | bytes 786440 | tf_op jit(solution)/shard_map/ppermute | solution.py:39
  13.6 6.0 %collective-permute-start.6 = (bf16[128,512]{1,0:T(8,128)(2,1)S(1)}, bf16[128,512]{1,0:T(8,128)(2,1)S(1)}, u32[]{:S(2)}, u32[]{:S(2)}) collective-permute-start(bf16[128,512]{1,0:T(8,128)(2,1)S(1)} %get-tuple-element.30), channel_id=1, source_target_pairs={{0,2},{1,3},{2,0},{3,1},{4,6},{5,7},{6,4},{7,5},{8,10},{9,11},{10,... | collective-permute-start | bytes 393224 | tf_op jit(solution)/shard_map/ppermute | solution.py:39
  15.3 17.5 %collective-permute-start.11 = (bf16[512,512]{1,0:T(8,128)(2,1)S(1)}, bf16[512,512]{1,0:T(8,128)(2,1)S(1)}, u32[]{:S(2)}, u32[]{:S(2)}) collective-permute-start(bf16[512,512]{1,0:T(8,128)(2,1)S(1)} %get-tuple-element.35), channel_id=1, source_target_pairs={{0,1},{1,0},{2,3},{3,2},{4,5},{5,4},{6,7},{7,6},{8,9},{9,8},{10,11... | collective-permute-start | bytes 1572872 | tf_op jit(solution)/shard_map/ppermute | solution.py:39
  15.6 6.8 %collective-permute-start.5 = (bf16[128,512]{1,0:T(8,128)(2,1)S(1)}, bf16[128,512]{1,0:T(8,128)(2,1)S(1)}, u32[]{:S(2)}, u32[]{:S(2)}) collective-permute-start(bf16[128,512]{1,0:T(8,128)(2,1)S(1)} %get-tuple-element.28), channel_id=1, source_target_pairs={{0,2},{1,3},{2,0},{3,1},{4,6},{5,7},{6,4},{7,5},{8,10},{9,11},{10,... | collective-permute-start | bytes 393224 | tf_op jit(solution)/shard_map/ppermute | solution.py:39
  19.7 8.5 %collective-permute-start.7 = (bf16[128,512]{1,0:T(8,128)(2,1)S(1)}, bf16[128,512]{1,0:T(8,128)(2,1)S(1)}, u32[]{:S(2)}, u32[]{:S(2)}) collective-permute-start(bf16[128,512]{1,0:T(8,128)(2,1)S(1)} %shard_map.101), channel_id=1, source_target_pairs={{0,4},{1,5},{2,6},{3,7},{4,0},{5,1},{6,2},{7,3},{8,12},{9,13},{10,... | collective-permute-start | bytes 393224 | tf_op jit(solution)/shard_map/ppermute | solution.py:39
  29.0 3.8 %collective-permute-start.13 = (bf16[256,512]{1,0:T(8,128)(2,1)S(1)}, bf16[256,512]{1,0:T(8,128)(2,1)S(1)}, u32[]{:S(2)}, u32[]{:S(2)}) collective-permute-start(bf16[256,512]{1,0:T(8,128)(2,1)S(1)} %get-tuple-element.39), channel_id=1, source_target_pairs={{0,1},{1,0},{2,3},{3,2},{4,5},{5,4},{6,7},{7,6},{8,9},{9,8},{10,11... | collective-permute-start | bytes 786440 | tf_op jit(solution)/shard_map/ppermute | solution.py:39
  29.1 9.7 %collective-permute-start.9 = (bf16[128,512]{1,0:T(8,128)(2,1)S(1)}, bf16[128,512]{1,0:T(8,128)(2,1)S(1)}, u32[]{:S(2)}, u32[]{:S(2)}) collective-permute-start(bf16[128,512]{1,0:T(8,128)(2,1)S(1)} %get-tuple-element.34.refs_1_), channel_id=1, source_target_pairs={{0,4},{1,5},{2,6},{3,7},{4,0},{5,1},{6,2},{7,3},{8,12},{9,13},{10,... | collective-permute-start | bytes 393224 | tf_op jit(solution)/shard_map/ppermute | solution.py:39
  29.3 15.3 %collective-permute-start.8 = (bf16[128,512]{1,0:T(8,128)(2,1)S(1)}, bf16[128,512]{1,0:T(8,128)(2,1)S(1)}, u32[]{:S(2)}, u32[]{:S(2)}) collective-permute-start(bf16[128,512]{1,0:T(8,128)(2,1)S(1)} %get-tuple-element.34.refs_1_), channel_id=1, source_target_pairs={{0,2},{1,3},{2,0},{3,1},{4,6},{5,7},{6,4},{7,5},{8,10},{9,11},{10,... | collective-permute-start | bytes 393224 | tf_op jit(solution)/shard_map/ppermute | solution.py:39
  32.9 6.0 %collective-permute-start.14 = (bf16[64,512]{1,0:T(8,128)(2,1)S(1)}, bf16[64,512]{1,0:T(8,128)(2,1)S(1)}, u32[]{:S(2)}, u32[]{:S(2)}) collective-permute-start(bf16[64,512]{1,0:T(8,128)(2,1)S(1)} %get-tuple-element.41), channel_id=1, source_target_pairs={{0,8},{8,0},{16,24},{24,16},{1,9},{9,1},{17,25},{25,17},{2,10},{10... | collective-permute-start | bytes 196616 | tf_op jit(solution)/shard_map/ppermute | solution.py:39
  34.1 5.0 %collective-permute-start.15 = (bf16[64,512]{1,0:T(8,128)(2,1)S(1)}, bf16[64,512]{1,0:T(8,128)(2,1)S(1)}, u32[]{:S(2)}, u32[]{:S(2)}) collective-permute-start(bf16[64,512]{1,0:T(8,128)(2,1)S(1)} %get-tuple-element.42), channel_id=1, source_target_pairs={{0,16},{8,24},{16,0},{24,8},{1,17},{9,25},{17,1},{25,9},{2,18},{10... | collective-permute-start | bytes 196616 | tf_op jit(solution)/shard_map/ppermute | solution.py:39
  35.0 5.2 %collective-permute-start.16 = (bf16[64,512]{1,0:T(8,128)(2,1)S(1)}, bf16[64,512]{1,0:T(8,128)(2,1)S(1)}, u32[]{:S(2)}, u32[]{:S(2)}) collective-permute-start(bf16[64,512]{1,0:T(8,128)(2,1)S(1)} %get-tuple-element.43), channel_id=1, source_target_pairs={{0,24},{8,16},{16,8},{24,0},{1,25},{9,17},{17,9},{25,1},{2,26},{10... | collective-permute-start | bytes 196616 | tf_op jit(solution)/shard_map/ppermute | solution.py:39
  38.8 6.5 %collective-permute-start.10 = (bf16[128,512]{1,0:T(8,128)(2,1)S(1)}, bf16[128,512]{1,0:T(8,128)(2,1)S(1)}, u32[]{:S(2)}, u32[]{:S(2)}) collective-permute-start(bf16[128,512]{1,0:T(8,128)(2,1)S(1)} %shard_map.104.refs_3_), channel_id=1, source_target_pairs={{0,2},{1,3},{2,0},{3,1},{4,6},{5,7},{6,4},{7,5},{8,10},{9,11},{10,... | collective-permute-start | bytes 393224 | tf_op jit(solution)/shard_map/ppermute | solution.py:39
  40.2 6.8 %collective-permute-start.17 = (bf16[64,512]{1,0:T(8,128)(2,1)S(1)}, bf16[64,512]{1,0:T(8,128)(2,1)S(1)}, u32[]{:S(2)}, u32[]{:S(2)}) collective-permute-start(bf16[64,512]{1,0:T(8,128)(2,1)S(1)} %shard_map.109.refs_0_), channel_id=1, source_target_pairs={{0,2},{1,3},{2,0},{3,1},{4,6},{5,7},{6,4},{7,5},{8,10},{9,11},{10,... | collective-permute-start | bytes 196616 | tf_op jit(solution)/shard_map/ppermute | solution.py:39
  41.0 7.5 %collective-permute-start.18 = (bf16[64,512]{1,0:T(8,128)(2,1)S(1)}, bf16[64,512]{1,0:T(8,128)(2,1)S(1)}, u32[]{:S(2)}, u32[]{:S(2)}) collective-permute-start(bf16[64,512]{1,0:T(8,128)(2,1)S(1)} %shard_map.109.refs_0_), channel_id=1, source_target_pairs={{0,4},{1,5},{2,6},{3,7},{4,0},{5,1},{6,2},{7,3},{8,12},{9,13},{10,... | collective-permute-start | bytes 196616 | tf_op jit(solution)/shard_map/ppermute | solution.py:39
  41.7 6.8 %collective-permute-start.19 = (bf16[64,512]{1,0:T(8,128)(2,1)S(1)}, bf16[64,512]{1,0:T(8,128)(2,1)S(1)}, u32[]{:S(2)}, u32[]{:S(2)}) collective-permute-start(bf16[64,512]{1,0:T(8,128)(2,1)S(1)} %shard_map.109.refs_0_), channel_id=1, source_target_pairs={{0,6},{1,7},{2,4},{3,5},{4,2},{5,3},{6,0},{7,1},{8,14},{9,15},{10,... | collective-permute-start | bytes 196616 | tf_op jit(solution)/shard_map/ppermute | solution.py:39
  45.7 2.8 %collective-permute-start.12 = (bf16[512,512]{1,0:T(8,128)(2,1)S(1)}, bf16[512,512]{1,0:T(8,128)(2,1)S(1)}, u32[]{:S(2)}, u32[]{:S(2)}) collective-permute-start(bf16[512,512]{1,0:T(8,128)(2,1)S(1)} %shard_map.106), channel_id=1, source_target_pairs={{0,1},{1,0},{2,3},{3,2},{4,5},{5,4},{6,7},{7,6},{8,9},{9,8},{10,11... | collective-permute-start | bytes 1572872 | tf_op jit(solution)/shard_map/ppermute | solution.py:39
  48.6 7.9 %collective-permute-start.20 = (bf16[192,512]{1,0:T(8,128)(2,1)S(1)}, bf16[192,512]{1,0:T(8,128)(2,1)S(1)}, u32[]{:S(2)}, u32[]{:S(2)}) collective-permute-start(bf16[192,512]{1,0:T(8,128)(2,1)S(1)} %get-tuple-element.45), channel_id=1, source_target_pairs={{0,8},{8,0},{16,24},{24,16},{1,9},{9,1},{17,25},{25,17},{2,10},{10... | collective-permute-start | bytes 589832 | tf_op jit(solution)/shard_map/ppermute | solution.py:39
  49.9 8.4 %collective-permute-start.21 = (bf16[192,512]{1,0:T(8,128)(2,1)S(1)}, bf16[192,512]{1,0:T(8,128)(2,1)S(1)}, u32[]{:S(2)}, u32[]{:S(2)}) collective-permute-start(bf16[192,512]{1,0:T(8,128)(2,1)S(1)} %get-tuple-element.46), channel_id=1, source_target_pairs={{0,16},{8,24},{16,0},{24,8},{1,17},{9,25},{17,1},{25,9},{2,18},{10... | collective-permute-start | bytes 589832 | tf_op jit(solution)/shard_map/ppermute | solution.py:39
  50.8 9.2 %collective-permute-start.22 = (bf16[192,512]{1,0:T(8,128)(2,1)S(1)}, bf16[192,512]{1,0:T(8,128)(2,1)S(1)}, u32[]{:S(2)}, u32[]{:S(2)}) collective-permute-start(bf16[192,512]{1,0:T(8,128)(2,1)S(1)} %get-tuple-element.47), channel_id=1, source_target_pairs={{0,24},{8,16},{16,8},{24,0},{1,25},{9,17},{17,9},{25,1},{2,26},{10... | collective-permute-start | bytes 589832 | tf_op jit(solution)/shard_map/ppermute | solution.py:39
  60.0 1.6 %collective-permute-start.23 = (bf16[256,512]{1,0:T(8,128)(2,1)S(1)}, bf16[256,512]{1,0:T(8,128)(2,1)S(1)}, u32[]{:S(2)}, u32[]{:S(2)}) collective-permute-start(bf16[256,512]{1,0:T(8,128)(2,1)S(1)} %shard_map.112.refs_4_.refs_0_), channel_id=1, source_target_pairs={{0,1},{1,0},{2,3},{3,2},{4,5},{5,4},{6,7},{7,6},{8,9},{9,8},{10,11... | collective-permute-start | bytes 786440 | tf_op jit(solution)/shard_map/ppermute | solution.py:39
  (6 other events, 37.3 us)

commit v8 on v7

--- a/solution.py
+++ b/solution.py
@@ -159,21 +159,24 @@
     out[...] = total.astype(BF16)
 
 
-def join(own, *refs):
-    *others, out = refs
-    me_row = lax.axis_index("row")
-    piece = own.shape[0]
-    out[pl.ds(pl.multiple_of(me_row * piece, piece), piece), :] = own[...]
-    for k, ref in enumerate(others):
-        at = pl.multiple_of((me_row ^ (k + 1)) * piece, piece)
-        out[pl.ds(at, piece), :] = ref[TILE:, :]
-
-
-def spread(mine, other, out):
-    core = lax.axis_index("col") & 1
-    half = mine.shape[0]
-    out[pl.ds(pl.multiple_of(core * half, half), half), :] = mine[...].astype(F32)
-    out[pl.ds(pl.multiple_of((1 - core) * half, half), half), :] = other[...].astype(F32)
+def join(*refs):
+    *pieces, out = refs
+    rows = out.shape[0] // len(pieces)
+    for k, ref in enumerate(pieces):
+        skip = ref.shape[0] - rows
+        out[k * rows : (k + 1) * rows, :] = ref[skip:, :]
+
+
+def spread(*refs):
+    *parts, out = refs
+    me_row, core = lax.axis_index("row"), lax.axis_index("col") & 1
+    n_row = lax.axis_size("row")
+    rows = out.shape[0] // 2 // n_row
+    for part, ref in enumerate(parts):
+        for k in range(n_row // 2):
+            place = (core ^ (part // 2)) * n_row + (me_row ^ (part % 2 * (n_row // 2) + k))
+            at = pl.multiple_of(place * rows, rows)
+            out[pl.ds(at, rows), :] = ref[k * rows : (k + 1) * rows, :].astype(F32)
 
 
 def local(feats, weight, cotangent, tile_values, tile_rows, tile_cols, tile_count):
@@ -260,10 +263,16 @@
     layer_out, done = call(
         activation, [like(TILE, width), like(8, TILE, dtype=F32)], (hidden,), us=1
     )
-    (half_w,) = call(join, [like(width // 2, width)], (final_w, *terms), after=(done,))
-    other_w = core_swap(half_w)
-    (feat_grad,) = call(add_rows, [like(TILE, width)], (back, *terms), after=(half_w,))
-    (weight_grad,) = call(spread, [like(width, width, dtype=F32)], (half_w, other_w))
+    half_row = n_row // 2
+    early = [final_w] + [t for t in terms[: half_row - 1]]
+    (early_w,) = call(join, [like(half_row * piece, width)], early, after=(done,))
+    early_other = core_swap(early_w)
+    (late_w,) = call(join, [like(half_row * piece, width)], terms[half_row - 1 :], after=(early_other,))
+    late_other = core_swap(late_w)
+    (feat_grad,) = call(add_rows, [like(TILE, width)], (back, *terms), after=(late_w,))
+    (weight_grad,) = call(
+        spread, [like(width, width, dtype=F32)], (early_w, late_w, early_other, late_other)
+    )
     return layer_out[None], feat_grad[None], weight_grad
 
 

time: 62.8 us -> 62.6 us (level)
  waiting for transfers between devices: 27 us -> 25.7 us
  Pallas kernels: 7.41 us -> 8.41 us
    ppermute x24 -> x25, waiting for transfers between devices: 27 us -> 25.7 us  [swap(): return lax.ppermute(value, axis, [(i, i ^ mask) for i in range(size)])]
    pallas_call x21 -> x22, Pallas kernels: 7.41 us -> 8.41 us  [call(): pl.pallas_call(body, out_shape=outs, in_specs=(specs or [VMEM] * len(args...]
    ppermute x24 -> x25, starting transfers between devices: 25.6 us -> 25.6 us  [swap(): return lax.ppermute(value, axis, [(i, i ^ mask) for i in range(size)])]
  transfers between devices with their start and end apart: 24 -> 25, of which waited for: 14 -> 14; matrix products, arithmetic and copies ran while one was open for 0% -> 0% of each run, Pallas kernels for 9% -> 11%
where the time goes in v8:
time: 62.6 us; the launch traced here: 62.5 us
  waiting for transfers between devices  25.7 us (41%)
  starting transfers between devices  25.6 us (41%)
  Pallas kernels  8.41 us (13%)
  between operations  1.53 us (2%)
  local copies, waits for them, and re-layouts  1.15 us (2%)
    ppermute x25, waiting for transfers between devices, swap(): return lax.ppermute(value, axis, [(i, i ^ mask) for i in range(size)])  25.7 us
    ppermute x25, starting transfers between devices, swap(): return lax.ppermute(value, axis, [(i, i ^ mask) for i in range(size)])  25.6 us
    pallas_call x22, Pallas kernels, call(): pl.pallas_call(body, out_shape=outs, in_specs=(specs or [VMEM] * len(args...  8.41 us
  transfers between devices with their start and end apart: 25, of which 14 were waited for; matrix products, arithmetic and copies ran while one was open for 0% of the time, Pallas kernels for 11%

profile of v8, /device:TPU:0, one launch (start us, length us, event | category | flops | bytes accessed | tf_op | source)
XLA Modules:
  0.0 62.5 jit_solution(2724530287252646732)
XLA Ops:
  0.7 3.0 %collective-permute-start = (bf16[128,512]{1,0:T(8,128)(2,1)}, bf16[128,512]{1,0:T(8,128)(2,1)S(1)}, u32[]{:S(2)}, u32[]{:S(2)}) collective-permute-start(bf16[128,512]{1,0:T(8,128)(2,1)} %bitcast.3), channel_id=1, source_target_pairs={{0,8},{8,0},{16,24},{24,16},{1,9},{9,1},{17,25},{25,17},{2,10},{10... | collective-permute-start | bytes 393224 | tf_op jit(solution)/shard_map/ppermute | solution.py:39
  3.7 1.5 %collective-permute-start.1 = (bf16[128,512]{1,0:T(8,128)(2,1)}, bf16[128,512]{1,0:T(8,128)(2,1)S(1)}, u32[]{:S(2)}, u32[]{:S(2)}) collective-permute-start(bf16[128,512]{1,0:T(8,128)(2,1)} %bitcast.4), channel_id=1, source_target_pairs={{0,16},{8,24},{16,0},{24,8},{1,17},{9,25},{17,1},{25,9},{2,18},{10... | collective-permute-start | bytes 393224 | tf_op jit(solution)/shard_map/ppermute | solution.py:39
  5.9 1.1 %copy-done.1 = bf16[1,1,24,128,128]{4,3,2,1,0:T(8,128)(2,1)S(1)} copy-done((bf16[1,1,24,128,128]{4,3,2,1,0:T(8,128)(2,1)S(1)}, bf16[1,1,24,128,128]{4,3,2,1,0:T(8,128)(2,1)}, u32[]{:S(2)}) %copy-start.1) | copy-done | bytes 786456
  7.0 2.7 %shard_map.94 = (bf16[1024,512]{1,0:T(8,128)(2,1)S(1)}, bf16[512,512]{1,0:T(8,128)(2,1)S(1)}, bf16[512,512]{1,0:T(8,128)(2,1)S(1)}) custom-call(bf16[1,1,24,128,128]{4,3,2,1,0:T(8,128)(2,1)S(1)} %copy-done.1, s32[1,1,24]{2,1,0:T(1,128)S(1)} %copy-done.4, s32[1,1,24]{2,1,0:T(1,128)S(1)} %copy-done.5, s32[1,1]{1,0:T(1,128)S(6)} %copy.10.refs_3_), custom_call_target="tpu_custom_call" | custom-call | tf_op jit(solution)/shard_map/pallas_call | solution.py:23
  9.7 1.9 %collective-permute-done.1.refs_3_ = bf16[128,512]{1,0:T(8,128)(2,1)S(1)} collective-permute-done((bf16[128,512]{1,0:T(8,128)(2,1)}, bf16[128,512]{1,0:T(8,128)(2,1)S(1)}, u32[]{:S(2)}, u32[]{:S(2)}) %collective-permute-start.1) | collective-permute-done | bytes 131104 | tf_op jit(solution)/shard_map/ppermute | solution.py:39
  13.6 1.6 %collective-permute-start.6 = (bf16[128,512]{1,0:T(8,128)(2,1)S(1)}, bf16[128,512]{1,0:T(8,128)(2,1)S(1)}, u32[]{:S(2)}, u32[]{:S(2)}) collective-permute-start(bf16[128,512]{1,0:T(8,128)(2,1)S(1)} %get-tuple-element.30), channel_id=1, source_target_pairs={{0,2},{1,3},{2,0},{3,1},{4,6},{5,7},{6,4},{7,5},{8,10},{9,11},{10,... | collective-permute-start | bytes 393224 | tf_op jit(solution)/shard_map/ppermute | solution.py:39
  16.1 3.5 %collective-permute-done.6.refs_1_ = bf16[128,512]{1,0:T(8,128)(2,1)S(1)} collective-permute-done((bf16[128,512]{1,0:T(8,128)(2,1)S(1)}, bf16[128,512]{1,0:T(8,128)(2,1)S(1)}, u32[]{:S(2)}, u32[]{:S(2)}) %collective-permute-start.6) | collective-permute-done | bytes 131104 | tf_op jit(solution)/shard_map/ppermute | solution.py:39
  19.7 2.7 %collective-permute-start.7 = (bf16[128,512]{1,0:T(8,128)(2,1)S(1)}, bf16[128,512]{1,0:T(8,128)(2,1)S(1)}, u32[]{:S(2)}, u32[]{:S(2)}) collective-permute-start(bf16[128,512]{1,0:T(8,128)(2,1)S(1)} %shard_map.101), channel_id=1, source_target_pairs={{0,4},{1,5},{2,6},{3,7},{4,0},{5,1},{6,2},{7,3},{8,12},{9,13},{10,... | collective-permute-start | bytes 393224 | tf_op jit(solution)/shard_map/ppermute | solution.py:39
  22.3 5.8 %collective-permute-done.7.refs_4_ = bf16[128,512]{1,0:T(8,128)(2,1)S(1)} collective-permute-done((bf16[128,512]{1,0:T(8,128)(2,1)S(1)}, bf16[128,512]{1,0:T(8,128)(2,1)S(1)}, u32[]{:S(2)}, u32[]{:S(2)}) %collective-permute-start.7) | collective-permute-done | bytes 131104 | tf_op jit(solution)/shard_map/ppermute | solution.py:39
  29.3 3.5 %collective-permute-start.8 = (bf16[128,512]{1,0:T(8,128)(2,1)S(1)}, bf16[128,512]{1,0:T(8,128)(2,1)S(1)}, u32[]{:S(2)}, u32[]{:S(2)}) collective-permute-start(bf16[128,512]{1,0:T(8,128)(2,1)S(1)} %get-tuple-element.34.refs_1_), channel_id=1, source_target_pairs={{0,2},{1,3},{2,0},{3,1},{4,6},{5,7},{6,4},{7,5},{8,10},{9,11},{10,... | collective-permute-start | bytes 393224 | tf_op jit(solution)/shard_map/ppermute | solution.py:39
  32.9 1.3 %collective-permute-start.14 = (bf16[64,512]{1,0:T(8,128)(2,1)S(1)}, bf16[64,512]{1,0:T(8,128)(2,1)S(1)}, u32[]{:S(2)}, u32[]{:S(2)}) collective-permute-start(bf16[64,512]{1,0:T(8,128)(2,1)S(1)} %get-tuple-element.41), channel_id=1, source_target_pairs={{0,8},{8,0},{16,24},{24,16},{1,9},{9,1},{17,25},{25,17},{2,10},{10... | collective-permute-start | bytes 196616 | tf_op jit(solution)/shard_map/ppermute | solution.py:39
  34.1 0.8 %collective-permute-start.15 = (bf16[64,512]{1,0:T(8,128)(2,1)S(1)}, bf16[64,512]{1,0:T(8,128)(2,1)S(1)}, u32[]{:S(2)}, u32[]{:S(2)}) collective-permute-start(bf16[64,512]{1,0:T(8,128)(2,1)S(1)} %get-tuple-element.42), channel_id=1, source_target_pairs={{0,16},{8,24},{16,0},{24,8},{1,17},{9,25},{17,1},{25,9},{2,18},{10... | collective-permute-start | bytes 196616 | tf_op jit(solution)/shard_map/ppermute | solution.py:39
  35.0 1.4 %collective-permute-start.16 = (bf16[64,512]{1,0:T(8,128)(2,1)S(1)}, bf16[64,512]{1,0:T(8,128)(2,1)S(1)}, u32[]{:S(2)}, u32[]{:S(2)}) collective-permute-start(bf16[64,512]{1,0:T(8,128)(2,1)S(1)} %get-tuple-element.43), channel_id=1, source_target_pairs={{0,24},{8,16},{16,8},{24,0},{1,25},{9,17},{17,9},{25,1},{2,26},{10... | collective-permute-start | bytes 196616 | tf_op jit(solution)/shard_map/ppermute | solution.py:39
  36.4 2.4 %collective-permute-done.9.refs_0_ = bf16[128,512]{1,0:T(8,128)(2,1)S(1)} collective-permute-done((bf16[128,512]{1,0:T(8,128)(2,1)S(1)}, bf16[128,512]{1,0:T(8,128)(2,1)S(1)}, u32[]{:S(2)}, u32[]{:S(2)}) %collective-permute-start.9) | collective-permute-done | bytes 131104 | tf_op jit(solution)/shard_map/ppermute | solution.py:39
  39.1 1.0 %collective-permute-done.16.refs_3_ = bf16[64,512]{1,0:T(8,128)(2,1)S(1)} collective-permute-done((bf16[64,512]{1,0:T(8,128)(2,1)S(1)}, bf16[64,512]{1,0:T(8,128)(2,1)S(1)}, u32[]{:S(2)}, u32[]{:S(2)}) %collective-permute-start.16) | collective-permute-done | bytes 65568 | tf_op jit(solution)/shard_map/ppermute | solution.py:39
  40.2 0.8 %collective-permute-start.17 = (bf16[64,512]{1,0:T(8,128)(2,1)S(1)}, bf16[64,512]{1,0:T(8,128)(2,1)S(1)}, u32[]{:S(2)}, u32[]{:S(2)}) collective-permute-start(bf16[64,512]{1,0:T(8,128)(2,1)S(1)} %shard_map.109.refs_0_), channel_id=1, source_target_pairs={{0,2},{1,3},{2,0},{3,1},{4,6},{5,7},{6,4},{7,5},{8,10},{9,11},{10,... | collective-permute-start | bytes 196616 | tf_op jit(solution)/shard_map/ppermute | solution.py:39
  41.7 2.9 %collective-permute-start.19 = (bf16[64,512]{1,0:T(8,128)(2,1)S(1)}, bf16[64,512]{1,0:T(8,128)(2,1)S(1)}, u32[]{:S(2)}, u32[]{:S(2)}) collective-permute-start(bf16[64,512]{1,0:T(8,128)(2,1)S(1)} %shard_map.109.refs_0_), channel_id=1, source_target_pairs={{0,6},{1,7},{2,4},{3,5},{4,2},{5,3},{6,0},{7,1},{8,14},{9,15},{10,... | collective-permute-start | bytes 196616 | tf_op jit(solution)/shard_map/ppermute | solution.py:39
  46.9 1.6 %collective-permute-done.18.refs_2_ = bf16[64,512]{1,0:T(8,128)(2,1)S(1)} collective-permute-done((bf16[64,512]{1,0:T(8,128)(2,1)S(1)}, bf16[64,512]{1,0:T(8,128)(2,1)S(1)}, u32[]{:S(2)}, u32[]{:S(2)}) %collective-permute-start.18) | collective-permute-done | bytes 65568 | tf_op jit(solution)/shard_map/ppermute | solution.py:39
  48.6 1.3 %collective-permute-start.20 = (bf16[192,512]{1,0:T(8,128)(2,1)S(1)}, bf16[192,512]{1,0:T(8,128)(2,1)S(1)}, u32[]{:S(2)}, u32[]{:S(2)}) collective-permute-start(bf16[192,512]{1,0:T(8,128)(2,1)S(1)} %get-tuple-element.45), channel_id=1, source_target_pairs={{0,8},{8,0},{16,24},{24,16},{1,9},{9,1},{17,25},{25,17},{2,10},{10... | collective-permute-start | bytes 589832 | tf_op jit(solution)/shard_map/ppermute | solution.py:39
  50.8 1.4 %collective-permute-start.22 = (bf16[192,512]{1,0:T(8,128)(2,1)S(1)}, bf16[192,512]{1,0:T(8,128)(2,1)S(1)}, u32[]{:S(2)}, u32[]{:S(2)}) collective-permute-start(bf16[192,512]{1,0:T(8,128)(2,1)S(1)} %get-tuple-element.47), channel_id=1, source_target_pairs={{0,24},{8,16},{16,8},{24,0},{1,25},{9,17},{17,9},{25,1},{2,26},{10... | collective-permute-start | bytes 589832 | tf_op jit(solution)/shard_map/ppermute | solution.py:39
  52.9 3.7 %collective-permute-done.20.refs_1_ = bf16[192,512]{1,0:T(8,128)(2,1)S(1)} collective-permute-done((bf16[192,512]{1,0:T(8,128)(2,1)S(1)}, bf16[192,512]{1,0:T(8,128)(2,1)S(1)}, u32[]{:S(2)}, u32[]{:S(2)}) %collective-permute-start.20) | collective-permute-done | bytes 196640 | tf_op jit(solution)/shard_map/ppermute | solution.py:39
  56.6 1.7 %collective-permute-done.21.refs_0_.refs_2_ = bf16[192,512]{1,0:T(8,128)(2,1)S(1)} collective-permute-done((bf16[192,512]{1,0:T(8,128)(2,1)S(1)}, bf16[192,512]{1,0:T(8,128)(2,1)S(1)}, u32[]{:S(2)}, u32[]{:S(2)}) %collective-permute-start.21) | collective-permute-done | bytes 196640 | tf_op jit(solution)/shard_map/ppermute | solution.py:39
  58.3 1.6 %collective-permute-done.22.refs_1_.refs_3_ = bf16[192,512]{1,0:T(8,128)(2,1)S(1)} collective-permute-done((bf16[192,512]{1,0:T(8,128)(2,1)S(1)}, bf16[192,512]{1,0:T(8,128)(2,1)S(1)}, u32[]{:S(2)}, u32[]{:S(2)}) %collective-permute-start.22) | collective-permute-done | bytes 196640 | tf_op jit(solution)/shard_map/ppermute | solution.py:39
  61.4 1.0 %shard_map.115 = f32[512,512]{1,0:T(8,128)} custom-call(bf16[128,512]{1,0:T(8,128)(2,1)S(1)} %shard_map.112.refs_0_, bf16[128,512]{1,0:T(8,128)(2,1)S(1)} %shard_map.113.refs_4_.refs_1_, bf16[128,512]{1,0:T(8,128)(2,1)S(1)} %collective-permute-done.23.refs_2_, bf16[128,512]{1,0:T(8,128)(2,1)S(1)} %collective-permute-done.24.refs_3_), custom_call_target="tpu_custom_call" | custom-call | tf_op jit(solution)/shard_map/pallas_call | solution.py:23
  (60 shorter events, 10.5 us)
Async XLA Ops:
  0.7 9.0 %collective-permute-start = (bf16[128,512]{1,0:T(8,128)(2,1)}, bf16[128,512]{1,0:T(8,128)(2,1)S(1)}, u32[]{:S(2)}, u32[]{:S(2)}) collective-permute-start(bf16[128,512]{1,0:T(8,128)(2,1)} %bitcast.3), channel_id=1, source_target_pairs={{0,8},{8,0},{16,24},{24,16},{1,9},{9,1},{17,25},{25,17},{2,10},{10... | collective-permute-start | bytes 393224 | tf_op jit(solution)/shard_map/ppermute | solution.py:39
  3.7 8.0 %collective-permute-start.1 = (bf16[128,512]{1,0:T(8,128)(2,1)}, bf16[128,512]{1,0:T(8,128)(2,1)S(1)}, u32[]{:S(2)}, u32[]{:S(2)}) collective-permute-start(bf16[128,512]{1,0:T(8,128)(2,1)} %bitcast.4), channel_id=1, source_target_pairs={{0,16},{8,24},{16,0},{24,8},{1,17},{9,25},{17,1},{25,9},{2,18},{10... | collective-permute-start | bytes 393224 | tf_op jit(solution)/shard_map/ppermute | solution.py:39
  5.2 6.5 %collective-permute-start.2 = (bf16[128,512]{1,0:T(8,128)(2,1)}, bf16[128,512]{1,0:T(8,128)(2,1)S(1)}, u32[]{:S(2)}, u32[]{:S(2)}) collective-permute-start(bf16[128,512]{1,0:T(8,128)(2,1)} %bitcast.5), channel_id=1, source_target_pairs={{0,24},{8,16},{16,8},{24,0},{1,25},{9,17},{17,9},{25,1},{2,26},{10... | collective-permute-start | bytes 393224 | tf_op jit(solution)/shard_map/ppermute | solution.py:39
  12.0 1.6 %collective-permute-start.4 = (bf16[256,512]{1,0:T(8,128)(2,1)S(1)}, bf16[256,512]{1,0:T(8,128)(2,1)S(1)}, u32[]{:S(2)}, u32[]{:S(2)}) collective-permute-start(bf16[256,512]{1,0:T(8,128)(2,1)S(1)} %shard_map.99), channel_id=1, source_target_pairs={{0,1},{1,0},{2,3},{3,2},{4,5},{5,4},{6,7},{7,6},{8,9},{9,8},{10,11... | collective-permute-start | bytes 786440 | tf_op jit(solution)/shard_map/ppermute | solution.py:39
  12.3 3.8 %collective-permute-start.3 = (bf16[256,512]{1,0:T(8,128)(2,1)S(1)}, bf16[256,512]{1,0:T(8,128)(2,1)S(1)}, u32[]{:S(2)}, u32[]{:S(2)}) collective-permute-start(bf16[256,512]{1,0:T(8,128)(2,1)S(1)} %shard_map.96), channel_id=1, source_target_pairs={{0,1},{1,0},{2,3},{3,2},{4,5},{5,4},{6,7},{7,6},{8,9},{9,8},{10,11... | collective-permute-start | bytes 786440 | tf_op jit(solution)/shard_map/ppermute | solution.py:39
  13.6 6.0 %collective-permute-start.6 = (bf16[128,512]{1,0:T(8,128)(2,1)S(1)}, bf16[128,512]{1,0:T(8,128)(2,1)S(1)}, u32[]{:S(2)}, u32[]{:S(2)}) collective-permute-start(bf16[128,512]{1,0:T(8,128)(2,1)S(1)} %get-tuple-element.30), channel_id=1, source_target_pairs={{0,2},{1,3},{2,0},{3,1},{4,6},{5,7},{6,4},{7,5},{8,10},{9,11},{10,... | collective-permute-start | bytes 393224 | tf_op jit(solution)/shard_map/ppermute | solution.py:39
  15.3 17.5 %collective-permute-start.11 = (bf16[512,512]{1,0:T(8,128)(2,1)S(1)}, bf16[512,512]{1,0:T(8,128)(2,1)S(1)}, u32[]{:S(2)}, u32[]{:S(2)}) collective-permute-start(bf16[512,512]{1,0:T(8,128)(2,1)S(1)} %get-tuple-element.35), channel_id=1, source_target_pairs={{0,1},{1,0},{2,3},{3,2},{4,5},{5,4},{6,7},{7,6},{8,9},{9,8},{10,11... | collective-permute-start | bytes 1572872 | tf_op jit(solution)/shard_map/ppermute | solution.py:39
  15.6 6.8 %collective-permute-start.5 = (bf16[128,512]{1,0:T(8,128)(2,1)S(1)}, bf16[128,512]{1,0:T(8,128)(2,1)S(1)}, u32[]{:S(2)}, u32[]{:S(2)}) collective-permute-start(bf16[128,512]{1,0:T(8,128)(2,1)S(1)} %get-tuple-element.28), channel_id=1, source_target_pairs={{0,2},{1,3},{2,0},{3,1},{4,6},{5,7},{6,4},{7,5},{8,10},{9,11},{10,... | collective-permute-start | bytes 393224 | tf_op jit(solution)/shard_map/ppermute | solution.py:39
  19.7 8.5 %collective-permute-start.7 = (bf16[128,512]{1,0:T(8,128)(2,1)S(1)}, bf16[128,512]{1,0:T(8,128)(2,1)S(1)}, u32[]{:S(2)}, u32[]{:S(2)}) collective-permute-start(bf16[128,512]{1,0:T(8,128)(2,1)S(1)} %shard_map.101), channel_id=1, source_target_pairs={{0,4},{1,5},{2,6},{3,7},{4,0},{5,1},{6,2},{7,3},{8,12},{9,13},{10,... | collective-permute-start | bytes 393224 | tf_op jit(solution)/shard_map/ppermute | solution.py:39
  29.0 3.8 %collective-permute-start.13 = (bf16[256,512]{1,0:T(8,128)(2,1)S(1)}, bf16[256,512]{1,0:T(8,128)(2,1)S(1)}, u32[]{:S(2)}, u32[]{:S(2)}) collective-permute-start(bf16[256,512]{1,0:T(8,128)(2,1)S(1)} %get-tuple-element.39), channel_id=1, source_target_pairs={{0,1},{1,0},{2,3},{3,2},{4,5},{5,4},{6,7},{7,6},{8,9},{9,8},{10,11... | collective-permute-start | bytes 786440 | tf_op jit(solution)/shard_map/ppermute | solution.py:39
  29.1 9.7 %collective-permute-start.9 = (bf16[128,512]{1,0:T(8,128)(2,1)S(1)}, bf16[128,512]{1,0:T(8,128)(2,1)S(1)}, u32[]{:S(2)}, u32[]{:S(2)}) collective-permute-start(bf16[128,512]{1,0:T(8,128)(2,1)S(1)} %get-tuple-element.34.refs_1_), channel_id=1, source_target_pairs={{0,4},{1,5},{2,6},{3,7},{4,0},{5,1},{6,2},{7,3},{8,12},{9,13},{10,... | collective-permute-start | bytes 393224 | tf_op jit(solution)/shard_map/ppermute | solution.py:39
  29.3 15.3 %collective-permute-start.8 = (bf16[128,512]{1,0:T(8,128)(2,1)S(1)}, bf16[128,512]{1,0:T(8,128)(2,1)S(1)}, u32[]{:S(2)}, u32[]{:S(2)}) collective-permute-start(bf16[128,512]{1,0:T(8,128)(2,1)S(1)} %get-tuple-element.34.refs_1_), channel_id=1, source_target_pairs={{0,2},{1,3},{2,0},{3,1},{4,6},{5,7},{6,4},{7,5},{8,10},{9,11},{10,... | collective-permute-start | bytes 393224 | tf_op jit(solution)/shard_map/ppermute | solution.py:39
  32.9 6.0 %collective-permute-start.14 = (bf16[64,512]{1,0:T(8,128)(2,1)S(1)}, bf16[64,512]{1,0:T(8,128)(2,1)S(1)}, u32[]{:S(2)}, u32[]{:S(2)}) collective-permute-start(bf16[64,512]{1,0:T(8,128)(2,1)S(1)} %get-tuple-element.41), channel_id=1, source_target_pairs={{0,8},{8,0},{16,24},{24,16},{1,9},{9,1},{17,25},{25,17},{2,10},{10... | collective-permute-start | bytes 196616 | tf_op jit(solution)/shard_map/ppermute | solution.py:39
  34.1 5.0 %collective-permute-start.15 = (bf16[64,512]{1,0:T(8,128)(2,1)S(1)}, bf16[64,512]{1,0:T(8,128)(2,1)S(1)}, u32[]{:S(2)}, u32[]{:S(2)}) collective-permute-start(bf16[64,512]{1,0:T(8,128)(2,1)S(1)} %get-tuple-element.42), channel_id=1, source_target_pairs={{0,16},{8,24},{16,0},{24,8},{1,17},{9,25},{17,1},{25,9},{2,18},{10... | collective-permute-start | bytes 196616 | tf_op jit(solution)/shard_map/ppermute | solution.py:39
  35.0 5.2 %collective-permute-start.16 = (bf16[64,512]{1,0:T(8,128)(2,1)S(1)}, bf16[64,512]{1,0:T(8,128)(2,1)S(1)}, u32[]{:S(2)}, u32[]{:S(2)}) collective-permute-start(bf16[64,512]{1,0:T(8,128)(2,1)S(1)} %get-tuple-element.43), channel_id=1, source_target_pairs={{0,24},{8,16},{16,8},{24,0},{1,25},{9,17},{17,9},{25,1},{2,26},{10... | collective-permute-start | bytes 196616 | tf_op jit(solution)/shard_map/ppermute | solution.py:39
  38.8 6.5 %collective-permute-start.10 = (bf16[128,512]{1,0:T(8,128)(2,1)S(1)}, bf16[128,512]{1,0:T(8,128)(2,1)S(1)}, u32[]{:S(2)}, u32[]{:S(2)}) collective-permute-start(bf16[128,512]{1,0:T(8,128)(2,1)S(1)} %shard_map.104.refs_3_), channel_id=1, source_target_pairs={{0,2},{1,3},{2,0},{3,1},{4,6},{5,7},{6,4},{7,5},{8,10},{9,11},{10,... | collective-permute-start | bytes 393224 | tf_op jit(solution)/shard_map/ppermute | solution.py:39
  40.2 6.8 %collective-permute-start.17 = (bf16[64,512]{1,0:T(8,128)(2,1)S(1)}, bf16[64,512]{1,0:T(8,128)(2,1)S(1)}, u32[]{:S(2)}, u32[]{:S(2)}) collective-permute-start(bf16[64,512]{1,0:T(8,128)(2,1)S(1)} %shard_map.109.refs_0_), channel_id=1, source_target_pairs={{0,2},{1,3},{2,0},{3,1},{4,6},{5,7},{6,4},{7,5},{8,10},{9,11},{10,... | collective-permute-start | bytes 196616 | tf_op jit(solution)/shard_map/ppermute | solution.py:39
  41.0 7.5 %collective-permute-start.18 = (bf16[64,512]{1,0:T(8,128)(2,1)S(1)}, bf16[64,512]{1,0:T(8,128)(2,1)S(1)}, u32[]{:S(2)}, u32[]{:S(2)}) collective-permute-start(bf16[64,512]{1,0:T(8,128)(2,1)S(1)} %shard_map.109.refs_0_), channel_id=1, source_target_pairs={{0,4},{1,5},{2,6},{3,7},{4,0},{5,1},{6,2},{7,3},{8,12},{9,13},{10,... | collective-permute-start | bytes 196616 | tf_op jit(solution)/shard_map/ppermute | solution.py:39
  41.7 6.8 %collective-permute-start.19 = (bf16[64,512]{1,0:T(8,128)(2,1)S(1)}, bf16[64,512]{1,0:T(8,128)(2,1)S(1)}, u32[]{:S(2)}, u32[]{:S(2)}) collective-permute-start(bf16[64,512]{1,0:T(8,128)(2,1)S(1)} %shard_map.109.refs_0_), channel_id=1, source_target_pairs={{0,6},{1,7},{2,4},{3,5},{4,2},{5,3},{6,0},{7,1},{8,14},{9,15},{10,... | collective-permute-start | bytes 196616 | tf_op jit(solution)/shard_map/ppermute | solution.py:39
  45.7 2.8 %collective-permute-start.12 = (bf16[512,512]{1,0:T(8,128)(2,1)S(1)}, bf16[512,512]{1,0:T(8,128)(2,1)S(1)}, u32[]{:S(2)}, u32[]{:S(2)}) collective-permute-start(bf16[512,512]{1,0:T(8,128)(2,1)S(1)} %shard_map.106), channel_id=1, source_target_pairs={{0,1},{1,0},{2,3},{3,2},{4,5},{5,4},{6,7},{7,6},{8,9},{9,8},{10,11... | collective-permute-start | bytes 1572872 | tf_op jit(solution)/shard_map/ppermute | solution.py:39
  48.6 7.9 %collective-permute-start.20 = (bf16[192,512]{1,0:T(8,128)(2,1)S(1)}, bf16[192,512]{1,0:T(8,128)(2,1)S(1)}, u32[]{:S(2)}, u32[]{:S(2)}) collective-permute-start(bf16[192,512]{1,0:T(8,128)(2,1)S(1)} %get-tuple-element.45), channel_id=1, source_target_pairs={{0,8},{8,0},{16,24},{24,16},{1,9},{9,1},{17,25},{25,17},{2,10},{10... | collective-permute-start | bytes 589832 | tf_op jit(solution)/shard_map/ppermute | solution.py:39
  49.9 8.4 %collective-permute-start.21 = (bf16[192,512]{1,0:T(8,128)(2,1)S(1)}, bf16[192,512]{1,0:T(8,128)(2,1)S(1)}, u32[]{:S(2)}, u32[]{:S(2)}) collective-permute-start(bf16[192,512]{1,0:T(8,128)(2,1)S(1)} %get-tuple-element.46), channel_id=1, source_target_pairs={{0,16},{8,24},{16,0},{24,8},{1,17},{9,25},{17,1},{25,9},{2,18},{10... | collective-permute-start | bytes 589832 | tf_op jit(solution)/shard_map/ppermute | solution.py:39
  50.8 9.2 %collective-permute-start.22 = (bf16[192,512]{1,0:T(8,128)(2,1)S(1)}, bf16[192,512]{1,0:T(8,128)(2,1)S(1)}, u32[]{:S(2)}, u32[]{:S(2)}) collective-permute-start(bf16[192,512]{1,0:T(8,128)(2,1)S(1)} %get-tuple-element.47), channel_id=1, source_target_pairs={{0,24},{8,16},{16,8},{24,0},{1,25},{9,17},{17,9},{25,1},{2,26},{10... | collective-permute-start | bytes 589832 | tf_op jit(solution)/shard_map/ppermute | solution.py:39
  56.6 3.4 %collective-permute-start.23 = (bf16[128,512]{1,0:T(8,128)(2,1)S(1)}, bf16[128,512]{1,0:T(8,128)(2,1)S(1)}, u32[]{:S(2)}, u32[]{:S(2)}) collective-permute-start(bf16[128,512]{1,0:T(8,128)(2,1)S(1)} %shard_map.112.refs_0_), channel_id=1, source_target_pairs={{0,1},{1,0},{2,3},{3,2},{4,5},{5,4},{6,7},{7,6},{8,9},{9,8},{10,11... | collective-permute-start | bytes 393224 | tf_op jit(solution)/shard_map/ppermute | solution.py:39
  (7 other events, 38.7 us)
